TPU v7x, 256 devices: a whole 4x4x8 slice. The times are simulated.
256 devices in a mesh: row: 128 (over x, y, z), band: 2 (over core).
Axes of the slice: x: 4, y: 4, z: 8, core: 2. Of those that a mesh axis runs over, the one named last changes fastest.
Arguments:
- hamiltonian: bfloat16 [1280, 32, 128, 128], P('row'), may hold values from -0.09375 to 0.09375
- neighbours: int32 [1280, 32], P('row'), may hold values from 0 to 1279, as said below
- counts: int32 [1280], P('row'), may hold values from 16 to 32
- vectors: bfloat16 [163840, 128], P('row', 'band'), may hold values from -6 to 6
Outputs:
- filtered: bfloat16 [163840, 128], P('row', 'band')
- gram: float32 [128, 128], P('band')
- projected: float32 [128, 128], P('band')
Inputs may be any that keep to these rules, and one draw needn't show every extreme that they name: `neighbours`: entry [r, 0] is r; every entry lies within 8 of its block row r.
All inputs are finite; a program needn't handle non-finite values.
Results may differ from a plain program's by a relative error of at most 0.022.
Values may be sent and summed in bfloat16 or wider, within the bound.
No kernel may reach another device: no remote copies, remote signals or barrier semaphores. Data moves between devices by JAX's collectives and lax.ppermute only.
A program may use at most 128 MiB of HBM per device.

v0:
```python
import jax
import jax.numpy as jnp
from jax import lax
from jax.sharding import PartitionSpec as P

B = 128
DIST = 8


def from_behind(value, axis, steps):
    count = lax.axis_size(axis)
    first, last = (max(0, -steps), min(count, count - steps))
    return lax.ppermute(value, axis, [(source, source + steps) for source in range(first, last)])


def extend_field(shard):
    lower_parts = [from_behind(shard, "row", 1)]
    upper_parts = from_behind(shard, "row", -1)
    below = jnp.concatenate(lower_parts[::-1], axis=0)
    above = upper_parts
    below = below[below.shape[0] - DIST * B :]
    above = above[: DIST * B]
    return jnp.concatenate([below, shard, above], axis=0)


def build_band(hamiltonian, neighbours, counts, block_rows):
    slot_count = neighbours.shape[1]
    first_block = lax.axis_index("row") * block_rows
    own_rows = first_block + jnp.arange(block_rows, dtype=jnp.int32)
    offset_index = neighbours - own_rows[:, None] + DIST
    slots = jnp.arange(slot_count, dtype=jnp.int32)
    live = slots[None, :] < counts[:, None]
    diagonals = jnp.arange(2 * DIST + 1, dtype=jnp.int32)
    selector = ((offset_index[:, None, :] == diagonals[None, :, None]) & live[:, None, :]).astype(
        jnp.bfloat16
    )
    flat_blocks = hamiltonian.reshape(block_rows, slot_count, B * B)
    summed = lax.dot_general(
        selector, flat_blocks, (((2,), (1,)), ((0,), (0,))), preferred_element_type=jnp.float32
    )
    high_part = summed.astype(jnp.bfloat16)
    low_part = (summed - high_part.astype(jnp.float32)).astype(jnp.bfloat16)
    stacked = jnp.concatenate(
        [
            high_part.reshape(block_rows, 2 * DIST + 1, B, B),
            low_part.reshape(block_rows, 2 * DIST + 1, B, B),
        ],
        axis=2,
    )
    return stacked


def apply_local(banded, shard, block_rows):
    extended = extend_field(shard)
    width = shard.shape[1]
    ext_blocks = extended.reshape(block_rows + 2 * DIST, B, width)
    total = jnp.zeros((block_rows, 2 * B, width), jnp.float32)
    for offset in range(2 * DIST + 1):
        window = ext_blocks[offset : offset + block_rows]
        total = total + jnp.einsum(
            "rij,rjm->rim", banded[:, offset], window, preferred_element_type=jnp.float32
        )
    result = total[:, :B] + total[:, B:]
    return result.reshape(block_rows * B, width)


def body(hamiltonian, neighbours, counts, vectors):
    block_rows = hamiltonian.shape[0]
    banded = build_band(hamiltonian, neighbours, counts, block_rows)
    level1 = apply_local(banded, vectors, block_rows).astype(jnp.bfloat16)
    older, newer = (vectors, level1)
    for degree in range(3):
        applied = apply_local(banded, newer, block_rows)
        nextone = (2.0 * applied - older.astype(jnp.float32)).astype(jnp.bfloat16)
        older, newer = (newer, nextone)
    image = apply_local(banded, newer, block_rows).astype(jnp.bfloat16)
    all_filtered, all_image = (
        lax.all_gather(newer, "band", axis=1, tiled=True),
        lax.all_gather(image, "band", axis=1, tiled=True),
    )
    gram_part = jnp.dot(newer.T, all_filtered, preferred_element_type=jnp.float32)
    proj_part = jnp.dot(newer.T, all_image, preferred_element_type=jnp.float32)
    gram_sum, proj_sum = lax.psum((gram_part, proj_part), "row")
    scale_rows = 1.0 / (block_rows * lax.axis_size("row") * B)
    return (newer, gram_sum * scale_rows, proj_sum * scale_rows)


def solution(mesh):
    return jax.shard_map(
        body,
        mesh=mesh,
        in_specs=(P("row", None, None, None), P("row", None), P("row"), P("row", "band")),
        out_specs=(P("row", "band"), P("band", None), P("band", None)),
        check_vma=False,
    )
```

profile of v0, /device:TPU:32, one launch (start us, length us, event | category | flops | bytes accessed | tf_op | source)
XLA Modules:
  0.0 388.5 jit_solution(1094681352987330690)
XLA Ops:
  7.2 3.8 collective-permute-start
  11.1 2.0 collective-permute-start.1
  13.1 16.4 %reshape.140 = bf16[10,32,16384]{2,1,0:T(8,128)(2,1)} reshape(bf16[10,32,128,128]{3,2,1,0:T(8,128)(2,1)} %param.4) | data formatting | bytes 20971520 | tf_op jit(solution)/shard_map/reshape | solution.py:37
  29.6 11.7 %subtract_convert_fusion = (bf16[10,17,16384]{2,1,0:T(8,128)(2,1)}, bf16[10,17,16384]{2,1,0:T(8,128)(2,1)}) fusion(bf16[10,32,16384]{2,1,0:T(8,128)(2,1)} %reshape.140, s32[10,32]{1,0:T(8,128)S(1)} %subtract_add_fusion, pred[10,32]{1,0:T(8,128)(4,1)S(1)} %iota_compare_fusion.1), kind=kOutput, calls=%fused_computation | convolution fusion | flops 189409920 | bytes 21628480 | tf_op jit(solution)/shard_map/dot_general | solution.py:38
  41.4 9.7 %reshape.141 = bf16[10,17,128,128]{3,2,1,0:T(8,128)(2,1)} reshape(bf16[10,17,16384]{2,1,0:T(8,128)(2,1)} %get-tuple-element.6) | data formatting | bytes 11141120 | tf_op jit(solution)/shard_map/reshape | solution.py:45
  51.1 7.3 %constant_dynamic-update-slice_fusion.1 = bf16[10,17,256,128]{3,2,1,0:T(8,128)(2,1)} fusion(bf16[10,17,128,128]{3,2,1,0:T(8,128)(2,1)} %reshape.141), kind=kLoop, calls=%fused_computation.602 | loop fusion | bytes 11141120
  58.4 9.8 %reshape.142 = bf16[10,17,128,128]{3,2,1,0:T(8,128)(2,1)} reshape(bf16[10,17,16384]{2,1,0:T(8,128)(2,1)} %get-tuple-element.5) | data formatting | bytes 11141120 | tf_op jit(solution)/shard_map/reshape | solution.py:46
  68.2 7.2 %constant_dynamic-update-slice_fusion = bf16[10,17,256,128]{3,2,1,0:T(8,128)(2,1)} fusion(bf16[10,17,256,128]{3,2,1,0:T(8,128)(2,1)} %constant_dynamic-update-slice_fusion.1, bf16[10,17,128,128]{3,2,1,0:T(8,128)(2,1)} %reshape.142), kind=kLoop, calls=%fused_computation.601 | loop fusion | bytes 11141120 | tf_op jit(solution)/shard_map/concatenate | solution.py:43
  75.6 1.6 fusion.4
  77.2 1.9 convolution_add_fusion.79
  79.1 1.4 convolution_add_fusion.78
  80.5 1.4 convolution_add_fusion.77
  82.0 1.4 convolution_add_fusion.76
  84.1 0.4 convolution_add_fusion.73
  85.4 0.4 convolution_add_fusion.70
  85.7 0.4 convolution_add_fusion.69
  87.5 0.4 convolution_add_fusion.64
  87.9 1.9 collective-permute-start.3
  89.8 4.1 %collective-permute-start.2 = (bf16[1280,64]{0,1:T(8,128)(2,1)S(1)}, bf16[1280,64]{0,1:T(8,128)(2,1)S(1)}, u32[]{:S(2)}, u32[]{:S(2)}) collective-permute-start(bf16[1280,64]{0,1:T(8,128)(2,1)S(1)} %copy_bitcast_fusion.1), channel_id=1, source_target_pairs={{0,2},{2,4},{4,6},{6,8},{8,10},{10,12},{12,14},{14,16},{16,18},{18... | collective-permute-start | bytes 491528 | tf_op jit(solution)/shard_map/ppermute | solution.py:13
  94.0 1.6 collective-permute-done.3
  95.7 1.6 collective-permute-done.2
  98.2 0.4 convolution_add_fusion.62
  103.6 1.9 collective-permute-start.5
  105.5 4.5 %collective-permute-start.4 = (bf16[1280,64]{0,1:T(8,128)(2,1)S(1)}, bf16[1280,64]{0,1:T(8,128)(2,1)S(1)}, u32[]{:S(2)}, u32[]{:S(2)}) collective-permute-start(bf16[1280,64]{0,1:T(8,128)(2,1)S(1)} %fusion.7), channel_id=1, source_target_pairs={{0,2},{2,4},{4,6},{6,8},{8,10},{10,12},{12,14},{14,16},{16,18},{18... | collective-permute-start | bytes 491528 | tf_op jit(solution)/shard_map/ppermute | solution.py:13
  110.0 1.4 collective-permute-done.5
  111.5 1.3 collective-permute-done.4
  114.7 0.4 convolution_add_fusion.43
  115.8 0.4 convolution_add_fusion.40
  116.1 0.4 convolution_add_fusion.39
  117.5 0.4 convolution_add_fusion.35
  119.0 1.9 collective-permute-start.7
  120.9 4.9 %collective-permute-start.6 = (bf16[1280,64]{0,1:T(8,128)(2,1)S(1)}, bf16[1280,64]{0,1:T(8,128)(2,1)S(1)}, u32[]{:S(2)}, u32[]{:S(2)}) collective-permute-start(bf16[1280,64]{0,1:T(8,128)(2,1)S(1)} %fusion.6), channel_id=1, source_target_pairs={{0,2},{2,4},{4,6},{6,8},{8,10},{10,12},{12,14},{14,16},{16,18},{18... | collective-permute-start | bytes 491528 | tf_op jit(solution)/shard_map/ppermute | solution.py:13
  125.8 1.4 collective-permute-done.7
  127.4 1.3 collective-permute-done.6
  131.6 0.4 convolution_add_fusion.24
  132.7 0.4 convolution_add_fusion.21
  133.8 0.4 convolution_add_fusion.18
  134.1 0.4 convolution_add_fusion.17
  134.5 0.4 convolution_add_fusion.16
  134.9 1.9 collective-permute-start.9
  136.8 5.6 %collective-permute-start.8 = (bf16[1280,64]{0,1:T(8,128)(2,1)S(1)}, bf16[1280,64]{0,1:T(8,128)(2,1)S(1)}, u32[]{:S(2)}, u32[]{:S(2)}) collective-permute-start(bf16[1280,64]{0,1:T(8,128)(2,1)S(1)} %fusion.5), channel_id=1, source_target_pairs={{0,2},{2,4},{4,6},{6,8},{8,10},{10,12},{12,14},{14,16},{16,18},{18... | collective-permute-start | bytes 491528 | tf_op jit(solution)/shard_map/ppermute | solution.py:13
  142.5 2.3 all_gather.6
  144.7 0.9 fusion.340
  150.2 0.4 convolution_add_fusion.4
  152.0 2.0 all_gather.7
  154.1 0.9 fusion.341
  155.0 225.3 %all-reduce.3.cloned.1.call-done = (f32[64,128]{1,0:T(8,128)}, f32[64,128]{1,0:T(8,128)}) async-done(((f32[64,128]{1,0:T(8,128)}, f32[64,128]{1,0:T(8,128)}), (f32[64,128]{1,0:T(8,128)}, f32[64,128]{1,0:T(8,128)})) %all-reduce.3.cloned.1.call-update) | async-done | bytes 65552 | tf_op jit(solution)/shard_map/psum | solution.py:83
  380.2 1.4 broadcast_multiply_fusion
  (110 shorter events, 25.0 us)
Async XLA Ops:
  7.2 22.3 %copy-start.4 = (s32[10]{0:T(128)S(1)}, s32[10]{0:T(128)}, u32[]{:S(2)}) copy-start(s32[10]{0:T(128)} %param.6) | copy-start | bytes 124
  7.2 22.4 %copy-start.3 = (s32[10,32]{1,0:T(8,128)S(1)}, s32[10,32]{1,0:T(8,128)}, u32[]{:S(2)}) copy-start(s32[10,32]{1,0:T(8,128)} %param.5) | copy-start | bytes 3844
  7.2 373.0 %all-reduce.3.cloned.1.call-start = ((), (), s32[]{:S(2)}) async-start(), calls=%async_computation | async-start | bytes 131072 | tf_op jit(solution)/shard_map/psum | solution.py:83
  7.2 68.2 %collective-permute-start = (bf16[1280,64]{0,1:T(8,128)(2,1)}, bf16[1280,64]{0,1:T(8,128)(2,1)S(1)}, u32[]{:S(2)}, u32[]{:S(2)}) collective-permute-start(bf16[1280,64]{0,1:T(8,128)(2,1)} %param.7), channel_id=1, source_target_pairs={{0,2},{2,4},{4,6},{6,8},{8,10},{10,12},{12,14},{14,16},{16,18},{18... | collective-permute-start | bytes 491528 | tf_op jit(solution)/shard_map/ppermute | solution.py:13
  11.1 73.8 %collective-permute-start.1 = (bf16[1280,64]{0,1:T(8,128)(2,1)}, bf16[1280,64]{0,1:T(8,128)(2,1)S(1)}, u32[]{:S(2)}, u32[]{:S(2)}) collective-permute-start(bf16[1280,64]{0,1:T(8,128)(2,1)} %param.7), channel_id=1, source_target_pairs={{2,0},{4,2},{6,4},{8,6},{10,8},{12,10},{14,12},{16,14},{18,16},{20... | collective-permute-start | bytes 491528 | tf_op jit(solution)/shard_map/ppermute | solution.py:13
  58.4 17.0 %copy-start.2 = (bf16[1280,64]{0,1:T(8,128)(2,1)S(1)}, bf16[1280,64]{0,1:T(8,128)(2,1)}, u32[]{:S(2)}) copy-start(bf16[1280,64]{0,1:T(8,128)(2,1)} %param.7) | copy-start | bytes 491524
  75.4 8.0 %copy-start = (bf16[10,17,256,128]{3,2,1,0:T(8,128)(2,1)S(1)}, bf16[10,17,256,128]{3,2,1,0:T(8,128)(2,1)}, u32[]{:S(2)}) copy-start(bf16[10,17,256,128]{3,2,1,0:T(8,128)(2,1)} %constant_dynamic-update-slice_fusion) | copy-start | bytes 33423364
  87.9 7.6 %collective-permute-start.3 = (bf16[1280,64]{0,1:T(8,128)(2,1)S(1)}, bf16[1280,64]{0,1:T(8,128)(2,1)S(1)}, u32[]{:S(2)}, u32[]{:S(2)}) collective-permute-start(bf16[1280,64]{0,1:T(8,128)(2,1)S(1)} %copy_bitcast_fusion.1), channel_id=1, source_target_pairs={{2,0},{4,2},{6,4},{8,6},{10,8},{12,10},{14,12},{16,14},{18,16},{20... | collective-permute-start | bytes 491528 | tf_op jit(solution)/shard_map/ppermute | solution.py:13
  89.8 7.5 %collective-permute-start.2 = (bf16[1280,64]{0,1:T(8,128)(2,1)S(1)}, bf16[1280,64]{0,1:T(8,128)(2,1)S(1)}, u32[]{:S(2)}, u32[]{:S(2)}) collective-permute-start(bf16[1280,64]{0,1:T(8,128)(2,1)S(1)} %copy_bitcast_fusion.1), channel_id=1, source_target_pairs={{0,2},{2,4},{4,6},{6,8},{8,10},{10,12},{12,14},{14,16},{16,18},{18... | collective-permute-start | bytes 491528 | tf_op jit(solution)/shard_map/ppermute | solution.py:13
  103.6 7.7 %collective-permute-start.5 = (bf16[1280,64]{0,1:T(8,128)(2,1)S(1)}, bf16[1280,64]{0,1:T(8,128)(2,1)S(1)}, u32[]{:S(2)}, u32[]{:S(2)}) collective-permute-start(bf16[1280,64]{0,1:T(8,128)(2,1)S(1)} %fusion.7), channel_id=1, source_target_pairs={{2,0},{4,2},{6,4},{8,6},{10,8},{12,10},{14,12},{16,14},{18,16},{20... | collective-permute-start | bytes 491528 | tf_op jit(solution)/shard_map/ppermute | solution.py:13
  105.5 7.3 %collective-permute-start.4 = (bf16[1280,64]{0,1:T(8,128)(2,1)S(1)}, bf16[1280,64]{0,1:T(8,128)(2,1)S(1)}, u32[]{:S(2)}, u32[]{:S(2)}) collective-permute-start(bf16[1280,64]{0,1:T(8,128)(2,1)S(1)} %fusion.7), channel_id=1, source_target_pairs={{0,2},{2,4},{4,6},{6,8},{8,10},{10,12},{12,14},{14,16},{16,18},{18... | collective-permute-start | bytes 491528 | tf_op jit(solution)/shard_map/ppermute | solution.py:13
  119.0 8.2 %collective-permute-start.7 = (bf16[1280,64]{0,1:T(8,128)(2,1)S(1)}, bf16[1280,64]{0,1:T(8,128)(2,1)S(1)}, u32[]{:S(2)}, u32[]{:S(2)}) collective-permute-start(bf16[1280,64]{0,1:T(8,128)(2,1)S(1)} %fusion.6), channel_id=1, source_target_pairs={{2,0},{4,2},{6,4},{8,6},{10,8},{12,10},{14,12},{16,14},{18,16},{20... | collective-permute-start | bytes 491528 | tf_op jit(solution)/shard_map/ppermute | solution.py:13
  120.9 7.7 %collective-permute-start.6 = (bf16[1280,64]{0,1:T(8,128)(2,1)S(1)}, bf16[1280,64]{0,1:T(8,128)(2,1)S(1)}, u32[]{:S(2)}, u32[]{:S(2)}) collective-permute-start(bf16[1280,64]{0,1:T(8,128)(2,1)S(1)} %fusion.6), channel_id=1, source_target_pairs={{0,2},{2,4},{4,6},{6,8},{8,10},{10,12},{12,14},{14,16},{16,18},{18... | collective-permute-start | bytes 491528 | tf_op jit(solution)/shard_map/ppermute | solution.py:13
  134.9 19.2 %copy-start.1 = (bf16[1280,64]{0,1:T(8,128)(2,1)}, bf16[1280,64]{0,1:T(8,128)(2,1)S(1)}, u32[]{:S(2)}) copy-start(bf16[1280,64]{0,1:T(8,128)(2,1)S(1)} %fusion.5) | copy-start | bytes 491524
  134.9 10.7 %collective-permute-start.9 = (bf16[1280,64]{0,1:T(8,128)(2,1)S(1)}, bf16[1280,64]{0,1:T(8,128)(2,1)S(1)}, u32[]{:S(2)}, u32[]{:S(2)}) collective-permute-start(bf16[1280,64]{0,1:T(8,128)(2,1)S(1)} %fusion.5), channel_id=1, source_target_pairs={{2,0},{4,2},{6,4},{8,6},{10,8},{12,10},{14,12},{16,14},{18,16},{20... | collective-permute-start | bytes 491528 | tf_op jit(solution)/shard_map/ppermute | solution.py:13
  136.8 9.0 %collective-permute-start.8 = (bf16[1280,64]{0,1:T(8,128)(2,1)S(1)}, bf16[1280,64]{0,1:T(8,128)(2,1)S(1)}, u32[]{:S(2)}, u32[]{:S(2)}) collective-permute-start(bf16[1280,64]{0,1:T(8,128)(2,1)S(1)} %fusion.5), channel_id=1, source_target_pairs={{0,2},{2,4},{4,6},{6,8},{8,10},{10,12},{12,14},{14,16},{16,18},{18... | collective-permute-start | bytes 491528 | tf_op jit(solution)/shard_map/ppermute | solution.py:13
Sparse Core Ops, SparseCore 0:
  155.1 225.0 all-reduce.2
where the time goes:
time: 391 us; the launch traced here: 388 us
  waiting for transfers between devices  234 us (60%)
  local copies, waits for them, and re-layouts  50.5 us (13%)
  matrix products  49.3 us (13%)
  starting transfers between devices  32.6 us (8%)
  between operations  14.5 us (4%)
  blocking collectives  4.3 us (1%)
    psum x1, waiting for transfers between devices, body(): gram_sum, proj_sum = lax.psum((gram_part, proj_part), 'row')  225 us
    dot_general x85, matrix products, apply_local(): jnp.einsum('rij,rjm->rim', banded[:, offset], window, preferred_element_t...  35.8 us
    ppermute x10, starting transfers between devices, from_behind(): lax.ppermute(value, axis, [(source, source + steps) for source in range(f...  32.6 us
    reshape x1, local copies, waits for them, and re-layouts, build_band(): flat_blocks = hamiltonian.reshape(block_rows, slot_count, B * B)  16.4 us
    dot_general x1, matrix products, build_band(): lax.dot_general(selector, flat_blocks, (((2,), (1,)), ((0,), (0,))), pref...  11.7 us
    reshape x1, local copies, waits for them, and re-layouts, build_band(): low_part.reshape(block_rows, 2 * DIST + 1, B, B)  9.75 us
    reshape x1, local copies, waits for them, and re-layouts, build_band(): high_part.reshape(block_rows, 2 * DIST + 1, B, B)  9.72 us
    ppermute x10, waiting for transfers between devices, from_behind(): lax.ppermute(value, axis, [(source, source + steps) for source in range(f...  8.37 us
  transfers between devices with their start and end apart: 11, of which 7 were waited for; matrix products, arithmetic and copies ran while one was open for 19% of the time, Pallas kernels for 0%

commit v1 on v0

v1 whole, which is shorter than its diff:
```python
import jax
import jax.numpy as jnp
from jax import lax
from jax.experimental import pallas as pl
from jax.experimental.pallas import tpu as pltpu
from jax.sharding import Mesh, PartitionSpec as P

B = 128
DIST = 8
ROWS = ("x", "y", "z")
SURE = 16
CHUNK = 4
NT = (((1,), (1,)), ((), ()))
MIB = 1024 * 1024


def dot_nt(a, b):
    return lax.dot_general(a, b, NT, preferred_element_type=jnp.float32)


def slot_order(neighbours, counts, first_block):
    slot_count = neighbours.shape[1]
    slots = jnp.arange(slot_count, dtype=jnp.int32)[None, :]
    column = neighbours - first_block + DIST
    dead = neighbours.shape[0] + 2 * DIST
    key = jnp.where(slots < counts[:, None], column, dead) * slot_count + slots
    rank = jnp.sum((key[:, None, :] < key[:, :, None]).astype(jnp.int32), axis=2)
    picked = rank[:, :, None] == slots[:, None, :]
    return jnp.sum(jnp.where(picked, key[:, :, None], 0), axis=1)


def band_kernel(key_ref, count_ref, h_ref, a_ref, held, sems):
    block_rows, slot_count = held.shape[:2]
    extra = (slot_count - SURE) // CHUNK

    def part(r, k):
        if k < 0:
            rows = pl.ds(0, SURE)
        else:
            rows = pl.ds(SURE + k * CHUNK, CHUNK)
        return pltpu.make_async_copy(h_ref.at[r, rows], held.at[r, rows], sems.at[r, k + 1])

    def start(r, _):
        part(r, -1).start()
        for k in range(extra):
            pl.when(count_ref[r] > SURE + k * CHUNK)(lambda k=k: part(r, k).start())
        return 0

    lax.fori_loop(0, block_rows, start, 0)

    def one_row(r, _):
        rows = pl.ds(pl.multiple_of(r * B, B), B)
        base = pl.multiple_of((r // 2) * (2 * B), 2 * B)
        a_ref[rows, pl.ds(base, 18 * B)] = jnp.zeros((B, 18 * B), a_ref.dtype)
        part(r, -1).wait()
        for k in range(extra):
            pl.when(count_ref[r] > SURE + k * CHUNK)(lambda k=k: part(r, k).wait())

        def group(g, carry):
            total, last = carry
            for u in range(4):
                key = key_ref[r, g * 4 + u]
                column = key // slot_count
                slot = key % slot_count
                block = held[r, slot].astype(jnp.float32)
                total = jnp.where(column == last, total, 0.0) + block
                last = column
                lanes = pl.ds(pl.multiple_of(column * B, B), B)
                a_ref[rows, lanes] = total.astype(a_ref.dtype)
            return total, last

        groups = (count_ref[r] + 3) // 4
        lax.fori_loop(0, groups, group, (jnp.zeros((B, B), jnp.float32), jnp.int32(-1)))
        return 0

    lax.fori_loop(0, block_rows, one_row, 0)


def build_band(keys, counts, hamiltonian):
    block_rows, slot_count = hamiltonian.shape[:2]
    width = (block_rows + 2 * DIST + 1) * B
    return pl.pallas_call(
        band_kernel,
        out_shape=pltpu.VMEM((block_rows * B, width), jnp.bfloat16),
        in_specs=[
            pl.BlockSpec(memory_space=pltpu.SMEM),
            pl.BlockSpec(memory_space=pltpu.SMEM),
            pl.BlockSpec(memory_space=pltpu.HBM),
        ],
        out_specs=pl.BlockSpec(memory_space=pltpu.VMEM),
        scratch_shapes=[
            pltpu.VMEM(hamiltonian.shape, hamiltonian.dtype),
            pltpu.SemaphoreType.DMA((block_rows, 1 + (slot_count - SURE) // CHUNK)),
        ],
        compiler_params=pltpu.CompilerParams(vmem_limit_bytes=46 * MIB),
        name="band",
    )(keys, counts, hamiltonian)


def own_kernel(v_ref, a_ref, acc_ref):
    rows = acc_ref.shape[1]
    v = v_ref[...]
    for i in range(0, rows, 2 * B):
        acc_ref[:, i : i + 2 * B] = dot_nt(v, a_ref[i : i + 2 * B, DIST * B : DIST * B + rows])


def apply_halo(acc_ref, low_ref, high_ref, a_ref):
    rows = acc_ref.shape[1]
    step = 2 * B
    upper = DIST * B + rows
    for i in range(0, rows, step):
        total = acc_ref[:, i : i + step]
        if i < DIST * B:
            total += dot_nt(low_ref[:, i:], a_ref[i : i + step, i : DIST * B])
        depth = i + step - (rows - DIST * B)
        if depth > 0:
            total += dot_nt(high_ref[:, :depth], a_ref[i : i + step, upper : upper + depth])
        yield i, step, total


def first_kernel(acc_ref, low_ref, high_ref, a_ref, new_ref, top_ref, bottom_ref):
    for i, step, total in apply_halo(acc_ref, low_ref, high_ref, a_ref):
        new_ref[:, i : i + step] = total.astype(new_ref.dtype)
    halos(new_ref, top_ref, bottom_ref)


def halos(new_ref, top_ref, bottom_ref):
    reach = DIST * B
    top_ref[...] = new_ref[:, new_ref.shape[1] - reach :]
    bottom_ref[...] = new_ref[:, :reach]


def next_kernel(acc_ref, low_ref, high_ref, a_ref, older_ref, new_ref, top_ref, bottom_ref):
    for i, step, total in apply_halo(acc_ref, low_ref, high_ref, a_ref):
        older = older_ref[:, i : i + step].astype(jnp.float32)
        new_ref[:, i : i + step] = (2.0 * total - older).astype(new_ref.dtype)
    halos(new_ref, top_ref, bottom_ref)


def image_kernel(acc_ref, low_ref, high_ref, a_ref, new_ref):
    for i, step, total in apply_halo(acc_ref, low_ref, high_ref, a_ref):
        new_ref[:, i : i + step] = total.astype(new_ref.dtype)


def in_vmem(kernel, name, outs, *args, flops=0):
    specs = [pl.BlockSpec(memory_space=pltpu.VMEM)]
    return pl.pallas_call(
        kernel,
        out_shape=[pltpu.VMEM(s, d) for s, d in outs],
        in_specs=specs * len(args),
        out_specs=specs * len(outs),
        compiler_params=pltpu.CompilerParams(vmem_limit_bytes=16 * MIB),
        cost_estimate=pl.CostEstimate(flops=flops, bytes_accessed=0, transcendentals=0),
        name=name,
    )(*args)


def gram_kernel(band_ref, own_ref, other_ref, image_ref, other_image_ref, out_ref):
    own = own_ref[...]
    half = own.shape[0]
    is_first = band_ref[0] == 0

    def both(mine, others):
        a, b = dot_nt(own, mine), dot_nt(own, others)
        return jnp.concatenate([jnp.where(is_first, a, b), jnp.where(is_first, b, a)], axis=1)

    out_ref[:half, :] = both(own, other_ref[...])
    out_ref[half:, :] = both(image_ref[...], other_image_ref[...])


def exchange_halos(top, bottom):
    count = lax.axis_size(ROWS)
    up = [(i, (i + 1) % count) for i in range(count)]
    down = [(target, source) for source, target in up]
    return lax.ppermute(top, ROWS, up), lax.ppermute(bottom, ROWS, down)


def swapped(value, axis, distance):
    count = lax.axis_size(axis)
    return lax.ppermute(value, axis, [(i, i ^ distance) for i in range(count)])


def sum_over_rows(value):
    for axis in ("z", "y", "x"):
        one, two, three = (swapped(value, axis, k) for k in (1, 2, 3))
        value = (value + one) + (two + three)
    return value + swapped(value, "z", 4)


def body(hamiltonian, neighbours, counts, vectors):
    block_rows = hamiltonian.shape[0]
    rows, width = vectors.shape
    reach = DIST * B
    first_block = lax.axis_index(ROWS) * block_rows
    field = ((width, rows), jnp.bfloat16)
    halo = ((width, reach), jnp.bfloat16)
    part = ((width, rows), jnp.float32)
    own_flops = 2 * width * rows * rows

    def own_part(v, name):
        return in_vmem(own_kernel, name, [part], v, band, flops=own_flops)[0]

    start = vectors.T
    low, high = exchange_halos(start[:, rows - reach :], start[:, :reach])
    keys = slot_order(neighbours, counts, first_block)
    band = build_band(keys, counts, hamiltonian)
    acc = own_part(start, "own1")
    level1, top, bottom = in_vmem(first_kernel, "level1", [field, halo, halo], acc, low, high, band)
    older, newer = start, level1
    for degree in range(2, 5):
        low, high = exchange_halos(top, bottom)
        acc = own_part(newer, "own%d" % degree)
        latest, top, bottom = in_vmem(
            next_kernel, "level%d" % degree, [field, halo, halo], acc, low, high, band, older
        )
        older, newer = newer, latest
    low, high = exchange_halos(top, bottom)
    acc = own_part(newer, "own5")
    other = swapped(newer, "band", 1)
    (image,) = in_vmem(image_kernel, "image", [field], acc, low, high, band)
    other_image = swapped(image, "band", 1)
    both = ((2 * width, 2 * width), jnp.float32)
    index = lax.axis_index("band").astype(jnp.int32).reshape(1)
    sums = pl.pallas_call(
        gram_kernel,
        out_shape=jax.ShapeDtypeStruct((2 * width, 2 * width), jnp.float32),
        in_specs=[pl.BlockSpec(memory_space=pltpu.SMEM)]
        + [pl.BlockSpec(memory_space=pltpu.VMEM)] * 4,
        out_specs=pl.BlockSpec(memory_space=pltpu.VMEM),
        compiler_params=pltpu.CompilerParams(vmem_limit_bytes=16 * MIB),
        name="gram",
    )(index, newer, other, image, other_image)
    sums = sum_over_rows(sums) * (1.0 / (rows * lax.axis_size(ROWS)))
    return newer.T, sums[:width], sums[width:]


def solution(mesh):
    shape = tuple(mesh.shape[name] for name in mesh.axis_names)
    chips = Mesh(mesh.devices.reshape(4, 4, 8, shape[1]), (*ROWS, "band"))
    return jax.shard_map(
        body,
        mesh=chips,
        in_specs=(P(ROWS, None, None, None), P(ROWS, None), P(ROWS), P(ROWS, "band")),
        out_specs=(P(ROWS, "band"), P("band", None), P("band", None)),
        check_vma=False,
    )
```

time: 391 us -> 103 us (0.26)
  waiting for transfers between devices: 234 us -> 22.2 us
  matrix products: 49.3 us -> 0 us
  local copies, waits for them, and re-layouts: 50.5 us -> 2.36 us
  starting transfers between devices: 32.6 us -> 58.6 us
  Pallas kernels: 0 us -> 17.2 us
  between operations: 14.5 us -> 0.82 us
  blocking collectives: 4.3 us -> 0 us
    psum x1 -> x0, waiting for transfers between devices: 225 us -> none  [body(): gram_sum, proj_sum = lax.psum((gram_part, proj_part), 'row')]
    dot_general x88 -> x0, matrix products: 49.3 us -> none  [the longest x85 35.8 us: apply_local(): jnp.einsum('rij,rjm->rim', banded[:, offset], window, preferred_element_t...]
    reshape x3 -> x0, local copies, waits for them, and re-layouts: 35.8 us -> none  [the longest x1 16.4 us: build_band(): flat_blocks = hamiltonian.reshape(block_rows, slot_count, B * B)]
    ppermute x10 -> x22, starting transfers between devices: 32.6 us -> 58.6 us  [the longest x10 32.4 us: exchange_halos(): return (lax.ppermute(top, ROWS, up), lax.ppermute(bottom, ROWS, down))]
    pallas_call x0 -> x12, Pallas kernels: none -> 17.2 us  [the longest x10 10.1 us: in_vmem(): pl.pallas_call(kernel, out_shape=[pltpu.VMEM(s, d) for s, d in outs], in_...]
    ppermute x10 -> x22, waiting for transfers between devices: 8.37 us -> 22.2 us  [the longest x12 13.1 us: swapped(): return lax.ppermute(value, axis, [(i, i ^ distance) for i in range(count)])]
    concatenate x1 -> x0, local copies, waits for them, and re-layouts: 7.23 us -> none  [build_band(): jnp.concatenate([high_part.reshape(block_rows, 2 * DIST + 1, B, B), low_p...]
    unnamed x11 -> x3, local copies, waits for them, and re-layouts: 7.36 us -> 0.67 us
  transfers between devices with their start and end apart: 11 -> 22, of which waited for: 7 -> 12; matrix products, arithmetic and copies ran while one was open for 19% -> 2% of each run, Pallas kernels for 0% -> 13%
where the time goes in v1:
time: 103 us
  starting transfers between devices  58.6 us (57%)
  waiting for transfers between devices  22.2 us (22%)
  Pallas kernels  17.2 us (17%)
  local copies, waits for them, and re-layouts  2.36 us (2%)
  other arithmetic  1.93 us (2%)
    ppermute x10, starting transfers between devices, exchange_halos(): return (lax.ppermute(top, ROWS, up), lax.ppermute(bottom, ROWS, down))  32.4 us
    ppermute x12, starting transfers between devices, swapped(): return lax.ppermute(value, axis, [(i, i ^ distance) for i in range(count)])  26.2 us
    ppermute x12, waiting for transfers between devices, swapped(): return lax.ppermute(value, axis, [(i, i ^ distance) for i in range(count)])  13.1 us
    pallas_call x10, Pallas kernels, in_vmem(): pl.pallas_call(kernel, out_shape=[pltpu.VMEM(s, d) for s, d in outs], in_...  10.1 us
    ppermute x10, waiting for transfers between devices, exchange_halos(): return (lax.ppermute(top, ROWS, up), lax.ppermute(bottom, ROWS, down))  9.08 us
    pallas_call x1, Pallas kernels, build_band(): pl.pallas_call(band_kernel, out_shape=pltpu.VMEM((block_rows * B, width),...  6.64 us
  transfers between devices with their start and end apart: 22, of which 12 were waited for; matrix products, arithmetic and copies ran while one was open for 2% of the time, Pallas kernels for 13%

profile of v1, /device:TPU:32, one launch (start us, length us, event | category | flops | bytes accessed | tf_op | source)
XLA Modules:
  0.0 103.1 jit_solution(9720560780145826206)
XLA Ops:
  0.6 1.1 %fusion = (bf16[64,1024]{1,0:T(8,128)(2,1)S(1)}, bf16[64,1024]{1,0:T(8,128)(2,1)S(1)}) fusion(bf16[64,1280]{1,0:T(8,128)(2,1)} %bitcast.4), kind=kLoop, calls=%fused_computation.9 | loop fusion | bytes 524288 | tf_op jit(solution)/shard_map/slice | solution.py:204
  1.7 1.9 %collective-permute-start.1 = (bf16[64,1024]{1,0:T(8,128)(2,1)S(1)}, bf16[64,1024]{1,0:T(8,128)(2,1)S(1)}, u32[]{:S(2)}, u32[]{:S(2)}) collective-permute-start(bf16[64,1024]{1,0:T(8,128)(2,1)S(1)} %get-tuple-element.27), channel_id=1, source_target_pairs={{2,0},{4,2},{6,4},{8,6},{10,8},{12,10},{14,12},{16,14},{18,16},{20... | collective-permute-start | bytes 393224 | tf_op jit(solution)/shard_map/ppermute | solution.py:175
  3.6 0.2 collective-permute-start
  3.8 0.8 iota_add_fusion
  4.6 0.3 convert_reduce_fusion
  4.9 0.8 select_reduce_fusion.key_ref
  5.7 6.6 %band.1.a_ref = bf16[1280,3456]{1,0:T(8,128)(2,1)S(1)} custom-call(s32[10,32]{1,0:T(8,128)} %select_reduce_fusion.key_ref, s32[10]{0:T(128)} %count_ref.1, bf16[10,32,128,128]{3,2,1,0:T(8,128)(2,1)} %h_ref.1), custom_call_target="tpu_custom_call" | custom-call | tf_op jit(solution)/shard_map/band/pallas_call | solution.py:82
  12.3 1.1 %own1.1.acc_ref = f32[64,1280]{1,0:T(8,128)S(1)} custom-call(bf16[64,1280]{1,0:T(8,128)(2,1)S(1)} %bitcast.5, bf16[1280,3456]{1,0:T(8,128)(2,1)S(1)} %band.1.a_ref), custom_call_target="tpu_custom_call" | custom-call | flops 209715200 | tf_op jit(solution)/shard_map/own1/pallas_call | solution.py:147
  13.5 2.1 %collective-permute-done.low_ref = bf16[64,1024]{1,0:T(8,128)(2,1)S(1)} collective-permute-done((bf16[64,1024]{1,0:T(8,128)(2,1)S(1)}, bf16[64,1024]{1,0:T(8,128)(2,1)S(1)}, u32[]{:S(2)}, u32[]{:S(2)}) %collective-permute-start) | collective-permute-done | bytes 131104 | tf_op jit(solution)/shard_map/ppermute | solution.py:175
  15.6 0.9 level1.1
  16.5 0.1 collective-permute-start.2
  16.6 7.3 %collective-permute-start.3 = (bf16[64,1024]{1,0:T(8,128)(2,1)S(1)}, bf16[64,1024]{1,0:T(8,128)(2,1)S(1)}, u32[]{:S(2)}, u32[]{:S(2)}) collective-permute-start(bf16[64,1024]{1,0:T(8,128)(2,1)S(1)} %get-tuple-element.17), channel_id=1, source_target_pairs={{2,0},{4,2},{6,4},{8,6},{10,8},{12,10},{14,12},{16,14},{18,16},{20... | collective-permute-start | bytes 393224 | tf_op jit(solution)/shard_map/ppermute | solution.py:175
  23.9 1.1 %own2.1.acc_ref = f32[64,1280]{1,0:T(8,128)S(1)} custom-call(bf16[64,1280]{1,0:T(8,128)(2,1)S(1)} %get-tuple-element.15.v_ref.older_ref, bf16[1280,3456]{1,0:T(8,128)(2,1)S(1)} %band.1.a_ref), custom_call_target="tpu_custom_call" | custom-call | flops 209715200 | tf_op jit(solution)/shard_map/own2/pallas_call | solution.py:147
  25.0 1.7 %collective-permute-done.2.low_ref = bf16[64,1024]{1,0:T(8,128)(2,1)S(1)} collective-permute-done((bf16[64,1024]{1,0:T(8,128)(2,1)S(1)}, bf16[64,1024]{1,0:T(8,128)(2,1)S(1)}, u32[]{:S(2)}, u32[]{:S(2)}) %collective-permute-start.2) | collective-permute-done | bytes 131104 | tf_op jit(solution)/shard_map/ppermute | solution.py:175
  26.7 0.9 level2.1
  27.6 0.1 collective-permute-start.4
  27.7 7.5 %collective-permute-start.5 = (bf16[64,1024]{1,0:T(8,128)(2,1)S(1)}, bf16[64,1024]{1,0:T(8,128)(2,1)S(1)}, u32[]{:S(2)}, u32[]{:S(2)}) collective-permute-start(bf16[64,1024]{1,0:T(8,128)(2,1)S(1)} %get-tuple-element.20), channel_id=1, source_target_pairs={{2,0},{4,2},{6,4},{8,6},{10,8},{12,10},{14,12},{16,14},{18,16},{20... | collective-permute-start | bytes 393224 | tf_op jit(solution)/shard_map/ppermute | solution.py:175
  35.3 1.1 %own3.1.acc_ref = f32[64,1280]{1,0:T(8,128)S(1)} custom-call(bf16[64,1280]{1,0:T(8,128)(2,1)S(1)} %get-tuple-element.18.v_ref.older_ref, bf16[1280,3456]{1,0:T(8,128)(2,1)S(1)} %band.1.a_ref), custom_call_target="tpu_custom_call" | custom-call | flops 209715200 | tf_op jit(solution)/shard_map/own3/pallas_call | solution.py:147
  36.4 1.7 %collective-permute-done.4.low_ref = bf16[64,1024]{1,0:T(8,128)(2,1)S(1)} collective-permute-done((bf16[64,1024]{1,0:T(8,128)(2,1)S(1)}, bf16[64,1024]{1,0:T(8,128)(2,1)S(1)}, u32[]{:S(2)}, u32[]{:S(2)}) %collective-permute-start.4) | collective-permute-done | bytes 131104 | tf_op jit(solution)/shard_map/ppermute | solution.py:175
  38.1 0.9 level3.1
  39.1 7.5 %collective-permute-start.7 = (bf16[64,1024]{1,0:T(8,128)(2,1)S(1)}, bf16[64,1024]{1,0:T(8,128)(2,1)S(1)}, u32[]{:S(2)}, u32[]{:S(2)}) collective-permute-start(bf16[64,1024]{1,0:T(8,128)(2,1)S(1)} %get-tuple-element.23), channel_id=1, source_target_pairs={{2,0},{4,2},{6,4},{8,6},{10,8},{12,10},{14,12},{16,14},{18,16},{20... | collective-permute-start | bytes 393224 | tf_op jit(solution)/shard_map/ppermute | solution.py:175
  46.7 1.1 %own4.1.acc_ref = f32[64,1280]{1,0:T(8,128)S(1)} custom-call(bf16[64,1280]{1,0:T(8,128)(2,1)S(1)} %get-tuple-element.21.v_ref, bf16[1280,3456]{1,0:T(8,128)(2,1)S(1)} %band.1.a_ref), custom_call_target="tpu_custom_call" | custom-call | flops 209715200 | tf_op jit(solution)/shard_map/own4/pallas_call | solution.py:147
  47.8 1.7 %collective-permute-done.6.low_ref = bf16[64,1024]{1,0:T(8,128)(2,1)S(1)} collective-permute-done((bf16[64,1024]{1,0:T(8,128)(2,1)S(1)}, bf16[64,1024]{1,0:T(8,128)(2,1)S(1)}, u32[]{:S(2)}, u32[]{:S(2)}) %collective-permute-start.6) | collective-permute-done | bytes 131104 | tf_op jit(solution)/shard_map/ppermute | solution.py:175
  49.5 0.9 level4.1
  50.5 7.6 %collective-permute-start.10 = (bf16[64,1024]{1,0:T(8,128)(2,1)S(1)}, bf16[64,1024]{1,0:T(8,128)(2,1)S(1)}, u32[]{:S(2)}, u32[]{:S(2)}) collective-permute-start(bf16[64,1024]{1,0:T(8,128)(2,1)S(1)} %get-tuple-element.26), channel_id=1, source_target_pairs={{2,0},{4,2},{6,4},{8,6},{10,8},{12,10},{14,12},{16,14},{18,16},{20... | collective-permute-start | bytes 393224 | tf_op jit(solution)/shard_map/ppermute | solution.py:175
  58.1 1.1 %own5.1.acc_ref = f32[64,1280]{1,0:T(8,128)S(1)} custom-call(bf16[64,1280]{1,0:T(8,128)(2,1)S(1)} %get-tuple-element.24.v_ref.own_ref, bf16[1280,3456]{1,0:T(8,128)(2,1)S(1)} %band.1.a_ref), custom_call_target="tpu_custom_call" | custom-call | flops 209715200 | tf_op jit(solution)/shard_map/own5/pallas_call | solution.py:147
  59.3 1.7 %collective-permute-done.9.low_ref = bf16[64,1024]{1,0:T(8,128)(2,1)S(1)} collective-permute-done((bf16[64,1024]{1,0:T(8,128)(2,1)S(1)}, bf16[64,1024]{1,0:T(8,128)(2,1)S(1)}, u32[]{:S(2)}, u32[]{:S(2)}) %collective-permute-start.9) | collective-permute-done | bytes 131104 | tf_op jit(solution)/shard_map/ppermute | solution.py:175
  61.0 0.9 image.1.image_ref
  61.9 0.1 collective-permute-start.11
  62.0 1.4 %collective-permute-done.11.other_image_ref = bf16[64,1280]{1,0:T(8,128)(2,1)S(1)} collective-permute-done((bf16[64,1280]{1,0:T(8,128)(2,1)S(1)}, bf16[64,1280]{1,0:T(8,128)(2,1)S(1)}, u32[]{:S(2)}, u32[]{:S(2)}) %collective-permute-start.11) | collective-permute-done | bytes 163872 | tf_op jit(solution)/shard_map/ppermute | solution.py:180
  63.4 0.4 gram.1
  63.8 0.1 collective-permute-start.14
  63.9 9.9 %collective-permute-start.13 = (f32[128,128]{1,0:T(8,128)S(1)}, f32[128,128]{1,0:T(8,128)S(1)}, u32[]{:S(2)}, u32[]{:S(2)}) collective-permute-start(f32[128,128]{1,0:T(8,128)S(1)} %gram.1), channel_id=1, source_target_pairs={{0,4},{2,6},{4,0},{6,2},{8,12},{10,14},{12,8},{14,10},{1,5},{3,7},... | collective-permute-start | bytes 196616 | tf_op jit(solution)/shard_map/ppermute | solution.py:180
  73.8 4.3 %collective-permute-done.13 = f32[128,128]{1,0:T(8,128)S(1)} collective-permute-done((f32[128,128]{1,0:T(8,128)S(1)}, f32[128,128]{1,0:T(8,128)S(1)}, u32[]{:S(2)}, u32[]{:S(2)}) %collective-permute-start.13) | collective-permute-done | bytes 65568 | tf_op jit(solution)/shard_map/ppermute | solution.py:180
  78.0 0.1 collective-permute-start.17
  78.1 0.1 collective-permute-start.16
  78.2 4.0 %collective-permute-start.15 = (f32[128,128]{1,0:T(8,128)S(1)}, f32[128,128]{1,0:T(8,128)S(1)}, u32[]{:S(2)}, u32[]{:S(2)}) collective-permute-start(f32[128,128]{1,0:T(8,128)S(1)} %add_add_fusion.2), channel_id=1, source_target_pairs={{0,16},{16,0},{32,48},{48,32},{1,17},{17,1},{33,49},{49,33},{2,18}... | collective-permute-start | bytes 196616 | tf_op jit(solution)/shard_map/ppermute | solution.py:180
  82.2 2.1 %collective-permute-done.17 = f32[128,128]{1,0:T(8,128)S(1)} collective-permute-done((f32[128,128]{1,0:T(8,128)S(1)}, f32[128,128]{1,0:T(8,128)S(1)}, u32[]{:S(2)}, u32[]{:S(2)}) %collective-permute-start.17) | collective-permute-done | bytes 65568 | tf_op jit(solution)/shard_map/ppermute | solution.py:180
  84.3 0.9 collective-permute-done.15
  85.2 0.1 collective-permute-start.20
  85.3 0.1 collective-permute-start.19
  85.4 4.0 %collective-permute-start.18 = (f32[128,128]{1,0:T(8,128)S(1)}, f32[128,128]{1,0:T(8,128)S(1)}, u32[]{:S(2)}, u32[]{:S(2)}) collective-permute-start(f32[128,128]{1,0:T(8,128)S(1)} %add_add_fusion.1), channel_id=1, source_target_pairs={{0,64},{64,0},{128,192},{192,128},{1,65},{65,1},{129,193},{193,129... | collective-permute-start | bytes 196616 | tf_op jit(solution)/shard_map/ppermute | solution.py:180
  89.4 2.1 %collective-permute-done.20 = f32[128,128]{1,0:T(8,128)S(1)} collective-permute-done((f32[128,128]{1,0:T(8,128)S(1)}, f32[128,128]{1,0:T(8,128)S(1)}, u32[]{:S(2)}, u32[]{:S(2)}) %collective-permute-start.20) | collective-permute-done | bytes 65568 | tf_op jit(solution)/shard_map/ppermute | solution.py:180
  91.5 0.9 collective-permute-done.18
  92.3 7.8 %collective-permute-start.21 = (f32[128,128]{1,0:T(8,128)S(1)}, f32[128,128]{1,0:T(8,128)S(1)}, u32[]{:S(2)}, u32[]{:S(2)}) collective-permute-start(f32[128,128]{1,0:T(8,128)S(1)} %add_add_fusion), channel_id=1, source_target_pairs={{0,8},{2,10},{4,12},{6,14},{8,0},{10,2},{12,4},{14,6},{1,9},{3,11}... | collective-permute-start | bytes 196616 | tf_op jit(solution)/shard_map/ppermute | solution.py:180
  100.2 0.7 copy.7
  100.8 1.6 %collective-permute-done.21 = f32[128,128]{1,0:T(8,128)S(1)} collective-permute-done((f32[128,128]{1,0:T(8,128)S(1)}, f32[128,128]{1,0:T(8,128)S(1)}, u32[]{:S(2)}, u32[]{:S(2)}) %collective-permute-start.21) | collective-permute-done | bytes 65568 | tf_op jit(solution)/shard_map/ppermute | solution.py:180
  102.4 0.6 fusion.1
  (20 shorter events, 0.3 us)
Async XLA Ops:
  0.6 11.7 %copy-start = (bf16[1280,64]{0,1:T(8,128)(2,1)S(1)}, bf16[1280,64]{0,1:T(8,128)(2,1)}, u32[]{:S(2)}) copy-start(bf16[1280,64]{0,1:T(8,128)(2,1)} %param.7) | copy-start | bytes 491524
  1.7 11.8 %collective-permute-start.1 = (bf16[64,1024]{1,0:T(8,128)(2,1)S(1)}, bf16[64,1024]{1,0:T(8,128)(2,1)S(1)}, u32[]{:S(2)}, u32[]{:S(2)}) collective-permute-start(bf16[64,1024]{1,0:T(8,128)(2,1)S(1)} %get-tuple-element.27), channel_id=1, source_target_pairs={{2,0},{4,2},{6,4},{8,6},{10,8},{12,10},{14,12},{16,14},{18,16},{20... | collective-permute-start | bytes 393224 | tf_op jit(solution)/shard_map/ppermute | solution.py:175
  3.6 12.0 %collective-permute-start = (bf16[64,1024]{1,0:T(8,128)(2,1)S(1)}, bf16[64,1024]{1,0:T(8,128)(2,1)S(1)}, u32[]{:S(2)}, u32[]{:S(2)}) collective-permute-start(bf16[64,1024]{1,0:T(8,128)(2,1)S(1)} %get-tuple-element.28), channel_id=1, source_target_pairs={{0,2},{2,4},{4,6},{6,8},{8,10},{10,12},{12,14},{14,16},{16,18},{18... | collective-permute-start | bytes 393224 | tf_op jit(solution)/shard_map/ppermute | solution.py:175
  16.5 10.2 %collective-permute-start.2 = (bf16[64,1024]{1,0:T(8,128)(2,1)S(1)}, bf16[64,1024]{1,0:T(8,128)(2,1)S(1)}, u32[]{:S(2)}, u32[]{:S(2)}) collective-permute-start(bf16[64,1024]{1,0:T(8,128)(2,1)S(1)} %get-tuple-element.16), channel_id=1, source_target_pairs={{0,2},{2,4},{4,6},{6,8},{8,10},{10,12},{12,14},{14,16},{16,18},{18... | collective-permute-start | bytes 393224 | tf_op jit(solution)/shard_map/ppermute | solution.py:175
  16.6 10.1 %collective-permute-start.3 = (bf16[64,1024]{1,0:T(8,128)(2,1)S(1)}, bf16[64,1024]{1,0:T(8,128)(2,1)S(1)}, u32[]{:S(2)}, u32[]{:S(2)}) collective-permute-start(bf16[64,1024]{1,0:T(8,128)(2,1)S(1)} %get-tuple-element.17), channel_id=1, source_target_pairs={{2,0},{4,2},{6,4},{8,6},{10,8},{12,10},{14,12},{16,14},{18,16},{20... | collective-permute-start | bytes 393224 | tf_op jit(solution)/shard_map/ppermute | solution.py:175
  27.6 10.5 %collective-permute-start.4 = (bf16[64,1024]{1,0:T(8,128)(2,1)S(1)}, bf16[64,1024]{1,0:T(8,128)(2,1)S(1)}, u32[]{:S(2)}, u32[]{:S(2)}) collective-permute-start(bf16[64,1024]{1,0:T(8,128)(2,1)S(1)} %get-tuple-element.19), channel_id=1, source_target_pairs={{0,2},{2,4},{4,6},{6,8},{8,10},{10,12},{12,14},{14,16},{16,18},{18... | collective-permute-start | bytes 393224 | tf_op jit(solution)/shard_map/ppermute | solution.py:175
  27.7 10.4 %collective-permute-start.5 = (bf16[64,1024]{1,0:T(8,128)(2,1)S(1)}, bf16[64,1024]{1,0:T(8,128)(2,1)S(1)}, u32[]{:S(2)}, u32[]{:S(2)}) collective-permute-start(bf16[64,1024]{1,0:T(8,128)(2,1)S(1)} %get-tuple-element.20), channel_id=1, source_target_pairs={{2,0},{4,2},{6,4},{8,6},{10,8},{12,10},{14,12},{16,14},{18,16},{20... | collective-permute-start | bytes 393224 | tf_op jit(solution)/shard_map/ppermute | solution.py:175
  39.0 10.5 %collective-permute-start.6 = (bf16[64,1024]{1,0:T(8,128)(2,1)S(1)}, bf16[64,1024]{1,0:T(8,128)(2,1)S(1)}, u32[]{:S(2)}, u32[]{:S(2)}) collective-permute-start(bf16[64,1024]{1,0:T(8,128)(2,1)S(1)} %get-tuple-element.22), channel_id=1, source_target_pairs={{0,2},{2,4},{4,6},{6,8},{8,10},{10,12},{12,14},{14,16},{16,18},{18... | collective-permute-start | bytes 393224 | tf_op jit(solution)/shard_map/ppermute | solution.py:175
  39.1 10.4 %collective-permute-start.7 = (bf16[64,1024]{1,0:T(8,128)(2,1)S(1)}, bf16[64,1024]{1,0:T(8,128)(2,1)S(1)}, u32[]{:S(2)}, u32[]{:S(2)}) collective-permute-start(bf16[64,1024]{1,0:T(8,128)(2,1)S(1)} %get-tuple-element.23), channel_id=1, source_target_pairs={{2,0},{4,2},{6,4},{8,6},{10,8},{12,10},{14,12},{16,14},{18,16},{20... | collective-permute-start | bytes 393224 | tf_op jit(solution)/shard_map/ppermute | solution.py:175
  50.4 10.6 %collective-permute-start.9 = (bf16[64,1024]{1,0:T(8,128)(2,1)S(1)}, bf16[64,1024]{1,0:T(8,128)(2,1)S(1)}, u32[]{:S(2)}, u32[]{:S(2)}) collective-permute-start(bf16[64,1024]{1,0:T(8,128)(2,1)S(1)} %get-tuple-element.25), channel_id=1, source_target_pairs={{0,2},{2,4},{4,6},{6,8},{8,10},{10,12},{12,14},{14,16},{16,18},{18... | collective-permute-start | bytes 393224 | tf_op jit(solution)/shard_map/ppermute | solution.py:175
  50.5 10.5 %collective-permute-start.10 = (bf16[64,1024]{1,0:T(8,128)(2,1)S(1)}, bf16[64,1024]{1,0:T(8,128)(2,1)S(1)}, u32[]{:S(2)}, u32[]{:S(2)}) collective-permute-start(bf16[64,1024]{1,0:T(8,128)(2,1)S(1)} %get-tuple-element.26), channel_id=1, source_target_pairs={{2,0},{4,2},{6,4},{8,6},{10,8},{12,10},{14,12},{16,14},{18,16},{20... | collective-permute-start | bytes 393224 | tf_op jit(solution)/shard_map/ppermute | solution.py:175
  58.1 3.9 %collective-permute-start.8 = (bf16[64,1280]{1,0:T(8,128)(2,1)S(1)}, bf16[64,1280]{1,0:T(8,128)(2,1)S(1)}, u32[]{:S(2)}, u32[]{:S(2)}) collective-permute-start(bf16[64,1280]{1,0:T(8,128)(2,1)S(1)} %get-tuple-element.24.v_ref.own_ref), channel_id=1, source_target_pairs={{0,1},{1,0},{2,3},{3,2},{4,5},{5,4},{6,7},{7,6},{8,9},{9,8},{10,11... | collective-permute-start | bytes 491528 | tf_op jit(solution)/shard_map/ppermute | solution.py:180
  61.9 1.5 %collective-permute-start.11 = (bf16[64,1280]{1,0:T(8,128)(2,1)S(1)}, bf16[64,1280]{1,0:T(8,128)(2,1)S(1)}, u32[]{:S(2)}, u32[]{:S(2)}) collective-permute-start(bf16[64,1280]{1,0:T(8,128)(2,1)S(1)} %image.1.image_ref), channel_id=1, source_target_pairs={{0,1},{1,0},{2,3},{3,2},{4,5},{5,4},{6,7},{7,6},{8,9},{9,8},{10,11... | collective-permute-start | bytes 491528 | tf_op jit(solution)/shard_map/ppermute | solution.py:180
  63.8 10.0 %collective-permute-start.14 = (f32[128,128]{1,0:T(8,128)S(1)}, f32[128,128]{1,0:T(8,128)S(1)}, u32[]{:S(2)}, u32[]{:S(2)}) collective-permute-start(f32[128,128]{1,0:T(8,128)S(1)} %gram.1), channel_id=1, source_target_pairs={{0,6},{2,4},{4,2},{6,0},{8,14},{10,12},{12,10},{14,8},{1,7},{3,5},... | collective-permute-start | bytes 196616 | tf_op jit(solution)/shard_map/ppermute | solution.py:180
  63.9 14.1 %collective-permute-start.13 = (f32[128,128]{1,0:T(8,128)S(1)}, f32[128,128]{1,0:T(8,128)S(1)}, u32[]{:S(2)}, u32[]{:S(2)}) collective-permute-start(f32[128,128]{1,0:T(8,128)S(1)} %gram.1), channel_id=1, source_target_pairs={{0,4},{2,6},{4,0},{6,2},{8,12},{10,14},{12,8},{14,10},{1,5},{3,7},... | collective-permute-start | bytes 196616 | tf_op jit(solution)/shard_map/ppermute | solution.py:180
  73.7 4.3 %collective-permute-start.12 = (f32[128,128]{1,0:T(8,128)S(1)}, f32[128,128]{1,0:T(8,128)S(1)}, u32[]{:S(2)}, u32[]{:S(2)}) collective-permute-start(f32[128,128]{1,0:T(8,128)S(1)} %gram.1), channel_id=1, source_target_pairs={{0,2},{2,0},{4,6},{6,4},{8,10},{10,8},{12,14},{14,12},{1,3},{3,1},... | collective-permute-start | bytes 196616 | tf_op jit(solution)/shard_map/ppermute | solution.py:180
  78.0 6.3 %collective-permute-start.17 = (f32[128,128]{1,0:T(8,128)S(1)}, f32[128,128]{1,0:T(8,128)S(1)}, u32[]{:S(2)}, u32[]{:S(2)}) collective-permute-start(f32[128,128]{1,0:T(8,128)S(1)} %add_add_fusion.2), channel_id=1, source_target_pairs={{0,48},{16,32},{32,16},{48,0},{1,49},{17,33},{33,17},{49,1},{2,50}... | collective-permute-start | bytes 196616 | tf_op jit(solution)/shard_map/ppermute | solution.py:180
  78.1 6.2 %collective-permute-start.16 = (f32[128,128]{1,0:T(8,128)S(1)}, f32[128,128]{1,0:T(8,128)S(1)}, u32[]{:S(2)}, u32[]{:S(2)}) collective-permute-start(f32[128,128]{1,0:T(8,128)S(1)} %add_add_fusion.2), channel_id=1, source_target_pairs={{0,32},{16,48},{32,0},{48,16},{1,33},{17,49},{33,1},{49,17},{2,34}... | collective-permute-start | bytes 196616 | tf_op jit(solution)/shard_map/ppermute | solution.py:180
  78.2 6.9 %collective-permute-start.15 = (f32[128,128]{1,0:T(8,128)S(1)}, f32[128,128]{1,0:T(8,128)S(1)}, u32[]{:S(2)}, u32[]{:S(2)}) collective-permute-start(f32[128,128]{1,0:T(8,128)S(1)} %add_add_fusion.2), channel_id=1, source_target_pairs={{0,16},{16,0},{32,48},{48,32},{1,17},{17,1},{33,49},{49,33},{2,18}... | collective-permute-start | bytes 196616 | tf_op jit(solution)/shard_map/ppermute | solution.py:180
  85.2 6.3 %collective-permute-start.20 = (f32[128,128]{1,0:T(8,128)S(1)}, f32[128,128]{1,0:T(8,128)S(1)}, u32[]{:S(2)}, u32[]{:S(2)}) collective-permute-start(f32[128,128]{1,0:T(8,128)S(1)} %add_add_fusion.1), channel_id=1, source_target_pairs={{0,192},{64,128},{128,64},{192,0},{1,193},{65,129},{129,65},{193,1... | collective-permute-start | bytes 196616 | tf_op jit(solution)/shard_map/ppermute | solution.py:180
  85.3 6.2 %collective-permute-start.19 = (f32[128,128]{1,0:T(8,128)S(1)}, f32[128,128]{1,0:T(8,128)S(1)}, u32[]{:S(2)}, u32[]{:S(2)}) collective-permute-start(f32[128,128]{1,0:T(8,128)S(1)} %add_add_fusion.1), channel_id=1, source_target_pairs={{0,128},{64,192},{128,0},{192,64},{1,129},{65,193},{129,1},{193,65... | collective-permute-start | bytes 196616 | tf_op jit(solution)/shard_map/ppermute | solution.py:180
  85.4 6.9 %collective-permute-start.18 = (f32[128,128]{1,0:T(8,128)S(1)}, f32[128,128]{1,0:T(8,128)S(1)}, u32[]{:S(2)}, u32[]{:S(2)}) collective-permute-start(f32[128,128]{1,0:T(8,128)S(1)} %add_add_fusion.1), channel_id=1, source_target_pairs={{0,64},{64,0},{128,192},{192,128},{1,65},{65,1},{129,193},{193,129... | collective-permute-start | bytes 196616 | tf_op jit(solution)/shard_map/ppermute | solution.py:180
  92.3 10.1 %collective-permute-start.21 = (f32[128,128]{1,0:T(8,128)S(1)}, f32[128,128]{1,0:T(8,128)S(1)}, u32[]{:S(2)}, u32[]{:S(2)}) collective-permute-start(f32[128,128]{1,0:T(8,128)S(1)} %add_add_fusion), channel_id=1, source_target_pairs={{0,8},{2,10},{4,12},{6,14},{8,0},{10,2},{12,4},{14,6},{1,9},{3,11}... | collective-permute-start | bytes 196616 | tf_op jit(solution)/shard_map/ppermute | solution.py:180

commit v2 on v1

v2 whole, which is shorter than its diff:
```python
import jax
import jax.numpy as jnp
from jax import lax
from jax.experimental import pallas as pl
from jax.experimental.pallas import tpu as pltpu
from jax.sharding import Mesh, PartitionSpec as P

B = 128
DIST = 8
ROWS = ("x", "y", "z")
UNROLL = 4
NT = (((1,), (1,)), ((), ()))
MIB = 1024 * 1024


def dot_nt(a, b):
    return lax.dot_general(a, b, NT, preferred_element_type=jnp.float32)


def sorted_slots(neighbours, counts):
    block_rows, slot_count = neighbours.shape
    slots = lax.broadcasted_iota(jnp.int32, neighbours.shape, 1)
    square = (block_rows, block_rows)
    own = lax.broadcasted_iota(jnp.int32, square, 0) == lax.broadcasted_iota(jnp.int32, square, 1)
    counts = jnp.sum(jnp.where(own, counts, 0), axis=1, keepdims=True)
    column = neighbours - neighbours[:1, :1] + DIST
    dead = block_rows + 2 * DIST
    key = jnp.where(slots < counts, column, dead) * slot_count + slots
    rank = jnp.zeros_like(key)
    for t in range(slot_count):
        rank += (key[:, t : t + 1] < key).astype(jnp.int32)
    ordered = jnp.zeros_like(key)
    for s in range(slot_count):
        ordered = jnp.where(rank[:, s : s + 1] == slots, key[:, s : s + 1], ordered)
    return ordered, counts


def band_kernel(count_ref, near_ref, h_ref, a_ref, held, staged, key_ref, sems, key_sem):
    block_rows, slot_count = held.shape[:2]

    def part(r):
        return pltpu.make_async_copy(h_ref.at[r], held.at[r], sems.at[r])

    def start(r, _):
        part(r).start()
        return 0

    def clear(r, _):
        base = pl.multiple_of((r // 2) * (2 * B), 2 * B)
        rows = pl.ds(pl.multiple_of(r * B, B), B)
        a_ref[rows, pl.ds(base, 18 * B)] = jnp.zeros((B, 18 * B), a_ref.dtype)
        return 0

    lax.fori_loop(0, block_rows, start, 0)
    ordered, counts = sorted_slots(near_ref[...], count_ref[...])
    staged[:block_rows, :slot_count] = ordered
    staged[:block_rows, slot_count : slot_count + 1] = counts
    keys = pltpu.make_async_copy(staged, key_ref, key_sem)
    keys.start()
    lax.fori_loop(0, block_rows, clear, 0)
    keys.wait()

    def one_row(r, _):
        rows = pl.ds(pl.multiple_of(r * B, B), B)
        part(r).wait()

        def group(g, carry):
            total, last = carry
            for u in range(UNROLL):
                key = key_ref[r, g * UNROLL + u]
                column = key // slot_count
                block = held[r, key % slot_count].astype(jnp.float32)
                total = jnp.where(column == last, total, 0.0) + block
                last = column
                lanes = pl.ds(pl.multiple_of(column * B, B), B)
                a_ref[rows, lanes] = total.astype(a_ref.dtype)
            return total, last

        groups = (key_ref[r, slot_count] + UNROLL - 1) // UNROLL
        lax.fori_loop(0, groups, group, (jnp.zeros((B, B), jnp.float32), jnp.int32(-1)))
        return 0

    lax.fori_loop(0, block_rows, one_row, 0)


def build_band(neighbours, counts, hamiltonian):
    block_rows, slot_count = hamiltonian.shape[:2]
    width = (block_rows + 2 * DIST + 1) * B
    return pl.pallas_call(
        band_kernel,
        out_shape=pltpu.VMEM((block_rows * B, width), jnp.bfloat16),
        in_specs=[
            pl.BlockSpec(memory_space=pltpu.VMEM),
            pl.BlockSpec(memory_space=pltpu.VMEM),
            pl.BlockSpec(memory_space=pltpu.HBM),
        ],
        out_specs=pl.BlockSpec(memory_space=pltpu.VMEM),
        scratch_shapes=[
            pltpu.VMEM(hamiltonian.shape, hamiltonian.dtype),
            pltpu.VMEM((16, B), jnp.int32),
            pltpu.SMEM((16, B), jnp.int32),
            pltpu.SemaphoreType.DMA((block_rows,)),
            pltpu.SemaphoreType.DMA,
        ],
        compiler_params=pltpu.CompilerParams(vmem_limit_bytes=46 * MIB),
        name="band",
    )(counts.reshape(1, block_rows), neighbours, hamiltonian)


def own_kernel(v_ref, a_ref, acc_ref):
    rows = acc_ref.shape[1]
    v = v_ref[...]
    for i in range(0, rows, 2 * B):
        acc_ref[:, i : i + 2 * B] = dot_nt(v, a_ref[i : i + 2 * B, DIST * B : DIST * B + rows])


def apply_halo(acc_ref, low, high, a_ref):
    rows = acc_ref.shape[1]
    step = 2 * B
    upper = DIST * B + rows
    for i in range(0, rows, step):
        total = acc_ref[:, i : i + step]
        if i < DIST * B:
            total += dot_nt(low[:, i:], a_ref[i : i + step, i : DIST * B])
        depth = i + step - (rows - DIST * B)
        if depth > 0:
            total += dot_nt(high[:, :depth], a_ref[i : i + step, upper : upper + depth])
        yield i, step, total


def on_first_core():
    return lax.axis_index("band") == 0


def arrived(there_ref, back_ref):
    there, back = there_ref[...], back_ref[...]
    return jnp.where(on_first_core(), there, back), jnp.where(on_first_core(), back, there)


def depart(new_ref, there_ref, back_ref):
    reach = DIST * B
    top = new_ref[:, new_ref.shape[1] - reach :]
    bottom = new_ref[:, :reach]
    there_ref[...] = jnp.where(on_first_core(), top, bottom)
    back_ref[...] = jnp.where(on_first_core(), bottom, top)


def edges_kernel(new_ref, top_ref, bottom_ref):
    reach = DIST * B
    top_ref[...] = new_ref[:, new_ref.shape[1] - reach :]
    bottom_ref[...] = new_ref[:, :reach]


def first_kernel(acc_ref, low_ref, high_ref, a_ref, new_ref, there_ref, back_ref):
    for i, step, total in apply_halo(acc_ref, low_ref[...], high_ref[...], a_ref):
        new_ref[:, i : i + step] = total.astype(new_ref.dtype)
    depart(new_ref, there_ref, back_ref)


def next_kernel(acc_ref, from_ref, to_ref, a_ref, older_ref, new_ref, there_ref, back_ref):
    for i, step, total in apply_halo(acc_ref, *arrived(from_ref, to_ref), a_ref):
        older = older_ref[:, i : i + step].astype(jnp.float32)
        new_ref[:, i : i + step] = (2.0 * total - older).astype(new_ref.dtype)
    depart(new_ref, there_ref, back_ref)


def image_kernel(acc_ref, from_ref, to_ref, a_ref, new_ref):
    for i, step, total in apply_halo(acc_ref, *arrived(from_ref, to_ref), a_ref):
        new_ref[:, i : i + step] = total.astype(new_ref.dtype)


def in_vmem(kernel, name, outs, *args, flops=0):
    specs = [pl.BlockSpec(memory_space=pltpu.VMEM)]
    return pl.pallas_call(
        kernel,
        out_shape=[pltpu.VMEM(s, d) for s, d in outs],
        in_specs=specs * len(args),
        out_specs=specs * len(outs),
        compiler_params=pltpu.CompilerParams(vmem_limit_bytes=16 * MIB),
        cost_estimate=pl.CostEstimate(flops=flops, bytes_accessed=0, transcendentals=0),
        name=name,
    )(*args)


def gram_kernel(own_ref, other_ref, image_ref, other_image_ref, out_ref):
    own = own_ref[...]
    half = own.shape[0]
    is_first = on_first_core()

    def both(mine, others):
        a, b = dot_nt(own, mine), dot_nt(own, others)
        return jnp.concatenate([jnp.where(is_first, a, b), jnp.where(is_first, b, a)], axis=1)

    out_ref[:half, :] = both(own, other_ref[...])
    out_ref[half:, :] = both(image_ref[...], other_image_ref[...])


def exchange_ring(top, bottom):
    count = lax.axis_size(ROWS)
    up = [(i, (i + 1) % count) for i in range(count)]
    down = [(target, source) for source, target in up]
    return lax.ppermute(top, ROWS, up), lax.ppermute(bottom, ROWS, down)


def exchange_loop(there, back):
    count = lax.axis_size(ROWS)
    loop = [2 * i for i in range(count)] + [2 * i + 1 for i in reversed(range(count))]
    forth = list(zip(loop, loop[1:] + loop[:1]))
    every = (*ROWS, "band")
    return (
        lax.ppermute(there, every, forth),
        lax.ppermute(back, every, [(target, source) for source, target in forth]),
    )


def swapped(value, axis, distance):
    count = lax.axis_size(axis)
    return lax.ppermute(value, axis, [(i, i ^ distance) for i in range(count)])


def sum_over_rows(value):
    for axis, distances in (("z", (1, 2, 3)), ("z", (6,)), ("y", (1, 2, 3)), ("x", (1, 2, 3))):
        own = lax.reduce_precision(value, exponent_bits=8, mantissa_bits=7)
        sent = own.astype(jnp.bfloat16)
        others = [swapped(sent, axis, k).astype(jnp.float32) for k in distances]
        value = own + others[0]
        if len(others) == 3:
            value = value + (others[1] + others[2])
    return value


def body(hamiltonian, neighbours, counts, vectors):
    block_rows = hamiltonian.shape[0]
    rows, width = vectors.shape
    reach = DIST * B
    field = ((width, rows), jnp.bfloat16)
    halo = ((width, reach), jnp.bfloat16)
    part = ((width, rows), jnp.float32)
    own_flops = 2 * width * rows * rows

    def own_part(v, name):
        return in_vmem(own_kernel, name, [part], v, band, flops=own_flops)[0]

    start = vectors.T
    low, high = exchange_ring(*in_vmem(edges_kernel, "edges", [halo, halo], start))
    band = build_band(neighbours, counts, hamiltonian)
    acc = own_part(start, "own1")
    level1, there, back = in_vmem(first_kernel, "level1", [field, halo, halo], acc, low, high, band)
    older, newer = start, level1
    for degree in range(2, 5):
        there, back = exchange_loop(there, back)
        acc = own_part(newer, "own%d" % degree)
        latest, there, back = in_vmem(
            next_kernel, "level%d" % degree, [field, halo, halo], acc, there, back, band, older
        )
        older, newer = newer, latest
    there, back = exchange_loop(there, back)
    acc = own_part(newer, "own5")
    other = swapped(newer, "band", 1)
    (image,) = in_vmem(image_kernel, "image", [field], acc, there, back, band)
    other_image = swapped(image, "band", 1)
    both = ((2 * width, 2 * width), jnp.float32)
    sums = pl.pallas_call(
        gram_kernel,
        out_shape=jax.ShapeDtypeStruct((2 * width, 2 * width), jnp.float32),
        in_specs=[pl.BlockSpec(memory_space=pltpu.VMEM)] * 4,
        out_specs=pl.BlockSpec(memory_space=pltpu.VMEM),
        compiler_params=pltpu.CompilerParams(vmem_limit_bytes=16 * MIB),
        name="gram",
    )(newer, other, image, other_image)
    sums = sum_over_rows(sums) * (1.0 / (rows * lax.axis_size(ROWS)))
    return newer.T, sums[:width], sums[width:]


def solution(mesh):
    shape = tuple(mesh.shape[name] for name in mesh.axis_names)
    chips = Mesh(mesh.devices.reshape(4, 4, 8, shape[1]), (*ROWS, "band"))
    return jax.shard_map(
        body,
        mesh=chips,
        in_specs=(P(ROWS, None, None, None), P(ROWS, None), P(ROWS), P(ROWS, "band")),
        out_specs=(P(ROWS, "band"), P("band", None), P("band", None)),
        check_vma=False,
    )
```

time: 103 us -> 92.2 us (0.90); the launches traced: 103 us -> 90.6 us
  starting transfers between devices: 58.6 us -> 47.3 us
  other arithmetic: 1.93 us -> 0.11 us
  waiting for transfers between devices: 22.2 us -> 24 us
  Pallas kernels: 17.2 us -> 16.1 us
    ppermute x10, starting transfers between devices: 32.4 us -> 17.4 us  [the longest x4 11.2 us: exchange_loop(): lax.ppermute(back, every, [(target, source) for source, target in forth])]
    ppermute x12, starting transfers between devices: 26.2 us -> 29.9 us  [swapped(): return lax.ppermute(value, axis, [(i, i ^ distance) for i in range(count)])]
    ppermute x10, waiting for transfers between devices: 9.08 us -> 11 us  [the longest x4 10 us: exchange_loop(): lax.ppermute(there, every, forth)]
    reduce_sum x2 -> x0, other arithmetic: 1.1 us -> none  [the longest x1 0.77 us: slot_order(): return jnp.sum(jnp.where(picked, key[:, :, None], 0), axis=1)]
    slice x1 -> x0, local copies, waits for them, and re-layouts: 1.06 us -> none  [body(): low, high = exchange_halos(start[:, rows - reach:], start[:, :reach])]
    pallas_call x1, Pallas kernels: 6.64 us -> 5.6 us  [build_band(): pl.pallas_call(band_kernel, out_shape=pltpu.VMEM((block_rows * B, width),...]
    pallas_call x10 -> x11, Pallas kernels: 10.1 us -> 10.2 us  [in_vmem(): pl.pallas_call(kernel, out_shape=[pltpu.VMEM(s, d) for s, d in outs], in_...]
  transfers between devices with their start and end apart: 22 -> 22, of which waited for: 12 -> 15; matrix products, arithmetic and copies ran while one was open for 2% -> 1% of each run, Pallas kernels for 13% -> 13%
where the time goes in v2:
time: 92.2 us; the launch traced here: 90.6 us
  starting transfers between devices  47.3 us (51%)
  waiting for transfers between devices  24 us (26%)
  Pallas kernels  16.1 us (17%)
  local copies, waits for them, and re-layouts  2.21 us (2%)
    ppermute x12, starting transfers between devices, swapped(): return lax.ppermute(value, axis, [(i, i ^ distance) for i in range(count)])  29.9 us
    ppermute x12, waiting for transfers between devices, swapped(): return lax.ppermute(value, axis, [(i, i ^ distance) for i in range(count)])  13.1 us
    ppermute x4, starting transfers between devices, exchange_loop(): lax.ppermute(back, every, [(target, source) for source, target in forth])  11.2 us
    pallas_call x11, Pallas kernels, in_vmem(): pl.pallas_call(kernel, out_shape=[pltpu.VMEM(s, d) for s, d in outs], in_...  10.2 us
    ppermute x4, waiting for transfers between devices, exchange_loop(): lax.ppermute(there, every, forth)  10 us
    pallas_call x1, Pallas kernels, build_band(): pl.pallas_call(band_kernel, out_shape=pltpu.VMEM((block_rows * B, width),...  5.6 us
    ppermute x4, starting transfers between devices, exchange_loop(): lax.ppermute(there, every, forth)  4.12 us
    ppermute x2, starting transfers between devices, exchange_ring(): return (lax.ppermute(top, ROWS, up), lax.ppermute(bottom, ROWS, down))  2.1 us
  transfers between devices with their start and end apart: 22, of which 15 were waited for; matrix products, arithmetic and copies ran while one was open for 1% of the time, Pallas kernels for 13%

profile of v2, /device:TPU:32, one launch (start us, length us, event | category | flops | bytes accessed | tf_op | source)
XLA Modules:
  0.0 90.6 jit_solution(1487317170292586729)
XLA Ops:
  0.6 0.9 %copy-done = bf16[1280,64]{0,1:T(8,128)(2,1)S(1)} copy-done((bf16[1280,64]{0,1:T(8,128)(2,1)S(1)}, bf16[1280,64]{0,1:T(8,128)(2,1)}, u32[]{:S(2)}) %copy-start) | copy-done | bytes 163864
  1.6 2.0 %collective-permute-start = (bf16[64,1024]{1,0:T(8,128)(2,1)S(1)}, bf16[64,1024]{1,0:T(8,128)(2,1)S(1)}, u32[]{:S(2)}, u32[]{:S(2)}) collective-permute-start(bf16[64,1024]{1,0:T(8,128)(2,1)S(1)} %get-tuple-element.17), channel_id=1, source_target_pairs={{0,2},{2,4},{4,6},{6,8},{8,10},{10,12},{12,14},{14,16},{16,18},{18... | collective-permute-start | bytes 393224 | tf_op jit(solution)/shard_map/ppermute | solution.py:202
  3.6 0.1 collective-permute-start.1
  3.7 5.6 %band.1.a_ref = bf16[1280,3456]{1,0:T(8,128)(2,1)S(1)} custom-call(s32[1,10]{1,0:T(1,128)} %bitcast.7, s32[10,32]{1,0:T(8,128)} %near_ref.1, bf16[10,32,128,128]{3,2,1,0:T(8,128)(2,1)} %h_ref.1), custom_call_target="tpu_custom_call" | custom-call | tf_op jit(solution)/shard_map/band/pallas_call | solution.py:89
  9.3 1.1 %own1.1.acc_ref = f32[64,1280]{1,0:T(8,128)S(1)} custom-call(bf16[64,1280]{1,0:T(8,128)(2,1)S(1)} %bitcast.5, bf16[1280,3456]{1,0:T(8,128)(2,1)S(1)} %band.1.a_ref), custom_call_target="tpu_custom_call" | custom-call | flops 209715200 | tf_op jit(solution)/shard_map/own1/pallas_call | solution.py:174
  10.4 0.9 %level1.1 = (bf16[64,1280]{1,0:T(8,128)(2,1)S(1)}, bf16[64,1024]{1,0:T(8,128)(2,1)S(1)}, bf16[64,1024]{1,0:T(8,128)(2,1)S(1)}) custom-call(f32[64,1280]{1,0:T(8,128)S(1)} %own1.1.acc_ref, bf16[64,1024]{1,0:T(8,128)(2,1)S(1)} %collective-permute-done.low_ref, bf16[64,1024]{1,0:T(8,128)(2,1)S(1)} %collective-permute-done.1.high_ref, ...), custom_call_target="tpu_custom_call" | custom-call | tf_op jit(solution)/shard_map/level1/pallas_call | solution.py:174
  11.4 1.9 %collective-permute-start.2 = (bf16[64,1024]{1,0:T(8,128)(2,1)S(1)}, bf16[64,1024]{1,0:T(8,128)(2,1)S(1)}, u32[]{:S(2)}, u32[]{:S(2)}) collective-permute-start(bf16[64,1024]{1,0:T(8,128)(2,1)S(1)} %get-tuple-element.20), channel_id=1, source_target_pairs={{0,2},{2,4},{4,6},{6,8},{8,10},{10,12},{12,14},{14,16},{16,18},{18... | collective-permute-start | bytes 393224 | tf_op jit(solution)/shard_map/ppermute | solution.py:211
  13.2 7.1 %collective-permute-start.3 = (bf16[64,1024]{1,0:T(8,128)(2,1)S(1)}, bf16[64,1024]{1,0:T(8,128)(2,1)S(1)}, u32[]{:S(2)}, u32[]{:S(2)}) collective-permute-start(bf16[64,1024]{1,0:T(8,128)(2,1)S(1)} %get-tuple-element.21), channel_id=1, source_target_pairs={{2,0},{4,2},{6,4},{8,6},{10,8},{12,10},{14,12},{16,14},{18,16},{20... | collective-permute-start | bytes 393224 | tf_op jit(solution)/shard_map/ppermute | solution.py:212
  20.4 1.1 %own2.1.acc_ref = f32[64,1280]{1,0:T(8,128)S(1)} custom-call(bf16[64,1280]{1,0:T(8,128)(2,1)S(1)} %get-tuple-element.19.v_ref.older_ref, bf16[1280,3456]{1,0:T(8,128)(2,1)S(1)} %band.1.a_ref), custom_call_target="tpu_custom_call" | custom-call | flops 209715200 | tf_op jit(solution)/shard_map/own2/pallas_call | solution.py:174
  21.5 2.8 %collective-permute-done.2.from_ref = bf16[64,1024]{1,0:T(8,128)(2,1)S(1)} collective-permute-done((bf16[64,1024]{1,0:T(8,128)(2,1)S(1)}, bf16[64,1024]{1,0:T(8,128)(2,1)S(1)}, u32[]{:S(2)}, u32[]{:S(2)}) %collective-permute-start.2) | collective-permute-done | bytes 131104 | tf_op jit(solution)/shard_map/ppermute | solution.py:211
  24.3 0.9 %level2.1 = (bf16[64,1280]{1,0:T(8,128)(2,1)S(1)}, bf16[64,1024]{1,0:T(8,128)(2,1)S(1)}, bf16[64,1024]{1,0:T(8,128)(2,1)S(1)}) custom-call(f32[64,1280]{1,0:T(8,128)S(1)} %own2.1.acc_ref, bf16[64,1024]{1,0:T(8,128)(2,1)S(1)} %collective-permute-done.2.from_ref, bf16[64,1024]{1,0:T(8,128)(2,1)S(1)} %collective-permute-done.3.to_ref, ...), custom_call_target="tpu_custom_call" | custom-call | tf_op jit(solution)/shard_map/level2/pallas_call | solution.py:174
  25.3 2.0 %collective-permute-start.5 = (bf16[64,1024]{1,0:T(8,128)(2,1)S(1)}, bf16[64,1024]{1,0:T(8,128)(2,1)S(1)}, u32[]{:S(2)}, u32[]{:S(2)}) collective-permute-start(bf16[64,1024]{1,0:T(8,128)(2,1)S(1)} %get-tuple-element.24), channel_id=1, source_target_pairs={{2,0},{4,2},{6,4},{8,6},{10,8},{12,10},{14,12},{16,14},{18,16},{20... | collective-permute-start | bytes 393224 | tf_op jit(solution)/shard_map/ppermute | solution.py:212
  27.3 1.1 %own3.1.acc_ref = f32[64,1280]{1,0:T(8,128)S(1)} custom-call(bf16[64,1280]{1,0:T(8,128)(2,1)S(1)} %get-tuple-element.22.v_ref.older_ref, bf16[1280,3456]{1,0:T(8,128)(2,1)S(1)} %band.1.a_ref), custom_call_target="tpu_custom_call" | custom-call | flops 209715200 | tf_op jit(solution)/shard_map/own3/pallas_call | solution.py:174
  28.4 2.5 %collective-permute-done.4.from_ref = bf16[64,1024]{1,0:T(8,128)(2,1)S(1)} collective-permute-done((bf16[64,1024]{1,0:T(8,128)(2,1)S(1)}, bf16[64,1024]{1,0:T(8,128)(2,1)S(1)}, u32[]{:S(2)}, u32[]{:S(2)}) %collective-permute-start.4) | collective-permute-done | bytes 131104 | tf_op jit(solution)/shard_map/ppermute | solution.py:211
  30.9 0.9 %level3.1 = (bf16[64,1280]{1,0:T(8,128)(2,1)S(1)}, bf16[64,1024]{1,0:T(8,128)(2,1)S(1)}, bf16[64,1024]{1,0:T(8,128)(2,1)S(1)}) custom-call(f32[64,1280]{1,0:T(8,128)S(1)} %own3.1.acc_ref, bf16[64,1024]{1,0:T(8,128)(2,1)S(1)} %collective-permute-done.4.from_ref, bf16[64,1024]{1,0:T(8,128)(2,1)S(1)} %collective-permute-done.5.to_ref, ...), custom_call_target="tpu_custom_call" | custom-call | tf_op jit(solution)/shard_map/level3/pallas_call | solution.py:174
  31.9 0.8 collective-permute-start.6
  32.6 1.3 %collective-permute-start.7 = (bf16[64,1024]{1,0:T(8,128)(2,1)S(1)}, bf16[64,1024]{1,0:T(8,128)(2,1)S(1)}, u32[]{:S(2)}, u32[]{:S(2)}) collective-permute-start(bf16[64,1024]{1,0:T(8,128)(2,1)S(1)} %get-tuple-element.27), channel_id=1, source_target_pairs={{2,0},{4,2},{6,4},{8,6},{10,8},{12,10},{14,12},{16,14},{18,16},{20... | collective-permute-start | bytes 393224 | tf_op jit(solution)/shard_map/ppermute | solution.py:212
  34.0 1.1 %own4.1.acc_ref = f32[64,1280]{1,0:T(8,128)S(1)} custom-call(bf16[64,1280]{1,0:T(8,128)(2,1)S(1)} %get-tuple-element.25.v_ref, bf16[1280,3456]{1,0:T(8,128)(2,1)S(1)} %band.1.a_ref), custom_call_target="tpu_custom_call" | custom-call | flops 209715200 | tf_op jit(solution)/shard_map/own4/pallas_call | solution.py:174
  35.1 2.4 %collective-permute-done.6.from_ref = bf16[64,1024]{1,0:T(8,128)(2,1)S(1)} collective-permute-done((bf16[64,1024]{1,0:T(8,128)(2,1)S(1)}, bf16[64,1024]{1,0:T(8,128)(2,1)S(1)}, u32[]{:S(2)}, u32[]{:S(2)}) %collective-permute-start.6) | collective-permute-done | bytes 131104 | tf_op jit(solution)/shard_map/ppermute | solution.py:211
  37.5 0.1 collective-permute-done.7.to_ref
  37.6 0.9 %level4.1 = (bf16[64,1280]{1,0:T(8,128)(2,1)S(1)}, bf16[64,1024]{1,0:T(8,128)(2,1)S(1)}, bf16[64,1024]{1,0:T(8,128)(2,1)S(1)}) custom-call(f32[64,1280]{1,0:T(8,128)S(1)} %own4.1.acc_ref, bf16[64,1024]{1,0:T(8,128)(2,1)S(1)} %collective-permute-done.6.from_ref, bf16[64,1024]{1,0:T(8,128)(2,1)S(1)} %collective-permute-done.7.to_ref, ...), custom_call_target="tpu_custom_call" | custom-call | tf_op jit(solution)/shard_map/level4/pallas_call | solution.py:174
  38.5 1.4 %collective-permute-start.9 = (bf16[64,1024]{1,0:T(8,128)(2,1)S(1)}, bf16[64,1024]{1,0:T(8,128)(2,1)S(1)}, u32[]{:S(2)}, u32[]{:S(2)}) collective-permute-start(bf16[64,1024]{1,0:T(8,128)(2,1)S(1)} %get-tuple-element.29), channel_id=1, source_target_pairs={{0,2},{2,4},{4,6},{6,8},{8,10},{10,12},{12,14},{14,16},{16,18},{18... | collective-permute-start | bytes 393224 | tf_op jit(solution)/shard_map/ppermute | solution.py:211
  39.9 0.7 collective-permute-start.10
  40.6 1.1 %own5.1.acc_ref = f32[64,1280]{1,0:T(8,128)S(1)} custom-call(bf16[64,1280]{1,0:T(8,128)(2,1)S(1)} %get-tuple-element.28.v_ref.own_ref, bf16[1280,3456]{1,0:T(8,128)(2,1)S(1)} %band.1.a_ref), custom_call_target="tpu_custom_call" | custom-call | flops 209715200 | tf_op jit(solution)/shard_map/own5/pallas_call | solution.py:174
  41.8 2.3 %collective-permute-done.9.from_ref = bf16[64,1024]{1,0:T(8,128)(2,1)S(1)} collective-permute-done((bf16[64,1024]{1,0:T(8,128)(2,1)S(1)}, bf16[64,1024]{1,0:T(8,128)(2,1)S(1)}, u32[]{:S(2)}, u32[]{:S(2)}) %collective-permute-start.9) | collective-permute-done | bytes 131104 | tf_op jit(solution)/shard_map/ppermute | solution.py:211
  44.1 0.8 collective-permute-done.10.to_ref
  44.9 0.9 image.1.image_ref
  45.9 1.4 %collective-permute-done.11.other_image_ref = bf16[64,1280]{1,0:T(8,128)(2,1)S(1)} collective-permute-done((bf16[64,1280]{1,0:T(8,128)(2,1)S(1)}, bf16[64,1280]{1,0:T(8,128)(2,1)S(1)}, u32[]{:S(2)}, u32[]{:S(2)}) %collective-permute-start.11) | collective-permute-done | bytes 163872 | tf_op jit(solution)/shard_map/ppermute | solution.py:218
  47.3 0.4 gram.1
  47.7 1.7 %collective-permute-start.14 = (bf16[128,128]{1,0:T(8,128)(2,1)S(1)}, bf16[128,128]{1,0:T(8,128)(2,1)S(1)}, u32[]{:S(2)}, u32[]{:S(2)}) collective-permute-start(bf16[128,128]{1,0:T(8,128)(2,1)S(1)} %reduce-precision_convert_fusion), channel_id=1, source_target_pairs={{0,6},{2,4},{4,2},{6,0},{8,14},{10,12},{12,10},{14,8},{1,7},{3,5},... | collective-permute-start | bytes 98312 | tf_op jit(solution)/shard_map/ppermute | solution.py:218
  49.3 1.5 %collective-permute-start.13 = (bf16[128,128]{1,0:T(8,128)(2,1)S(1)}, bf16[128,128]{1,0:T(8,128)(2,1)S(1)}, u32[]{:S(2)}, u32[]{:S(2)}) collective-permute-start(bf16[128,128]{1,0:T(8,128)(2,1)S(1)} %reduce-precision_convert_fusion), channel_id=1, source_target_pairs={{0,4},{2,6},{4,0},{6,2},{8,12},{10,14},{12,8},{14,10},{1,5},{3,7},... | collective-permute-start | bytes 98312 | tf_op jit(solution)/shard_map/ppermute | solution.py:218
  50.8 1.2 %collective-permute-start.12 = (bf16[128,128]{1,0:T(8,128)(2,1)S(1)}, bf16[128,128]{1,0:T(8,128)(2,1)S(1)}, u32[]{:S(2)}, u32[]{:S(2)}) collective-permute-start(bf16[128,128]{1,0:T(8,128)(2,1)S(1)} %reduce-precision_convert_fusion), channel_id=1, source_target_pairs={{0,2},{2,0},{4,6},{6,4},{8,10},{10,8},{12,14},{14,12},{1,3},{3,1},... | collective-permute-start | bytes 98312 | tf_op jit(solution)/shard_map/ppermute | solution.py:218
  52.1 2.1 %collective-permute-done.13 = bf16[128,128]{1,0:T(8,128)(2,1)S(1)} collective-permute-done((bf16[128,128]{1,0:T(8,128)(2,1)S(1)}, bf16[128,128]{1,0:T(8,128)(2,1)S(1)}, u32[]{:S(2)}, u32[]{:S(2)}) %collective-permute-start.13) | collective-permute-done | bytes 32800 | tf_op jit(solution)/shard_map/ppermute | solution.py:218
  54.2 0.7 collective-permute-done.12
  54.9 7.1 %collective-permute-start.15 = (bf16[128,128]{1,0:T(8,128)(2,1)S(1)}, bf16[128,128]{1,0:T(8,128)(2,1)S(1)}, u32[]{:S(2)}, u32[]{:S(2)}) collective-permute-start(bf16[128,128]{1,0:T(8,128)(2,1)S(1)} %get-tuple-element.31), channel_id=1, source_target_pairs={{0,12},{2,14},{4,8},{6,10},{8,4},{10,6},{12,0},{14,2},{1,13},{3,15... | collective-permute-start | bytes 98312 | tf_op jit(solution)/shard_map/ppermute | solution.py:218
  62.0 1.9 %collective-permute-done.15 = bf16[128,128]{1,0:T(8,128)(2,1)S(1)} collective-permute-done((bf16[128,128]{1,0:T(8,128)(2,1)S(1)}, bf16[128,128]{1,0:T(8,128)(2,1)S(1)}, u32[]{:S(2)}, u32[]{:S(2)}) %collective-permute-start.15) | collective-permute-done | bytes 32800 | tf_op jit(solution)/shard_map/ppermute | solution.py:218
  63.9 13.2 %collective-permute-start.18 = (bf16[128,128]{1,0:T(8,128)(2,1)S(1)}, bf16[128,128]{1,0:T(8,128)(2,1)S(1)}, u32[]{:S(2)}, u32[]{:S(2)}) collective-permute-start(bf16[128,128]{1,0:T(8,128)(2,1)S(1)} %fusion), channel_id=1, source_target_pairs={{0,48},{16,32},{32,16},{48,0},{1,49},{17,33},{33,17},{49,1},{2,50}... | collective-permute-start | bytes 98312 | tf_op jit(solution)/shard_map/ppermute | solution.py:218
  77.1 1.0 %collective-permute-start.16 = (bf16[128,128]{1,0:T(8,128)(2,1)S(1)}, bf16[128,128]{1,0:T(8,128)(2,1)S(1)}, u32[]{:S(2)}, u32[]{:S(2)}) collective-permute-start(bf16[128,128]{1,0:T(8,128)(2,1)S(1)} %fusion), channel_id=1, source_target_pairs={{0,16},{16,0},{32,48},{48,32},{1,17},{17,1},{33,49},{49,33},{2,18}... | collective-permute-start | bytes 98312 | tf_op jit(solution)/shard_map/ppermute | solution.py:218
  78.1 0.9 %collective-permute-done.18 = bf16[128,128]{1,0:T(8,128)(2,1)S(1)} collective-permute-done((bf16[128,128]{1,0:T(8,128)(2,1)S(1)}, bf16[128,128]{1,0:T(8,128)(2,1)S(1)}, u32[]{:S(2)}, u32[]{:S(2)}) %collective-permute-start.18) | collective-permute-done | bytes 32800 | tf_op jit(solution)/shard_map/ppermute | solution.py:218
  79.0 3.5 %collective-permute-done.17 = bf16[128,128]{1,0:T(8,128)(2,1)S(1)} collective-permute-done((bf16[128,128]{1,0:T(8,128)(2,1)S(1)}, bf16[128,128]{1,0:T(8,128)(2,1)S(1)}, u32[]{:S(2)}, u32[]{:S(2)}) %collective-permute-start.17) | collective-permute-done | bytes 32800 | tf_op jit(solution)/shard_map/ppermute | solution.py:218
  82.6 1.7 %collective-permute-start.21 = (bf16[128,128]{1,0:T(8,128)(2,1)S(1)}, bf16[128,128]{1,0:T(8,128)(2,1)S(1)}, u32[]{:S(2)}, u32[]{:S(2)}) collective-permute-start(bf16[128,128]{1,0:T(8,128)(2,1)S(1)} %fusion.1), channel_id=1, source_target_pairs={{0,192},{64,128},{128,64},{192,0},{1,193},{65,129},{129,65},{193,1... | collective-permute-start | bytes 98312 | tf_op jit(solution)/shard_map/ppermute | solution.py:218
  84.3 1.7 %collective-permute-start.20 = (bf16[128,128]{1,0:T(8,128)(2,1)S(1)}, bf16[128,128]{1,0:T(8,128)(2,1)S(1)}, u32[]{:S(2)}, u32[]{:S(2)}) collective-permute-start(bf16[128,128]{1,0:T(8,128)(2,1)S(1)} %fusion.1), channel_id=1, source_target_pairs={{0,128},{64,192},{128,0},{192,64},{1,129},{65,193},{129,1},{193,65... | collective-permute-start | bytes 98312 | tf_op jit(solution)/shard_map/ppermute | solution.py:218
  86.0 0.7 collective-permute-start.19
  86.7 0.7 copy.7
  87.4 0.4 collective-permute-done.21
  87.8 1.9 %collective-permute-done.20 = bf16[128,128]{1,0:T(8,128)(2,1)S(1)} collective-permute-done((bf16[128,128]{1,0:T(8,128)(2,1)S(1)}, bf16[128,128]{1,0:T(8,128)(2,1)S(1)}, u32[]{:S(2)}, u32[]{:S(2)}) %collective-permute-start.20) | collective-permute-done | bytes 32800 | tf_op jit(solution)/shard_map/ppermute | solution.py:218
  89.7 0.2 collective-permute-done.19
  90.0 0.6 fusion.3
  (20 shorter events, 0.3 us)
Async XLA Ops:
  0.6 0.9 %copy-start = (bf16[1280,64]{0,1:T(8,128)(2,1)S(1)}, bf16[1280,64]{0,1:T(8,128)(2,1)}, u32[]{:S(2)}) copy-start(bf16[1280,64]{0,1:T(8,128)(2,1)} %param.7) | copy-start | bytes 491524
  1.5 7.7 %copy-start.1 = (bf16[1280,64]{0,1:T(8,128)(2,1)S(1)}, bf16[1280,64]{0,1:T(8,128)(2,1)}, u32[]{:S(2)}) copy-start(bf16[1280,64]{0,1:T(8,128)(2,1)} %param.7) | copy-start | bytes 491524
  1.6 8.8 %collective-permute-start = (bf16[64,1024]{1,0:T(8,128)(2,1)S(1)}, bf16[64,1024]{1,0:T(8,128)(2,1)S(1)}, u32[]{:S(2)}, u32[]{:S(2)}) collective-permute-start(bf16[64,1024]{1,0:T(8,128)(2,1)S(1)} %get-tuple-element.17), channel_id=1, source_target_pairs={{0,2},{2,4},{4,6},{6,8},{8,10},{10,12},{12,14},{14,16},{16,18},{18... | collective-permute-start | bytes 393224 | tf_op jit(solution)/shard_map/ppermute | solution.py:202
  3.6 6.9 %collective-permute-start.1 = (bf16[64,1024]{1,0:T(8,128)(2,1)S(1)}, bf16[64,1024]{1,0:T(8,128)(2,1)S(1)}, u32[]{:S(2)}, u32[]{:S(2)}) collective-permute-start(bf16[64,1024]{1,0:T(8,128)(2,1)S(1)} %get-tuple-element.18), channel_id=1, source_target_pairs={{2,0},{4,2},{6,4},{8,6},{10,8},{12,10},{14,12},{16,14},{18,16},{20... | collective-permute-start | bytes 393224 | tf_op jit(solution)/shard_map/ppermute | solution.py:202
  11.4 12.9 %collective-permute-start.2 = (bf16[64,1024]{1,0:T(8,128)(2,1)S(1)}, bf16[64,1024]{1,0:T(8,128)(2,1)S(1)}, u32[]{:S(2)}, u32[]{:S(2)}) collective-permute-start(bf16[64,1024]{1,0:T(8,128)(2,1)S(1)} %get-tuple-element.20), channel_id=1, source_target_pairs={{0,2},{2,4},{4,6},{6,8},{8,10},{10,12},{12,14},{14,16},{16,18},{18... | collective-permute-start | bytes 393224 | tf_op jit(solution)/shard_map/ppermute | solution.py:211
  13.2 11.1 %collective-permute-start.3 = (bf16[64,1024]{1,0:T(8,128)(2,1)S(1)}, bf16[64,1024]{1,0:T(8,128)(2,1)S(1)}, u32[]{:S(2)}, u32[]{:S(2)}) collective-permute-start(bf16[64,1024]{1,0:T(8,128)(2,1)S(1)} %get-tuple-element.21), channel_id=1, source_target_pairs={{2,0},{4,2},{6,4},{8,6},{10,8},{12,10},{14,12},{16,14},{18,16},{20... | collective-permute-start | bytes 393224 | tf_op jit(solution)/shard_map/ppermute | solution.py:212
  25.2 5.7 %collective-permute-start.4 = (bf16[64,1024]{1,0:T(8,128)(2,1)S(1)}, bf16[64,1024]{1,0:T(8,128)(2,1)S(1)}, u32[]{:S(2)}, u32[]{:S(2)}) collective-permute-start(bf16[64,1024]{1,0:T(8,128)(2,1)S(1)} %get-tuple-element.23), channel_id=1, source_target_pairs={{0,2},{2,4},{4,6},{6,8},{8,10},{10,12},{12,14},{14,16},{16,18},{18... | collective-permute-start | bytes 393224 | tf_op jit(solution)/shard_map/ppermute | solution.py:211
  25.3 5.6 %collective-permute-start.5 = (bf16[64,1024]{1,0:T(8,128)(2,1)S(1)}, bf16[64,1024]{1,0:T(8,128)(2,1)S(1)}, u32[]{:S(2)}, u32[]{:S(2)}) collective-permute-start(bf16[64,1024]{1,0:T(8,128)(2,1)S(1)} %get-tuple-element.24), channel_id=1, source_target_pairs={{2,0},{4,2},{6,4},{8,6},{10,8},{12,10},{14,12},{16,14},{18,16},{20... | collective-permute-start | bytes 393224 | tf_op jit(solution)/shard_map/ppermute | solution.py:212
  31.9 5.6 %collective-permute-start.6 = (bf16[64,1024]{1,0:T(8,128)(2,1)S(1)}, bf16[64,1024]{1,0:T(8,128)(2,1)S(1)}, u32[]{:S(2)}, u32[]{:S(2)}) collective-permute-start(bf16[64,1024]{1,0:T(8,128)(2,1)S(1)} %get-tuple-element.26), channel_id=1, source_target_pairs={{0,2},{2,4},{4,6},{6,8},{8,10},{10,12},{12,14},{14,16},{16,18},{18... | collective-permute-start | bytes 393224 | tf_op jit(solution)/shard_map/ppermute | solution.py:211
  32.6 5.0 %collective-permute-start.7 = (bf16[64,1024]{1,0:T(8,128)(2,1)S(1)}, bf16[64,1024]{1,0:T(8,128)(2,1)S(1)}, u32[]{:S(2)}, u32[]{:S(2)}) collective-permute-start(bf16[64,1024]{1,0:T(8,128)(2,1)S(1)} %get-tuple-element.27), channel_id=1, source_target_pairs={{2,0},{4,2},{6,4},{8,6},{10,8},{12,10},{14,12},{16,14},{18,16},{20... | collective-permute-start | bytes 393224 | tf_op jit(solution)/shard_map/ppermute | solution.py:212
  38.5 5.6 %collective-permute-start.9 = (bf16[64,1024]{1,0:T(8,128)(2,1)S(1)}, bf16[64,1024]{1,0:T(8,128)(2,1)S(1)}, u32[]{:S(2)}, u32[]{:S(2)}) collective-permute-start(bf16[64,1024]{1,0:T(8,128)(2,1)S(1)} %get-tuple-element.29), channel_id=1, source_target_pairs={{0,2},{2,4},{4,6},{6,8},{8,10},{10,12},{12,14},{14,16},{16,18},{18... | collective-permute-start | bytes 393224 | tf_op jit(solution)/shard_map/ppermute | solution.py:211
  39.9 5.0 %collective-permute-start.10 = (bf16[64,1024]{1,0:T(8,128)(2,1)S(1)}, bf16[64,1024]{1,0:T(8,128)(2,1)S(1)}, u32[]{:S(2)}, u32[]{:S(2)}) collective-permute-start(bf16[64,1024]{1,0:T(8,128)(2,1)S(1)} %get-tuple-element.30), channel_id=1, source_target_pairs={{2,0},{4,2},{6,4},{8,6},{10,8},{12,10},{14,12},{16,14},{18,16},{20... | collective-permute-start | bytes 393224 | tf_op jit(solution)/shard_map/ppermute | solution.py:212
  40.6 5.3 %collective-permute-start.8 = (bf16[64,1280]{1,0:T(8,128)(2,1)S(1)}, bf16[64,1280]{1,0:T(8,128)(2,1)S(1)}, u32[]{:S(2)}, u32[]{:S(2)}) collective-permute-start(bf16[64,1280]{1,0:T(8,128)(2,1)S(1)} %get-tuple-element.28.v_ref.own_ref), channel_id=1, source_target_pairs={{0,1},{1,0},{2,3},{3,2},{4,5},{5,4},{6,7},{7,6},{8,9},{9,8},{10,11... | collective-permute-start | bytes 491528 | tf_op jit(solution)/shard_map/ppermute | solution.py:218
  45.8 1.5 %collective-permute-start.11 = (bf16[64,1280]{1,0:T(8,128)(2,1)S(1)}, bf16[64,1280]{1,0:T(8,128)(2,1)S(1)}, u32[]{:S(2)}, u32[]{:S(2)}) collective-permute-start(bf16[64,1280]{1,0:T(8,128)(2,1)S(1)} %image.1.image_ref), channel_id=1, source_target_pairs={{0,1},{1,0},{2,3},{3,2},{4,5},{5,4},{6,7},{7,6},{8,9},{9,8},{10,11... | collective-permute-start | bytes 491528 | tf_op jit(solution)/shard_map/ppermute | solution.py:218
  47.7 4.4 %collective-permute-start.14 = (bf16[128,128]{1,0:T(8,128)(2,1)S(1)}, bf16[128,128]{1,0:T(8,128)(2,1)S(1)}, u32[]{:S(2)}, u32[]{:S(2)}) collective-permute-start(bf16[128,128]{1,0:T(8,128)(2,1)S(1)} %reduce-precision_convert_fusion), channel_id=1, source_target_pairs={{0,6},{2,4},{4,2},{6,0},{8,14},{10,12},{12,10},{14,8},{1,7},{3,5},... | collective-permute-start | bytes 98312 | tf_op jit(solution)/shard_map/ppermute | solution.py:218
  49.3 4.8 %collective-permute-start.13 = (bf16[128,128]{1,0:T(8,128)(2,1)S(1)}, bf16[128,128]{1,0:T(8,128)(2,1)S(1)}, u32[]{:S(2)}, u32[]{:S(2)}) collective-permute-start(bf16[128,128]{1,0:T(8,128)(2,1)S(1)} %reduce-precision_convert_fusion), channel_id=1, source_target_pairs={{0,4},{2,6},{4,0},{6,2},{8,12},{10,14},{12,8},{14,10},{1,5},{3,7},... | collective-permute-start | bytes 98312 | tf_op jit(solution)/shard_map/ppermute | solution.py:218
  50.8 4.1 %collective-permute-start.12 = (bf16[128,128]{1,0:T(8,128)(2,1)S(1)}, bf16[128,128]{1,0:T(8,128)(2,1)S(1)}, u32[]{:S(2)}, u32[]{:S(2)}) collective-permute-start(bf16[128,128]{1,0:T(8,128)(2,1)S(1)} %reduce-precision_convert_fusion), channel_id=1, source_target_pairs={{0,2},{2,0},{4,6},{6,4},{8,10},{10,8},{12,14},{14,12},{1,3},{3,1},... | collective-permute-start | bytes 98312 | tf_op jit(solution)/shard_map/ppermute | solution.py:218
  54.9 9.0 %collective-permute-start.15 = (bf16[128,128]{1,0:T(8,128)(2,1)S(1)}, bf16[128,128]{1,0:T(8,128)(2,1)S(1)}, u32[]{:S(2)}, u32[]{:S(2)}) collective-permute-start(bf16[128,128]{1,0:T(8,128)(2,1)S(1)} %get-tuple-element.31), channel_id=1, source_target_pairs={{0,12},{2,14},{4,8},{6,10},{8,4},{10,6},{12,0},{14,2},{1,13},{3,15... | collective-permute-start | bytes 98312 | tf_op jit(solution)/shard_map/ppermute | solution.py:218
  63.9 15.1 %collective-permute-start.18 = (bf16[128,128]{1,0:T(8,128)(2,1)S(1)}, bf16[128,128]{1,0:T(8,128)(2,1)S(1)}, u32[]{:S(2)}, u32[]{:S(2)}) collective-permute-start(bf16[128,128]{1,0:T(8,128)(2,1)S(1)} %fusion), channel_id=1, source_target_pairs={{0,48},{16,32},{32,16},{48,0},{1,49},{17,33},{33,17},{49,1},{2,50}... | collective-permute-start | bytes 98312 | tf_op jit(solution)/shard_map/ppermute | solution.py:218
  77.1 5.4 %collective-permute-start.17 = (bf16[128,128]{1,0:T(8,128)(2,1)S(1)}, bf16[128,128]{1,0:T(8,128)(2,1)S(1)}, u32[]{:S(2)}, u32[]{:S(2)}) collective-permute-start(bf16[128,128]{1,0:T(8,128)(2,1)S(1)} %fusion), channel_id=1, source_target_pairs={{0,32},{16,48},{32,0},{48,16},{1,33},{17,49},{33,1},{49,17},{2,34}... | collective-permute-start | bytes 98312 | tf_op jit(solution)/shard_map/ppermute | solution.py:218
  77.1 5.4 %collective-permute-start.16 = (bf16[128,128]{1,0:T(8,128)(2,1)S(1)}, bf16[128,128]{1,0:T(8,128)(2,1)S(1)}, u32[]{:S(2)}, u32[]{:S(2)}) collective-permute-start(bf16[128,128]{1,0:T(8,128)(2,1)S(1)} %fusion), channel_id=1, source_target_pairs={{0,16},{16,0},{32,48},{48,32},{1,17},{17,1},{33,49},{49,33},{2,18}... | collective-permute-start | bytes 98312 | tf_op jit(solution)/shard_map/ppermute | solution.py:218
  82.6 5.2 %collective-permute-start.21 = (bf16[128,128]{1,0:T(8,128)(2,1)S(1)}, bf16[128,128]{1,0:T(8,128)(2,1)S(1)}, u32[]{:S(2)}, u32[]{:S(2)}) collective-permute-start(bf16[128,128]{1,0:T(8,128)(2,1)S(1)} %fusion.1), channel_id=1, source_target_pairs={{0,192},{64,128},{128,64},{192,0},{1,193},{65,129},{129,65},{193,1... | collective-permute-start | bytes 98312 | tf_op jit(solution)/shard_map/ppermute | solution.py:218
  84.3 5.4 %collective-permute-start.20 = (bf16[128,128]{1,0:T(8,128)(2,1)S(1)}, bf16[128,128]{1,0:T(8,128)(2,1)S(1)}, u32[]{:S(2)}, u32[]{:S(2)}) collective-permute-start(bf16[128,128]{1,0:T(8,128)(2,1)S(1)} %fusion.1), channel_id=1, source_target_pairs={{0,128},{64,192},{128,0},{192,64},{1,129},{65,193},{129,1},{193,65... | collective-permute-start | bytes 98312 | tf_op jit(solution)/shard_map/ppermute | solution.py:218
  86.0 3.9 %collective-permute-start.19 = (bf16[128,128]{1,0:T(8,128)(2,1)S(1)}, bf16[128,128]{1,0:T(8,128)(2,1)S(1)}, u32[]{:S(2)}, u32[]{:S(2)}) collective-permute-start(bf16[128,128]{1,0:T(8,128)(2,1)S(1)} %fusion.1), channel_id=1, source_target_pairs={{0,64},{64,0},{128,192},{192,128},{1,65},{65,1},{129,193},{193,129... | collective-permute-start | bytes 98312 | tf_op jit(solution)/shard_map/ppermute | solution.py:218

commit v3 on v2

--- a/solution.py
+++ b/solution.py
@@ -132,40 +132,42 @@
     return lax.axis_index("band") == 0
 
 
-def arrived(there_ref, back_ref):
-    there, back = there_ref[...], back_ref[...]
-    return jnp.where(on_first_core(), there, back), jnp.where(on_first_core(), back, there)
-
-
-def depart(new_ref, there_ref, back_ref):
+def on_even_chip():
+    return lax.axis_index("z") % 2 == 0
+
+
+def arrived(right_ref, left_ref):
+    right, left = right_ref[...], left_ref[...]
+    return jnp.where(on_even_chip(), left, right), jnp.where(on_even_chip(), right, left)
+
+
+def depart(new_ref, right_ref, left_ref):
     reach = DIST * B
     top = new_ref[:, new_ref.shape[1] - reach :]
     bottom = new_ref[:, :reach]
-    there_ref[...] = jnp.where(on_first_core(), top, bottom)
-    back_ref[...] = jnp.where(on_first_core(), bottom, top)
-
-
-def edges_kernel(new_ref, top_ref, bottom_ref):
-    reach = DIST * B
-    top_ref[...] = new_ref[:, new_ref.shape[1] - reach :]
-    bottom_ref[...] = new_ref[:, :reach]
-
-
-def first_kernel(acc_ref, low_ref, high_ref, a_ref, new_ref, there_ref, back_ref):
-    for i, step, total in apply_halo(acc_ref, low_ref[...], high_ref[...], a_ref):
+    right_ref[...] = jnp.where(on_even_chip(), top, bottom)
+    left_ref[...] = jnp.where(on_even_chip(), bottom, top)
+
+
+def edges_kernel(new_ref, to_left_ref, to_right_ref):
+    depart(new_ref, to_right_ref, to_left_ref)
+
+
+def first_kernel(acc_ref, right_ref, left_ref, a_ref, new_ref, to_right_ref, to_left_ref):
+    for i, step, total in apply_halo(acc_ref, *arrived(right_ref, left_ref), a_ref):
         new_ref[:, i : i + step] = total.astype(new_ref.dtype)
-    depart(new_ref, there_ref, back_ref)
-
-
-def next_kernel(acc_ref, from_ref, to_ref, a_ref, older_ref, new_ref, there_ref, back_ref):
-    for i, step, total in apply_halo(acc_ref, *arrived(from_ref, to_ref), a_ref):
+    depart(new_ref, to_right_ref, to_left_ref)
+
+
+def next_kernel(acc_ref, right_ref, left_ref, a_ref, older_ref, new_ref, to_right_ref, to_left_ref):
+    for i, step, total in apply_halo(acc_ref, *arrived(right_ref, left_ref), a_ref):
         older = older_ref[:, i : i + step].astype(jnp.float32)
         new_ref[:, i : i + step] = (2.0 * total - older).astype(new_ref.dtype)
-    depart(new_ref, there_ref, back_ref)
-
-
-def image_kernel(acc_ref, from_ref, to_ref, a_ref, new_ref):
-    for i, step, total in apply_halo(acc_ref, *arrived(from_ref, to_ref), a_ref):
+    depart(new_ref, to_right_ref, to_left_ref)
+
+
+def image_kernel(acc_ref, right_ref, left_ref, a_ref, new_ref):
+    for i, step, total in apply_halo(acc_ref, *arrived(right_ref, left_ref), a_ref):
         new_ref[:, i : i + step] = total.astype(new_ref.dtype)
 
 
@@ -195,22 +197,21 @@
     out_ref[half:, :] = both(image_ref[...], other_image_ref[...])
 
 
-def exchange_ring(top, bottom):
+def exchange(to_right, to_left, left_first=False):
     count = lax.axis_size(ROWS)
-    up = [(i, (i + 1) % count) for i in range(count)]
-    down = [(target, source) for source, target in up]
-    return lax.ppermute(top, ROWS, up), lax.ppermute(bottom, ROWS, down)
-
-
-def exchange_loop(there, back):
-    count = lax.axis_size(ROWS)
-    loop = [2 * i for i in range(count)] + [2 * i + 1 for i in reversed(range(count))]
-    forth = list(zip(loop, loop[1:] + loop[:1]))
     every = (*ROWS, "band")
-    return (
-        lax.ppermute(there, every, forth),
-        lax.ppermute(back, every, [(target, source) for source, target in forth]),
-    )
+    pairs = [(i, i + 1) for i in range(0, count, 2)], [(i, i + 1) for i in range(1, count - 1, 2)]
+    right, left = [
+        [(2 * a + core, 2 * b + core) for core in (0, 1) for i, j in p for a, b in ((i, j), (j, i))]
+        for p in pairs
+    ]
+    for end in (0, count - 1):
+        left += [(2 * end, 2 * end + 1), (2 * end + 1, 2 * end)]
+    if left_first:
+        from_left = lax.ppermute(to_left, every, left)
+        return lax.ppermute(to_right, every, right), from_left
+    from_right = lax.ppermute(to_right, every, right)
+    return from_right, lax.ppermute(to_left, every, left)
 
 
 def swapped(value, axis, distance):
@@ -242,24 +243,24 @@
         return in_vmem(own_kernel, name, [part], v, band, flops=own_flops)[0]
 
     start = vectors.T
-    low, high = exchange_ring(*in_vmem(edges_kernel, "edges", [halo, halo], start))
+    to_left, to_right = in_vmem(edges_kernel, "edges", [halo, halo], start)
+    right, left = exchange(to_right, to_left, left_first=True)
     band = build_band(neighbours, counts, hamiltonian)
     acc = own_part(start, "own1")
-    level1, there, back = in_vmem(first_kernel, "level1", [field, halo, halo], acc, low, high, band)
+    level1, *edges = in_vmem(first_kernel, "level1", [field, halo, halo], acc, right, left, band)
     older, newer = start, level1
     for degree in range(2, 5):
-        there, back = exchange_loop(there, back)
+        right, left = exchange(*edges)
         acc = own_part(newer, "own%d" % degree)
-        latest, there, back = in_vmem(
-            next_kernel, "level%d" % degree, [field, halo, halo], acc, there, back, band, older
+        latest, *edges = in_vmem(
+            next_kernel, "level%d" % degree, [field, halo, halo], acc, right, left, band, older
         )
         older, newer = newer, latest
-    there, back = exchange_loop(there, back)
-    acc = own_part(newer, "own5")
-    other = swapped(newer, "band", 1)
-    (image,) = in_vmem(image_kernel, "image", [field], acc, there, back, band)
+    right, left = exchange(*edges)
+    acc, mine = lax.optimization_barrier((own_part(newer, "own5"), newer))
+    other = swapped(mine, "band", 1)
+    (image,) = in_vmem(image_kernel, "image", [field], acc, right, left, band)
     other_image = swapped(image, "band", 1)
-    both = ((2 * width, 2 * width), jnp.float32)
     sums = pl.pallas_call(
         gram_kernel,
         out_shape=jax.ShapeDtypeStruct((2 * width, 2 * width), jnp.float32),

time: 92.2 us -> 90.2 us (0.978); the launches traced: 90.6 us -> 90.3 us
  waiting for transfers between devices: 24 us -> 21.6 us
  starting transfers between devices: 47.3 us -> 49.1 us
    ppermute x10, waiting for transfers between devices: 11 us -> 7.24 us  [the longest x4 6.24 us: exchange(): return (from_right, lax.ppermute(to_left, every, left))]
    ppermute x10, starting transfers between devices: 17.4 us -> 19.1 us  [the longest x4 14.8 us: exchange(): return (from_right, lax.ppermute(to_left, every, left))]
    ppermute x12, waiting for transfers between devices: 13.1 us -> 14.3 us  [swapped(): return lax.ppermute(value, axis, [(i, i ^ distance) for i in range(count)])]
  transfers between devices with their start and end apart: 22 -> 22, of which waited for: 15 -> 14; matrix products, arithmetic and copies ran while one was open for 1% -> 1% of each run, Pallas kernels for 13% -> 14%
where the time goes in v3:
time: 90.2 us; the launch traced here: 90.3 us
  starting transfers between devices  49.1 us (54%)
  waiting for transfers between devices  21.6 us (24%)
  Pallas kernels  16.4 us (18%)
  local copies, waits for them, and re-layouts  2.21 us (2%)
    ppermute x12, starting transfers between devices, swapped(): return lax.ppermute(value, axis, [(i, i ^ distance) for i in range(count)])  30.1 us
    ppermute x4, starting transfers between devices, exchange(): return (from_right, lax.ppermute(to_left, every, left))  14.8 us
    ppermute x12, waiting for transfers between devices, swapped(): return lax.ppermute(value, axis, [(i, i ^ distance) for i in range(count)])  14.3 us
    pallas_call x11, Pallas kernels, in_vmem(): pl.pallas_call(kernel, out_shape=[pltpu.VMEM(s, d) for s, d in outs], in_...  10.2 us
    ppermute x4, waiting for transfers between devices, exchange(): return (from_right, lax.ppermute(to_left, every, left))  6.24 us
    pallas_call x1, Pallas kernels, build_band(): pl.pallas_call(band_kernel, out_shape=pltpu.VMEM((block_rows * B, width),...  5.87 us
    ppermute x1, starting transfers between devices, exchange(): from_left = lax.ppermute(to_left, every, left)  1.99 us
    ppermute x1, starting transfers between devices, exchange(): return (lax.ppermute(to_right, every, right), from_left)  1.93 us
  transfers between devices with their start and end apart: 22, of which 14 were waited for; matrix products, arithmetic and copies ran while one was open for 1% of the time, Pallas kernels for 14%

profile of v3, /device:TPU:32, one launch (start us, length us, event | category | flops | bytes accessed | tf_op | source)
XLA Modules:
  0.0 90.3 jit_solution(17290001475922924615)
XLA Ops:
  0.6 0.9 %copy-done = bf16[1280,64]{0,1:T(8,128)(2,1)S(1)} copy-done((bf16[1280,64]{0,1:T(8,128)(2,1)S(1)}, bf16[1280,64]{0,1:T(8,128)(2,1)}, u32[]{:S(2)}) %copy-start) | copy-done | bytes 163864
  1.6 1.9 %collective-permute-start = (bf16[64,1024]{1,0:T(8,128)(2,1)S(1)}, bf16[64,1024]{1,0:T(8,128)(2,1)S(1)}, u32[]{:S(2)}, u32[]{:S(2)}) collective-permute-start(bf16[64,1024]{1,0:T(8,128)(2,1)S(1)} %get-tuple-element.19), channel_id=1, source_target_pairs={{0,2},{2,0},{4,6},{6,4},{8,10},{10,8},{12,14},{14,12},{16,18},{18,... | collective-permute-start | bytes 393224 | tf_op jit(solution)/shard_map/ppermute | solution.py:212
  3.5 2.0 %collective-permute-start.1 = (bf16[64,1024]{1,0:T(8,128)(2,1)S(1)}, bf16[64,1024]{1,0:T(8,128)(2,1)S(1)}, u32[]{:S(2)}, u32[]{:S(2)}) collective-permute-start(bf16[64,1024]{1,0:T(8,128)(2,1)S(1)} %get-tuple-element.20), channel_id=1, source_target_pairs={{2,4},{4,2},{6,8},{8,6},{10,12},{12,10},{14,16},{16,14},{18,20},{2... | collective-permute-start | bytes 393224 | tf_op jit(solution)/shard_map/ppermute | solution.py:211
  5.5 5.9 %band.1.a_ref = bf16[1280,3456]{1,0:T(8,128)(2,1)S(1)} custom-call(s32[1,10]{1,0:T(1,128)} %bitcast.7, s32[10,32]{1,0:T(8,128)} %near_ref.1, bf16[10,32,128,128]{3,2,1,0:T(8,128)(2,1)} %h_ref.1), custom_call_target="tpu_custom_call" | custom-call | tf_op jit(solution)/shard_map/band/pallas_call | solution.py:89
  11.4 1.1 %own1.1.acc_ref = f32[64,1280]{1,0:T(8,128)S(1)} custom-call(bf16[64,1280]{1,0:T(8,128)(2,1)S(1)} %bitcast.5, bf16[1280,3456]{1,0:T(8,128)(2,1)S(1)} %band.1.a_ref), custom_call_target="tpu_custom_call" | custom-call | flops 209715200 | tf_op jit(solution)/shard_map/own1/pallas_call | solution.py:176
  12.5 0.9 %level1.1 = (bf16[64,1280]{1,0:T(8,128)(2,1)S(1)}, bf16[64,1024]{1,0:T(8,128)(2,1)S(1)}, bf16[64,1024]{1,0:T(8,128)(2,1)S(1)}) custom-call(f32[64,1280]{1,0:T(8,128)S(1)} %own1.1.acc_ref, bf16[64,1024]{1,0:T(8,128)(2,1)S(1)} %collective-permute-done.right_ref, bf16[64,1024]{1,0:T(8,128)(2,1)S(1)} %collective-permute-done.1.left_ref, ...), custom_call_target="tpu_custom_call" | custom-call | tf_op jit(solution)/shard_map/level1/pallas_call | solution.py:176
  13.5 0.1 collective-permute-start.2
  13.6 4.2 %collective-permute-start.3 = (bf16[64,1024]{1,0:T(8,128)(2,1)S(1)}, bf16[64,1024]{1,0:T(8,128)(2,1)S(1)}, u32[]{:S(2)}, u32[]{:S(2)}) collective-permute-start(bf16[64,1024]{1,0:T(8,128)(2,1)S(1)} %get-tuple-element.23), channel_id=1, source_target_pairs={{2,4},{4,2},{6,8},{8,6},{10,12},{12,10},{14,16},{16,14},{18,20},{2... | collective-permute-start | bytes 393224 | tf_op jit(solution)/shard_map/ppermute | solution.py:214
  17.7 1.1 %own2.1.acc_ref = f32[64,1280]{1,0:T(8,128)S(1)} custom-call(bf16[64,1280]{1,0:T(8,128)(2,1)S(1)} %get-tuple-element.21.v_ref.older_ref, bf16[1280,3456]{1,0:T(8,128)(2,1)S(1)} %band.1.a_ref), custom_call_target="tpu_custom_call" | custom-call | flops 209715200 | tf_op jit(solution)/shard_map/own2/pallas_call | solution.py:176
  18.9 1.8 %collective-permute-done.3.left_ref = bf16[64,1024]{1,0:T(8,128)(2,1)S(1)} collective-permute-done((bf16[64,1024]{1,0:T(8,128)(2,1)S(1)}, bf16[64,1024]{1,0:T(8,128)(2,1)S(1)}, u32[]{:S(2)}, u32[]{:S(2)}) %collective-permute-start.3) | collective-permute-done | bytes 131104 | tf_op jit(solution)/shard_map/ppermute | solution.py:214
  20.7 0.9 %level2.1 = (bf16[64,1280]{1,0:T(8,128)(2,1)S(1)}, bf16[64,1024]{1,0:T(8,128)(2,1)S(1)}, bf16[64,1024]{1,0:T(8,128)(2,1)S(1)}) custom-call(f32[64,1280]{1,0:T(8,128)S(1)} %own2.1.acc_ref, bf16[64,1024]{1,0:T(8,128)(2,1)S(1)} %collective-permute-done.2.right_ref, bf16[64,1024]{1,0:T(8,128)(2,1)S(1)} %collective-permute-done.3.left_ref, ...), custom_call_target="tpu_custom_call" | custom-call | tf_op jit(solution)/shard_map/level2/pallas_call | solution.py:176
  21.6 0.1 collective-permute-start.4
  21.7 3.3 %collective-permute-start.5 = (bf16[64,1024]{1,0:T(8,128)(2,1)S(1)}, bf16[64,1024]{1,0:T(8,128)(2,1)S(1)}, u32[]{:S(2)}, u32[]{:S(2)}) collective-permute-start(bf16[64,1024]{1,0:T(8,128)(2,1)S(1)} %get-tuple-element.26), channel_id=1, source_target_pairs={{2,4},{4,2},{6,8},{8,6},{10,12},{12,10},{14,16},{16,14},{18,20},{2... | collective-permute-start | bytes 393224 | tf_op jit(solution)/shard_map/ppermute | solution.py:214
  25.0 1.1 %own3.1.acc_ref = f32[64,1280]{1,0:T(8,128)S(1)} custom-call(bf16[64,1280]{1,0:T(8,128)(2,1)S(1)} %get-tuple-element.24.v_ref.older_ref, bf16[1280,3456]{1,0:T(8,128)(2,1)S(1)} %band.1.a_ref), custom_call_target="tpu_custom_call" | custom-call | flops 209715200 | tf_op jit(solution)/shard_map/own3/pallas_call | solution.py:176
  26.1 0.5 collective-permute-done.4.right_ref
  26.7 1.3 %collective-permute-done.5.left_ref = bf16[64,1024]{1,0:T(8,128)(2,1)S(1)} collective-permute-done((bf16[64,1024]{1,0:T(8,128)(2,1)S(1)}, bf16[64,1024]{1,0:T(8,128)(2,1)S(1)}, u32[]{:S(2)}, u32[]{:S(2)}) %collective-permute-start.5) | collective-permute-done | bytes 131104 | tf_op jit(solution)/shard_map/ppermute | solution.py:214
  28.0 0.9 %level3.1 = (bf16[64,1280]{1,0:T(8,128)(2,1)S(1)}, bf16[64,1024]{1,0:T(8,128)(2,1)S(1)}, bf16[64,1024]{1,0:T(8,128)(2,1)S(1)}) custom-call(f32[64,1280]{1,0:T(8,128)S(1)} %own3.1.acc_ref, bf16[64,1024]{1,0:T(8,128)(2,1)S(1)} %collective-permute-done.4.right_ref, bf16[64,1024]{1,0:T(8,128)(2,1)S(1)} %collective-permute-done.5.left_ref, ...), custom_call_target="tpu_custom_call" | custom-call | tf_op jit(solution)/shard_map/level3/pallas_call | solution.py:176
  28.9 0.1 collective-permute-start.6
  29.0 3.9 %collective-permute-start.7 = (bf16[64,1024]{1,0:T(8,128)(2,1)S(1)}, bf16[64,1024]{1,0:T(8,128)(2,1)S(1)}, u32[]{:S(2)}, u32[]{:S(2)}) collective-permute-start(bf16[64,1024]{1,0:T(8,128)(2,1)S(1)} %get-tuple-element.29), channel_id=1, source_target_pairs={{2,4},{4,2},{6,8},{8,6},{10,12},{12,10},{14,16},{16,14},{18,20},{2... | collective-permute-start | bytes 393224 | tf_op jit(solution)/shard_map/ppermute | solution.py:214
  32.9 1.1 %own4.1.acc_ref = f32[64,1280]{1,0:T(8,128)S(1)} custom-call(bf16[64,1280]{1,0:T(8,128)(2,1)S(1)} %get-tuple-element.27.v_ref, bf16[1280,3456]{1,0:T(8,128)(2,1)S(1)} %band.1.a_ref), custom_call_target="tpu_custom_call" | custom-call | flops 209715200 | tf_op jit(solution)/shard_map/own4/pallas_call | solution.py:176
  34.1 1.8 %collective-permute-done.7.left_ref = bf16[64,1024]{1,0:T(8,128)(2,1)S(1)} collective-permute-done((bf16[64,1024]{1,0:T(8,128)(2,1)S(1)}, bf16[64,1024]{1,0:T(8,128)(2,1)S(1)}, u32[]{:S(2)}, u32[]{:S(2)}) %collective-permute-start.7) | collective-permute-done | bytes 131104 | tf_op jit(solution)/shard_map/ppermute | solution.py:214
  35.9 0.9 %level4.1 = (bf16[64,1280]{1,0:T(8,128)(2,1)S(1)}, bf16[64,1024]{1,0:T(8,128)(2,1)S(1)}, bf16[64,1024]{1,0:T(8,128)(2,1)S(1)}) custom-call(f32[64,1280]{1,0:T(8,128)S(1)} %own4.1.acc_ref, bf16[64,1024]{1,0:T(8,128)(2,1)S(1)} %collective-permute-done.6.right_ref, bf16[64,1024]{1,0:T(8,128)(2,1)S(1)} %collective-permute-done.7.left_ref, ...), custom_call_target="tpu_custom_call" | custom-call | tf_op jit(solution)/shard_map/level4/pallas_call | solution.py:176
  36.8 0.1 collective-permute-start.9
  36.9 3.3 %collective-permute-start.10 = (bf16[64,1024]{1,0:T(8,128)(2,1)S(1)}, bf16[64,1024]{1,0:T(8,128)(2,1)S(1)}, u32[]{:S(2)}, u32[]{:S(2)}) collective-permute-start(bf16[64,1024]{1,0:T(8,128)(2,1)S(1)} %get-tuple-element.34), channel_id=1, source_target_pairs={{2,4},{4,2},{6,8},{8,6},{10,12},{12,10},{14,16},{16,14},{18,20},{2... | collective-permute-start | bytes 393224 | tf_op jit(solution)/shard_map/ppermute | solution.py:214
  40.2 1.1 %own5.1.acc_ref = f32[64,1280]{1,0:T(8,128)S(1)} custom-call(bf16[64,1280]{1,0:T(8,128)(2,1)S(1)} %get-tuple-element.31.v_ref.own_ref, bf16[1280,3456]{1,0:T(8,128)(2,1)S(1)} %band.1.a_ref), custom_call_target="tpu_custom_call" | custom-call | flops 209715200 | tf_op jit(solution)/shard_map/own5/pallas_call | solution.py:176
  41.4 0.5 collective-permute-done.9.right_ref
  41.9 1.3 %collective-permute-done.10.left_ref = bf16[64,1024]{1,0:T(8,128)(2,1)S(1)} collective-permute-done((bf16[64,1024]{1,0:T(8,128)(2,1)S(1)}, bf16[64,1024]{1,0:T(8,128)(2,1)S(1)}, u32[]{:S(2)}, u32[]{:S(2)}) %collective-permute-start.10) | collective-permute-done | bytes 131104 | tf_op jit(solution)/shard_map/ppermute | solution.py:214
  43.2 0.9 image.1.image_ref
  44.2 1.4 %collective-permute-done.11.other_image_ref = bf16[64,1280]{1,0:T(8,128)(2,1)S(1)} collective-permute-done((bf16[64,1280]{1,0:T(8,128)(2,1)S(1)}, bf16[64,1280]{1,0:T(8,128)(2,1)S(1)}, u32[]{:S(2)}, u32[]{:S(2)}) %collective-permute-start.11) | collective-permute-done | bytes 163872 | tf_op jit(solution)/shard_map/ppermute | solution.py:219
  45.6 0.4 gram.1
  46.0 2.1 %collective-permute-start.14 = (bf16[128,128]{1,0:T(8,128)(2,1)S(1)}, bf16[128,128]{1,0:T(8,128)(2,1)S(1)}, u32[]{:S(2)}, u32[]{:S(2)}) collective-permute-start(bf16[128,128]{1,0:T(8,128)(2,1)S(1)} %reduce-precision_convert_fusion), channel_id=1, source_target_pairs={{0,6},{2,4},{4,2},{6,0},{8,14},{10,12},{12,10},{14,8},{1,7},{3,5},... | collective-permute-start | bytes 98312 | tf_op jit(solution)/shard_map/ppermute | solution.py:219
  48.1 1.6 %collective-permute-start.13 = (bf16[128,128]{1,0:T(8,128)(2,1)S(1)}, bf16[128,128]{1,0:T(8,128)(2,1)S(1)}, u32[]{:S(2)}, u32[]{:S(2)}) collective-permute-start(bf16[128,128]{1,0:T(8,128)(2,1)S(1)} %reduce-precision_convert_fusion), channel_id=1, source_target_pairs={{0,4},{2,6},{4,0},{6,2},{8,12},{10,14},{12,8},{14,10},{1,5},{3,7},... | collective-permute-start | bytes 98312 | tf_op jit(solution)/shard_map/ppermute | solution.py:219
  49.7 1.2 %collective-permute-start.12 = (bf16[128,128]{1,0:T(8,128)(2,1)S(1)}, bf16[128,128]{1,0:T(8,128)(2,1)S(1)}, u32[]{:S(2)}, u32[]{:S(2)}) collective-permute-start(bf16[128,128]{1,0:T(8,128)(2,1)S(1)} %reduce-precision_convert_fusion), channel_id=1, source_target_pairs={{0,2},{2,0},{4,6},{6,4},{8,10},{10,8},{12,14},{14,12},{1,3},{3,1},... | collective-permute-start | bytes 98312 | tf_op jit(solution)/shard_map/ppermute | solution.py:219
  50.9 2.0 %collective-permute-done.13 = bf16[128,128]{1,0:T(8,128)(2,1)S(1)} collective-permute-done((bf16[128,128]{1,0:T(8,128)(2,1)S(1)}, bf16[128,128]{1,0:T(8,128)(2,1)S(1)}, u32[]{:S(2)}, u32[]{:S(2)}) %collective-permute-start.13) | collective-permute-done | bytes 32800 | tf_op jit(solution)/shard_map/ppermute | solution.py:219
  52.9 0.8 collective-permute-done.12
  53.7 5.4 %collective-permute-start.15 = (bf16[128,128]{1,0:T(8,128)(2,1)S(1)}, bf16[128,128]{1,0:T(8,128)(2,1)S(1)}, u32[]{:S(2)}, u32[]{:S(2)}) collective-permute-start(bf16[128,128]{1,0:T(8,128)(2,1)S(1)} %get-tuple-element.35), channel_id=1, source_target_pairs={{0,12},{2,14},{4,8},{6,10},{8,4},{10,6},{12,0},{14,2},{1,13},{3,15... | collective-permute-start | bytes 98312 | tf_op jit(solution)/shard_map/ppermute | solution.py:219
  59.2 1.9 %collective-permute-done.15 = bf16[128,128]{1,0:T(8,128)(2,1)S(1)} collective-permute-done((bf16[128,128]{1,0:T(8,128)(2,1)S(1)}, bf16[128,128]{1,0:T(8,128)(2,1)S(1)}, u32[]{:S(2)}, u32[]{:S(2)}) %collective-permute-start.15) | collective-permute-done | bytes 32800 | tf_op jit(solution)/shard_map/ppermute | solution.py:219
  61.1 11.6 %collective-permute-start.18 = (bf16[128,128]{1,0:T(8,128)(2,1)S(1)}, bf16[128,128]{1,0:T(8,128)(2,1)S(1)}, u32[]{:S(2)}, u32[]{:S(2)}) collective-permute-start(bf16[128,128]{1,0:T(8,128)(2,1)S(1)} %fusion), channel_id=1, source_target_pairs={{0,48},{16,32},{32,16},{48,0},{1,49},{17,33},{33,17},{49,1},{2,50}... | collective-permute-start | bytes 98312 | tf_op jit(solution)/shard_map/ppermute | solution.py:219
  72.7 1.0 %collective-permute-start.16 = (bf16[128,128]{1,0:T(8,128)(2,1)S(1)}, bf16[128,128]{1,0:T(8,128)(2,1)S(1)}, u32[]{:S(2)}, u32[]{:S(2)}) collective-permute-start(bf16[128,128]{1,0:T(8,128)(2,1)S(1)} %fusion), channel_id=1, source_target_pairs={{0,16},{16,0},{32,48},{48,32},{1,17},{17,1},{33,49},{49,33},{2,18}... | collective-permute-start | bytes 98312 | tf_op jit(solution)/shard_map/ppermute | solution.py:219
  73.7 0.9 %collective-permute-done.18 = bf16[128,128]{1,0:T(8,128)(2,1)S(1)} collective-permute-done((bf16[128,128]{1,0:T(8,128)(2,1)S(1)}, bf16[128,128]{1,0:T(8,128)(2,1)S(1)}, u32[]{:S(2)}, u32[]{:S(2)}) %collective-permute-start.18) | collective-permute-done | bytes 32800 | tf_op jit(solution)/shard_map/ppermute | solution.py:219
  74.6 3.5 %collective-permute-done.17 = bf16[128,128]{1,0:T(8,128)(2,1)S(1)} collective-permute-done((bf16[128,128]{1,0:T(8,128)(2,1)S(1)}, bf16[128,128]{1,0:T(8,128)(2,1)S(1)}, u32[]{:S(2)}, u32[]{:S(2)}) %collective-permute-start.17) | collective-permute-done | bytes 32800 | tf_op jit(solution)/shard_map/ppermute | solution.py:219
  78.2 6.0 %collective-permute-start.21 = (bf16[128,128]{1,0:T(8,128)(2,1)S(1)}, bf16[128,128]{1,0:T(8,128)(2,1)S(1)}, u32[]{:S(2)}, u32[]{:S(2)}) collective-permute-start(bf16[128,128]{1,0:T(8,128)(2,1)S(1)} %fusion.1), channel_id=1, source_target_pairs={{0,192},{64,128},{128,64},{192,0},{1,193},{65,129},{129,65},{193,1... | collective-permute-start | bytes 98312 | tf_op jit(solution)/shard_map/ppermute | solution.py:219
  84.2 0.3 collective-permute-start.20
  84.5 0.6 collective-permute-start.19
  85.1 0.7 copy.7
  85.8 0.3 collective-permute-done.21
  86.1 3.5 %collective-permute-done.20 = bf16[128,128]{1,0:T(8,128)(2,1)S(1)} collective-permute-done((bf16[128,128]{1,0:T(8,128)(2,1)S(1)}, bf16[128,128]{1,0:T(8,128)(2,1)S(1)}, u32[]{:S(2)}, u32[]{:S(2)}) %collective-permute-start.20) | collective-permute-done | bytes 32800 | tf_op jit(solution)/shard_map/ppermute | solution.py:219
  89.7 0.6 fusion.3
  (20 shorter events, 0.3 us)
Async XLA Ops:
  0.6 0.9 %copy-start = (bf16[1280,64]{0,1:T(8,128)(2,1)S(1)}, bf16[1280,64]{0,1:T(8,128)(2,1)}, u32[]{:S(2)}) copy-start(bf16[1280,64]{0,1:T(8,128)(2,1)} %param.7) | copy-start | bytes 491524
  1.5 9.8 %copy-start.1 = (bf16[1280,64]{0,1:T(8,128)(2,1)S(1)}, bf16[1280,64]{0,1:T(8,128)(2,1)}, u32[]{:S(2)}) copy-start(bf16[1280,64]{0,1:T(8,128)(2,1)} %param.7) | copy-start | bytes 491524
  1.6 10.9 %collective-permute-start = (bf16[64,1024]{1,0:T(8,128)(2,1)S(1)}, bf16[64,1024]{1,0:T(8,128)(2,1)S(1)}, u32[]{:S(2)}, u32[]{:S(2)}) collective-permute-start(bf16[64,1024]{1,0:T(8,128)(2,1)S(1)} %get-tuple-element.19), channel_id=1, source_target_pairs={{0,2},{2,0},{4,6},{6,4},{8,10},{10,8},{12,14},{14,12},{16,18},{18,... | collective-permute-start | bytes 393224 | tf_op jit(solution)/shard_map/ppermute | solution.py:212
  3.5 9.0 %collective-permute-start.1 = (bf16[64,1024]{1,0:T(8,128)(2,1)S(1)}, bf16[64,1024]{1,0:T(8,128)(2,1)S(1)}, u32[]{:S(2)}, u32[]{:S(2)}) collective-permute-start(bf16[64,1024]{1,0:T(8,128)(2,1)S(1)} %get-tuple-element.20), channel_id=1, source_target_pairs={{2,4},{4,2},{6,8},{8,6},{10,12},{12,10},{14,16},{16,14},{18,20},{2... | collective-permute-start | bytes 393224 | tf_op jit(solution)/shard_map/ppermute | solution.py:211
  13.5 5.4 %collective-permute-start.2 = (bf16[64,1024]{1,0:T(8,128)(2,1)S(1)}, bf16[64,1024]{1,0:T(8,128)(2,1)S(1)}, u32[]{:S(2)}, u32[]{:S(2)}) collective-permute-start(bf16[64,1024]{1,0:T(8,128)(2,1)S(1)} %get-tuple-element.22), channel_id=1, source_target_pairs={{0,2},{2,0},{4,6},{6,4},{8,10},{10,8},{12,14},{14,12},{16,18},{18,... | collective-permute-start | bytes 393224 | tf_op jit(solution)/shard_map/ppermute | solution.py:213
  13.6 7.1 %collective-permute-start.3 = (bf16[64,1024]{1,0:T(8,128)(2,1)S(1)}, bf16[64,1024]{1,0:T(8,128)(2,1)S(1)}, u32[]{:S(2)}, u32[]{:S(2)}) collective-permute-start(bf16[64,1024]{1,0:T(8,128)(2,1)S(1)} %get-tuple-element.23), channel_id=1, source_target_pairs={{2,4},{4,2},{6,8},{8,6},{10,12},{12,10},{14,16},{16,14},{18,20},{2... | collective-permute-start | bytes 393224 | tf_op jit(solution)/shard_map/ppermute | solution.py:214
  21.6 5.1 %collective-permute-start.4 = (bf16[64,1024]{1,0:T(8,128)(2,1)S(1)}, bf16[64,1024]{1,0:T(8,128)(2,1)S(1)}, u32[]{:S(2)}, u32[]{:S(2)}) collective-permute-start(bf16[64,1024]{1,0:T(8,128)(2,1)S(1)} %get-tuple-element.25), channel_id=1, source_target_pairs={{0,2},{2,0},{4,6},{6,4},{8,10},{10,8},{12,14},{14,12},{16,18},{18,... | collective-permute-start | bytes 393224 | tf_op jit(solution)/shard_map/ppermute | solution.py:213
  21.7 6.3 %collective-permute-start.5 = (bf16[64,1024]{1,0:T(8,128)(2,1)S(1)}, bf16[64,1024]{1,0:T(8,128)(2,1)S(1)}, u32[]{:S(2)}, u32[]{:S(2)}) collective-permute-start(bf16[64,1024]{1,0:T(8,128)(2,1)S(1)} %get-tuple-element.26), channel_id=1, source_target_pairs={{2,4},{4,2},{6,8},{8,6},{10,12},{12,10},{14,16},{16,14},{18,20},{2... | collective-permute-start | bytes 393224 | tf_op jit(solution)/shard_map/ppermute | solution.py:214
  28.9 5.2 %collective-permute-start.6 = (bf16[64,1024]{1,0:T(8,128)(2,1)S(1)}, bf16[64,1024]{1,0:T(8,128)(2,1)S(1)}, u32[]{:S(2)}, u32[]{:S(2)}) collective-permute-start(bf16[64,1024]{1,0:T(8,128)(2,1)S(1)} %get-tuple-element.28), channel_id=1, source_target_pairs={{0,2},{2,0},{4,6},{6,4},{8,10},{10,8},{12,14},{14,12},{16,18},{18,... | collective-permute-start | bytes 393224 | tf_op jit(solution)/shard_map/ppermute | solution.py:213
  29.0 6.9 %collective-permute-start.7 = (bf16[64,1024]{1,0:T(8,128)(2,1)S(1)}, bf16[64,1024]{1,0:T(8,128)(2,1)S(1)}, u32[]{:S(2)}, u32[]{:S(2)}) collective-permute-start(bf16[64,1024]{1,0:T(8,128)(2,1)S(1)} %get-tuple-element.29), channel_id=1, source_target_pairs={{2,4},{4,2},{6,8},{8,6},{10,12},{12,10},{14,16},{16,14},{18,20},{2... | collective-permute-start | bytes 393224 | tf_op jit(solution)/shard_map/ppermute | solution.py:214
  36.8 5.1 %collective-permute-start.9 = (bf16[64,1024]{1,0:T(8,128)(2,1)S(1)}, bf16[64,1024]{1,0:T(8,128)(2,1)S(1)}, u32[]{:S(2)}, u32[]{:S(2)}) collective-permute-start(bf16[64,1024]{1,0:T(8,128)(2,1)S(1)} %get-tuple-element.33), channel_id=1, source_target_pairs={{0,2},{2,0},{4,6},{6,4},{8,10},{10,8},{12,14},{14,12},{16,18},{18,... | collective-permute-start | bytes 393224 | tf_op jit(solution)/shard_map/ppermute | solution.py:213
  36.9 6.3 %collective-permute-start.10 = (bf16[64,1024]{1,0:T(8,128)(2,1)S(1)}, bf16[64,1024]{1,0:T(8,128)(2,1)S(1)}, u32[]{:S(2)}, u32[]{:S(2)}) collective-permute-start(bf16[64,1024]{1,0:T(8,128)(2,1)S(1)} %get-tuple-element.34), channel_id=1, source_target_pairs={{2,4},{4,2},{6,8},{8,6},{10,12},{12,10},{14,16},{16,14},{18,20},{2... | collective-permute-start | bytes 393224 | tf_op jit(solution)/shard_map/ppermute | solution.py:214
  41.4 2.8 %collective-permute-start.8 = (bf16[64,1280]{1,0:T(8,128)(2,1)S(1)}, bf16[64,1280]{1,0:T(8,128)(2,1)S(1)}, u32[]{:S(2)}, u32[]{:S(2)}) collective-permute-start(bf16[64,1280]{1,0:T(8,128)(2,1)S(1)} %get-tuple-element.31.v_ref.own_ref), channel_id=1, source_target_pairs={{0,1},{1,0},{2,3},{3,2},{4,5},{5,4},{6,7},{7,6},{8,9},{9,8},{10,11... | collective-permute-start | bytes 491528 | tf_op jit(solution)/shard_map/ppermute | solution.py:219
  44.1 1.5 %collective-permute-start.11 = (bf16[64,1280]{1,0:T(8,128)(2,1)S(1)}, bf16[64,1280]{1,0:T(8,128)(2,1)S(1)}, u32[]{:S(2)}, u32[]{:S(2)}) collective-permute-start(bf16[64,1280]{1,0:T(8,128)(2,1)S(1)} %image.1.image_ref), channel_id=1, source_target_pairs={{0,1},{1,0},{2,3},{3,2},{4,5},{5,4},{6,7},{7,6},{8,9},{9,8},{10,11... | collective-permute-start | bytes 491528 | tf_op jit(solution)/shard_map/ppermute | solution.py:219
  46.0 4.9 %collective-permute-start.14 = (bf16[128,128]{1,0:T(8,128)(2,1)S(1)}, bf16[128,128]{1,0:T(8,128)(2,1)S(1)}, u32[]{:S(2)}, u32[]{:S(2)}) collective-permute-start(bf16[128,128]{1,0:T(8,128)(2,1)S(1)} %reduce-precision_convert_fusion), channel_id=1, source_target_pairs={{0,6},{2,4},{4,2},{6,0},{8,14},{10,12},{12,10},{14,8},{1,7},{3,5},... | collective-permute-start | bytes 98312 | tf_op jit(solution)/shard_map/ppermute | solution.py:219
  48.1 4.8 %collective-permute-start.13 = (bf16[128,128]{1,0:T(8,128)(2,1)S(1)}, bf16[128,128]{1,0:T(8,128)(2,1)S(1)}, u32[]{:S(2)}, u32[]{:S(2)}) collective-permute-start(bf16[128,128]{1,0:T(8,128)(2,1)S(1)} %reduce-precision_convert_fusion), channel_id=1, source_target_pairs={{0,4},{2,6},{4,0},{6,2},{8,12},{10,14},{12,8},{14,10},{1,5},{3,7},... | collective-permute-start | bytes 98312 | tf_op jit(solution)/shard_map/ppermute | solution.py:219
  49.7 4.0 %collective-permute-start.12 = (bf16[128,128]{1,0:T(8,128)(2,1)S(1)}, bf16[128,128]{1,0:T(8,128)(2,1)S(1)}, u32[]{:S(2)}, u32[]{:S(2)}) collective-permute-start(bf16[128,128]{1,0:T(8,128)(2,1)S(1)} %reduce-precision_convert_fusion), channel_id=1, source_target_pairs={{0,2},{2,0},{4,6},{6,4},{8,10},{10,8},{12,14},{14,12},{1,3},{3,1},... | collective-permute-start | bytes 98312 | tf_op jit(solution)/shard_map/ppermute | solution.py:219
  53.7 7.3 %collective-permute-start.15 = (bf16[128,128]{1,0:T(8,128)(2,1)S(1)}, bf16[128,128]{1,0:T(8,128)(2,1)S(1)}, u32[]{:S(2)}, u32[]{:S(2)}) collective-permute-start(bf16[128,128]{1,0:T(8,128)(2,1)S(1)} %get-tuple-element.35), channel_id=1, source_target_pairs={{0,12},{2,14},{4,8},{6,10},{8,4},{10,6},{12,0},{14,2},{1,13},{3,15... | collective-permute-start | bytes 98312 | tf_op jit(solution)/shard_map/ppermute | solution.py:219
  61.1 13.5 %collective-permute-start.18 = (bf16[128,128]{1,0:T(8,128)(2,1)S(1)}, bf16[128,128]{1,0:T(8,128)(2,1)S(1)}, u32[]{:S(2)}, u32[]{:S(2)}) collective-permute-start(bf16[128,128]{1,0:T(8,128)(2,1)S(1)} %fusion), channel_id=1, source_target_pairs={{0,48},{16,32},{32,16},{48,0},{1,49},{17,33},{33,17},{49,1},{2,50}... | collective-permute-start | bytes 98312 | tf_op jit(solution)/shard_map/ppermute | solution.py:219
  72.7 5.4 %collective-permute-start.17 = (bf16[128,128]{1,0:T(8,128)(2,1)S(1)}, bf16[128,128]{1,0:T(8,128)(2,1)S(1)}, u32[]{:S(2)}, u32[]{:S(2)}) collective-permute-start(bf16[128,128]{1,0:T(8,128)(2,1)S(1)} %fusion), channel_id=1, source_target_pairs={{0,32},{16,48},{32,0},{48,16},{1,33},{17,49},{33,1},{49,17},{2,34}... | collective-permute-start | bytes 98312 | tf_op jit(solution)/shard_map/ppermute | solution.py:219
  72.7 5.4 %collective-permute-start.16 = (bf16[128,128]{1,0:T(8,128)(2,1)S(1)}, bf16[128,128]{1,0:T(8,128)(2,1)S(1)}, u32[]{:S(2)}, u32[]{:S(2)}) collective-permute-start(bf16[128,128]{1,0:T(8,128)(2,1)S(1)} %fusion), channel_id=1, source_target_pairs={{0,16},{16,0},{32,48},{48,32},{1,17},{17,1},{33,49},{49,33},{2,18}... | collective-permute-start | bytes 98312 | tf_op jit(solution)/shard_map/ppermute | solution.py:219
  78.2 7.9 %collective-permute-start.21 = (bf16[128,128]{1,0:T(8,128)(2,1)S(1)}, bf16[128,128]{1,0:T(8,128)(2,1)S(1)}, u32[]{:S(2)}, u32[]{:S(2)}) collective-permute-start(bf16[128,128]{1,0:T(8,128)(2,1)S(1)} %fusion.1), channel_id=1, source_target_pairs={{0,192},{64,128},{128,64},{192,0},{1,193},{65,129},{129,65},{193,1... | collective-permute-start | bytes 98312 | tf_op jit(solution)/shard_map/ppermute | solution.py:219
  84.2 5.4 %collective-permute-start.20 = (bf16[128,128]{1,0:T(8,128)(2,1)S(1)}, bf16[128,128]{1,0:T(8,128)(2,1)S(1)}, u32[]{:S(2)}, u32[]{:S(2)}) collective-permute-start(bf16[128,128]{1,0:T(8,128)(2,1)S(1)} %fusion.1), channel_id=1, source_target_pairs={{0,128},{64,192},{128,0},{192,64},{1,129},{65,193},{129,1},{193,65... | collective-permute-start | bytes 98312 | tf_op jit(solution)/shard_map/ppermute | solution.py:219
  84.5 5.1 %collective-permute-start.19 = (bf16[128,128]{1,0:T(8,128)(2,1)S(1)}, bf16[128,128]{1,0:T(8,128)(2,1)S(1)}, u32[]{:S(2)}, u32[]{:S(2)}) collective-permute-start(bf16[128,128]{1,0:T(8,128)(2,1)S(1)} %fusion.1), channel_id=1, source_target_pairs={{0,64},{64,0},{128,192},{192,128},{1,65},{65,1},{129,193},{193,129... | collective-permute-start | bytes 98312 | tf_op jit(solution)/shard_map/ppermute | solution.py:219

commit v4 on v3

--- a/solution.py
+++ b/solution.py
@@ -107,25 +107,51 @@
     )(counts.reshape(1, block_rows), neighbours, hamiltonian)
 
 
-def own_kernel(v_ref, a_ref, acc_ref):
-    rows = acc_ref.shape[1]
-    v = v_ref[...]
-    for i in range(0, rows, 2 * B):
-        acc_ref[:, i : i + 2 * B] = dot_nt(v, a_ref[i : i + 2 * B, DIST * B : DIST * B + rows])
-
-
-def apply_halo(acc_ref, low, high, a_ref):
+def low_part(low, a_ref, i, step):
+    if i >= DIST * B:
+        return 0.0
+    return dot_nt(low[:, i:], a_ref[i : i + step, i : DIST * B])
+
+
+def high_part(high, a_ref, i, step):
+    upper = a_ref.shape[0] + DIST * B
+    depth = i + step - (a_ref.shape[0] - DIST * B)
+    if depth <= 0:
+        return 0.0
+    return dot_nt(high[:, :depth], a_ref[i : i + step, upper : upper + depth])
+
+
+def near_kernel(v_ref, right_ref, a_ref, acc_ref):
     rows = acc_ref.shape[1]
     step = 2 * B
-    upper = DIST * B + rows
-    for i in range(0, rows, step):
-        total = acc_ref[:, i : i + step]
-        if i < DIST * B:
-            total += dot_nt(low[:, i:], a_ref[i : i + step, i : DIST * B])
-        depth = i + step - (rows - DIST * B)
-        if depth > 0:
-            total += dot_nt(high[:, :depth], a_ref[i : i + step, upper : upper + depth])
-        yield i, step, total
+    v = v_ref[...]
+
+    def run(part):
+        halo = right_ref[...]
+        for i in range(0, rows, step):
+            own = dot_nt(v, a_ref[i : i + step, DIST * B : DIST * B + rows])
+            acc_ref[:, i : i + step] = own + part(halo, a_ref, i, step)
+
+    pl.when(on_even_chip())(lambda: run(high_part))
+    pl.when(jnp.logical_not(on_even_chip()))(lambda: run(low_part))
+
+
+def finish(acc_ref, left_ref, a_ref, new_ref, older_ref=None):
+    rows = acc_ref.shape[1]
+    step = 2 * B
+
+    def run(halo, part):
+        for i in range(0, rows, step):
+            total = acc_ref[:, i : i + step] + part(halo, a_ref, i, step)
+            if older_ref is not None:
+                total = 2.0 * total - older_ref[:, i : i + step].astype(jnp.float32)
+            new_ref[:, i : i + step] = total.astype(new_ref.dtype)
+
+    reach = DIST * B
+    low = left_ref[:, left_ref.shape[1] - reach :]
+    high = left_ref[:, :reach]
+    pl.when(on_even_chip())(lambda: run(low, low_part))
+    pl.when(jnp.logical_not(on_even_chip()))(lambda: run(high, high_part))
 
 
 def on_first_core():
@@ -136,39 +162,31 @@
     return lax.axis_index("z") % 2 == 0
 
 
-def arrived(right_ref, left_ref):
-    right, left = right_ref[...], left_ref[...]
-    return jnp.where(on_even_chip(), left, right), jnp.where(on_even_chip(), right, left)
-
-
-def depart(new_ref, right_ref, left_ref):
+def depart(new_ref, to_right_ref, to_left_ref):
     reach = DIST * B
     top = new_ref[:, new_ref.shape[1] - reach :]
     bottom = new_ref[:, :reach]
-    right_ref[...] = jnp.where(on_even_chip(), top, bottom)
-    left_ref[...] = jnp.where(on_even_chip(), bottom, top)
-
-
-def edges_kernel(new_ref, to_left_ref, to_right_ref):
+    to_right_ref[...] = jnp.where(on_even_chip(), top, bottom)
+    if to_left_ref is not None:
+        to_left_ref[...] = jnp.where(on_even_chip(), bottom, top)
+
+
+def edge_kernel(new_ref, to_right_ref):
+    depart(new_ref, to_right_ref, None)
+
+
+def first_kernel(acc_ref, left_ref, a_ref, new_ref, to_right_ref, to_left_ref):
+    finish(acc_ref, left_ref, a_ref, new_ref)
     depart(new_ref, to_right_ref, to_left_ref)
 
 
-def first_kernel(acc_ref, right_ref, left_ref, a_ref, new_ref, to_right_ref, to_left_ref):
-    for i, step, total in apply_halo(acc_ref, *arrived(right_ref, left_ref), a_ref):
-        new_ref[:, i : i + step] = total.astype(new_ref.dtype)
+def next_kernel(acc_ref, left_ref, a_ref, older_ref, new_ref, to_right_ref, to_left_ref):
+    finish(acc_ref, left_ref, a_ref, new_ref, older_ref)
     depart(new_ref, to_right_ref, to_left_ref)
 
 
-def next_kernel(acc_ref, right_ref, left_ref, a_ref, older_ref, new_ref, to_right_ref, to_left_ref):
-    for i, step, total in apply_halo(acc_ref, *arrived(right_ref, left_ref), a_ref):
-        older = older_ref[:, i : i + step].astype(jnp.float32)
-        new_ref[:, i : i + step] = (2.0 * total - older).astype(new_ref.dtype)
-    depart(new_ref, to_right_ref, to_left_ref)
-
-
-def image_kernel(acc_ref, right_ref, left_ref, a_ref, new_ref):
-    for i, step, total in apply_halo(acc_ref, *arrived(right_ref, left_ref), a_ref):
-        new_ref[:, i : i + step] = total.astype(new_ref.dtype)
+def image_kernel(acc_ref, left_ref, a_ref, new_ref):
+    finish(acc_ref, left_ref, a_ref, new_ref)
 
 
 def in_vmem(kernel, name, outs, *args, flops=0):
@@ -197,7 +215,7 @@
     out_ref[half:, :] = both(image_ref[...], other_image_ref[...])
 
 
-def exchange(to_right, to_left, left_first=False):
+def exchange(to_right, to_left):
     count = lax.axis_size(ROWS)
     every = (*ROWS, "band")
     pairs = [(i, i + 1) for i in range(0, count, 2)], [(i, i + 1) for i in range(1, count - 1, 2)]
@@ -207,11 +225,7 @@
     ]
     for end in (0, count - 1):
         left += [(2 * end, 2 * end + 1), (2 * end + 1, 2 * end)]
-    if left_first:
-        from_left = lax.ppermute(to_left, every, left)
-        return lax.ppermute(to_right, every, right), from_left
-    from_right = lax.ppermute(to_right, every, right)
-    return from_right, lax.ppermute(to_left, every, left)
+    return lax.ppermute(to_right, every, right), lax.ppermute(to_left, every, left)
 
 
 def swapped(value, axis, distance):
@@ -237,29 +251,28 @@
     field = ((width, rows), jnp.bfloat16)
     halo = ((width, reach), jnp.bfloat16)
     part = ((width, rows), jnp.float32)
-    own_flops = 2 * width * rows * rows
-
-    def own_part(v, name):
-        return in_vmem(own_kernel, name, [part], v, band, flops=own_flops)[0]
+    near_flops = 3 * width * rows * rows
+
+    def near(v, right, name):
+        return in_vmem(near_kernel, name, [part], v, right, band, flops=near_flops)[0]
 
     start = vectors.T
-    to_left, to_right = in_vmem(edges_kernel, "edges", [halo, halo], start)
-    right, left = exchange(to_right, to_left, left_first=True)
+    right, left = exchange(*in_vmem(edge_kernel, "edge", [halo], start), start)
     band = build_band(neighbours, counts, hamiltonian)
-    acc = own_part(start, "own1")
-    level1, *edges = in_vmem(first_kernel, "level1", [field, halo, halo], acc, right, left, band)
+    acc = near(start, right, "near1")
+    level1, *edges = in_vmem(first_kernel, "level1", [field, halo, halo], acc, left, band)
     older, newer = start, level1
     for degree in range(2, 5):
         right, left = exchange(*edges)
-        acc = own_part(newer, "own%d" % degree)
+        acc = near(newer, right, "near%d" % degree)
         latest, *edges = in_vmem(
-            next_kernel, "level%d" % degree, [field, halo, halo], acc, right, left, band, older
+            next_kernel, "level%d" % degree, [field, halo, halo], acc, left, band, older
         )
         older, newer = newer, latest
     right, left = exchange(*edges)
-    acc, mine = lax.optimization_barrier((own_part(newer, "own5"), newer))
+    acc, mine = lax.optimization_barrier((near(newer, right, "near5"), newer))
     other = swapped(mine, "band", 1)
-    (image,) = in_vmem(image_kernel, "image", [field], acc, right, left, band)
+    (image,) = in_vmem(image_kernel, "image", [field], acc, left, band)
     other_image = swapped(image, "band", 1)
     sums = pl.pallas_call(
         gram_kernel,

time: 90.2 us -> 90.1 us (level)
  waiting for transfers between devices: 21.6 us -> 20.3 us
    ppermute x10, waiting for transfers between devices: 7.24 us -> 5.62 us  [the longest x5 2.86 us: exchange(): lax.ppermute(to_right, every, right)]
    ppermute x10, starting transfers between devices: 19.1 us -> 20.1 us  [the longest x5 17.5 us: exchange(): lax.ppermute(to_left, every, left)]
  transfers between devices with their start and end apart: 22 -> 22, of which waited for: 14 -> 15; matrix products, arithmetic and copies ran while one was open for 1% -> 1% of each run, Pallas kernels for 14% -> 15%
where the time goes in v4:
time: 90.1 us; the launch traced here: 89.7 us
  starting transfers between devices  49.7 us (55%)
  waiting for transfers between devices  20.3 us (23%)
  Pallas kernels  16.5 us (18%)
  local copies, waits for them, and re-layouts  2.25 us (2%)
    ppermute x12, starting transfers between devices, swapped(): return lax.ppermute(value, axis, [(i, i ^ distance) for i in range(count)])  29.6 us
    ppermute x5, starting transfers between devices, exchange(): lax.ppermute(to_left, every, left)  17.5 us
    ppermute x12, waiting for transfers between devices, swapped(): return lax.ppermute(value, axis, [(i, i ^ distance) for i in range(count)])  14.7 us
    pallas_call x11, Pallas kernels, in_vmem(): pl.pallas_call(kernel, out_shape=[pltpu.VMEM(s, d) for s, d in outs], in_...  10.4 us
    pallas_call x1, Pallas kernels, build_band(): pl.pallas_call(band_kernel, out_shape=pltpu.VMEM((block_rows * B, width),...  5.71 us
    ppermute x5, waiting for transfers between devices, exchange(): lax.ppermute(to_right, every, right)  2.86 us
    ppermute x5, waiting for transfers between devices, exchange(): lax.ppermute(to_left, every, left)  2.76 us
    ppermute x5, starting transfers between devices, exchange(): lax.ppermute(to_right, every, right)  2.67 us
  transfers between devices with their start and end apart: 22, of which 15 were waited for; matrix products, arithmetic and copies ran while one was open for 1% of the time, Pallas kernels for 15%

profile of v4, /device:TPU:32, one launch (start us, length us, event | category | flops | bytes accessed | tf_op | source)
XLA Modules:
  0.0 89.7 jit_solution(11339484248151746949)
XLA Ops:
  0.6 2.0 %collective-permute-start.1 = (bf16[64,1280]{1,0:T(8,128)(2,1)}, bf16[64,1280]{1,0:T(8,128)(2,1)S(1)}, u32[]{:S(2)}, u32[]{:S(2)}) collective-permute-start(bf16[64,1280]{1,0:T(8,128)(2,1)} %bitcast.4), channel_id=1, source_target_pairs={{2,4},{4,2},{6,8},{8,6},{10,12},{12,10},{14,16},{16,14},{18,20},{2... | collective-permute-start | bytes 491528 | tf_op jit(solution)/shard_map/ppermute | solution.py:228
  2.6 0.9 %copy-done = bf16[1280,64]{0,1:T(8,128)(2,1)S(1)} copy-done((bf16[1280,64]{0,1:T(8,128)(2,1)S(1)}, bf16[1280,64]{0,1:T(8,128)(2,1)}, u32[]{:S(2)}) %copy-start) | copy-done | bytes 163864
  3.6 0.1 collective-permute-start
  3.7 5.7 %band.1.a_ref = bf16[1280,3456]{1,0:T(8,128)(2,1)S(1)} custom-call(s32[1,10]{1,0:T(1,128)} %bitcast.8, s32[10,32]{1,0:T(8,128)} %near_ref.1, bf16[10,32,128,128]{3,2,1,0:T(8,128)(2,1)} %h_ref.1), custom_call_target="tpu_custom_call" | custom-call | tf_op jit(solution)/shard_map/band/pallas_call | solution.py:89
  9.5 1.5 %near1.1.acc_ref = f32[64,1280]{1,0:T(8,128)S(1)} custom-call(bf16[64,1280]{1,0:T(8,128)(2,1)S(1)} %bitcast.6, bf16[64,1024]{1,0:T(8,128)(2,1)S(1)} %collective-permute-done.right_ref, bf16[1280,3456]{1,0:T(8,128)(2,1)S(1)} %band.1.a_ref), custom_call_target="tpu_custom_call" | custom-call | flops 314572800 | tf_op jit(solution)/shard_map/near1/pallas_call | solution.py:194
  11.0 0.6 level1.1
  11.6 2.1 %collective-permute-start.2 = (bf16[64,1024]{1,0:T(8,128)(2,1)S(1)}, bf16[64,1024]{1,0:T(8,128)(2,1)S(1)}, u32[]{:S(2)}, u32[]{:S(2)}) collective-permute-start(bf16[64,1024]{1,0:T(8,128)(2,1)S(1)} %get-tuple-element.18), channel_id=1, source_target_pairs={{0,2},{2,0},{4,6},{6,4},{8,10},{10,8},{12,14},{14,12},{16,18},{18,... | collective-permute-start | bytes 393224 | tf_op jit(solution)/shard_map/ppermute | solution.py:228
  13.6 3.3 %collective-permute-start.3 = (bf16[64,1024]{1,0:T(8,128)(2,1)S(1)}, bf16[64,1024]{1,0:T(8,128)(2,1)S(1)}, u32[]{:S(2)}, u32[]{:S(2)}) collective-permute-start(bf16[64,1024]{1,0:T(8,128)(2,1)S(1)} %get-tuple-element.19), channel_id=1, source_target_pairs={{2,4},{4,2},{6,8},{8,6},{10,12},{12,10},{14,16},{16,14},{18,20},{2... | collective-permute-start | bytes 393224 | tf_op jit(solution)/shard_map/ppermute | solution.py:228
  17.0 0.2 collective-permute-done.2.right_ref
  17.2 1.5 %near2.1.acc_ref = f32[64,1280]{1,0:T(8,128)S(1)} custom-call(bf16[64,1280]{1,0:T(8,128)(2,1)S(1)} %get-tuple-element.17.v_ref.older_ref, bf16[64,1024]{1,0:T(8,128)(2,1)S(1)} %collective-permute-done.2.right_ref, bf16[1280,3456]{1,0:T(8,128)(2,1)S(1)} %band.1.a_ref), custom_call_target="tpu_custom_call" | custom-call | flops 314572800 | tf_op jit(solution)/shard_map/near2/pallas_call | solution.py:194
  18.7 1.2 %collective-permute-done.3.left_ref = bf16[64,1024]{1,0:T(8,128)(2,1)S(1)} collective-permute-done((bf16[64,1024]{1,0:T(8,128)(2,1)S(1)}, bf16[64,1024]{1,0:T(8,128)(2,1)S(1)}, u32[]{:S(2)}, u32[]{:S(2)}) %collective-permute-start.3) | collective-permute-done | bytes 131104 | tf_op jit(solution)/shard_map/ppermute | solution.py:228
  19.9 0.6 level2.1
  20.5 0.3 collective-permute-start.4
  20.8 4.9 %collective-permute-start.5 = (bf16[64,1024]{1,0:T(8,128)(2,1)S(1)}, bf16[64,1024]{1,0:T(8,128)(2,1)S(1)}, u32[]{:S(2)}, u32[]{:S(2)}) collective-permute-start(bf16[64,1024]{1,0:T(8,128)(2,1)S(1)} %get-tuple-element.22), channel_id=1, source_target_pairs={{2,4},{4,2},{6,8},{8,6},{10,12},{12,10},{14,16},{16,14},{18,20},{2... | collective-permute-start | bytes 393224 | tf_op jit(solution)/shard_map/ppermute | solution.py:228
  25.7 1.5 %near3.1.acc_ref = f32[64,1280]{1,0:T(8,128)S(1)} custom-call(bf16[64,1280]{1,0:T(8,128)(2,1)S(1)} %get-tuple-element.20.v_ref.older_ref, bf16[64,1024]{1,0:T(8,128)(2,1)S(1)} %collective-permute-done.4.right_ref, bf16[1280,3456]{1,0:T(8,128)(2,1)S(1)} %band.1.a_ref), custom_call_target="tpu_custom_call" | custom-call | flops 314572800 | tf_op jit(solution)/shard_map/near3/pallas_call | solution.py:194
  27.2 1.4 %collective-permute-done.5.left_ref = bf16[64,1024]{1,0:T(8,128)(2,1)S(1)} collective-permute-done((bf16[64,1024]{1,0:T(8,128)(2,1)S(1)}, bf16[64,1024]{1,0:T(8,128)(2,1)S(1)}, u32[]{:S(2)}, u32[]{:S(2)}) %collective-permute-start.5) | collective-permute-done | bytes 131104 | tf_op jit(solution)/shard_map/ppermute | solution.py:228
  28.6 0.6 level3.1
  29.2 0.1 collective-permute-start.6
  29.3 3.6 %collective-permute-start.7 = (bf16[64,1024]{1,0:T(8,128)(2,1)S(1)}, bf16[64,1024]{1,0:T(8,128)(2,1)S(1)}, u32[]{:S(2)}, u32[]{:S(2)}) collective-permute-start(bf16[64,1024]{1,0:T(8,128)(2,1)S(1)} %get-tuple-element.25), channel_id=1, source_target_pairs={{2,4},{4,2},{6,8},{8,6},{10,12},{12,10},{14,16},{16,14},{18,20},{2... | collective-permute-start | bytes 393224 | tf_op jit(solution)/shard_map/ppermute | solution.py:228
  32.9 1.4 %collective-permute-done.6.right_ref = bf16[64,1024]{1,0:T(8,128)(2,1)S(1)} collective-permute-done((bf16[64,1024]{1,0:T(8,128)(2,1)S(1)}, bf16[64,1024]{1,0:T(8,128)(2,1)S(1)}, u32[]{:S(2)}, u32[]{:S(2)}) %collective-permute-start.6) | collective-permute-done | bytes 131104 | tf_op jit(solution)/shard_map/ppermute | solution.py:228
  34.3 1.5 %near4.1.acc_ref = f32[64,1280]{1,0:T(8,128)S(1)} custom-call(bf16[64,1280]{1,0:T(8,128)(2,1)S(1)} %get-tuple-element.23.v_ref, bf16[64,1024]{1,0:T(8,128)(2,1)S(1)} %collective-permute-done.6.right_ref, bf16[1280,3456]{1,0:T(8,128)(2,1)S(1)} %band.1.a_ref), custom_call_target="tpu_custom_call" | custom-call | flops 314572800 | tf_op jit(solution)/shard_map/near4/pallas_call | solution.py:194
  35.8 0.6 level4.1
  36.5 3.7 %collective-permute-start.10 = (bf16[64,1024]{1,0:T(8,128)(2,1)S(1)}, bf16[64,1024]{1,0:T(8,128)(2,1)S(1)}, u32[]{:S(2)}, u32[]{:S(2)}) collective-permute-start(bf16[64,1024]{1,0:T(8,128)(2,1)S(1)} %get-tuple-element.30), channel_id=1, source_target_pairs={{2,4},{4,2},{6,8},{8,6},{10,12},{12,10},{14,16},{16,14},{18,20},{2... | collective-permute-start | bytes 393224 | tf_op jit(solution)/shard_map/ppermute | solution.py:228
  40.2 1.3 %collective-permute-done.8.right_ref = bf16[64,1024]{1,0:T(8,128)(2,1)S(1)} collective-permute-done((bf16[64,1024]{1,0:T(8,128)(2,1)S(1)}, bf16[64,1024]{1,0:T(8,128)(2,1)S(1)}, u32[]{:S(2)}, u32[]{:S(2)}) %collective-permute-start.8) | collective-permute-done | bytes 131104 | tf_op jit(solution)/shard_map/ppermute | solution.py:228
  41.4 1.5 %near5.1.acc_ref = f32[64,1280]{1,0:T(8,128)S(1)} custom-call(bf16[64,1280]{1,0:T(8,128)(2,1)S(1)} %get-tuple-element.28.v_ref.own_ref, bf16[64,1024]{1,0:T(8,128)(2,1)S(1)} %collective-permute-done.8.right_ref, bf16[1280,3456]{1,0:T(8,128)(2,1)S(1)} %band.1.a_ref), custom_call_target="tpu_custom_call" | custom-call | flops 314572800 | tf_op jit(solution)/shard_map/near5/pallas_call | solution.py:194
  43.1 0.5 image.1.image_ref
  43.6 0.5 collective-permute-start.11
  44.1 0.3 collective-permute-done.9.other_ref
  44.4 0.8 collective-permute-done.11.other_image_ref
  45.2 0.4 gram.1
  45.6 2.1 %collective-permute-start.14 = (bf16[128,128]{1,0:T(8,128)(2,1)S(1)}, bf16[128,128]{1,0:T(8,128)(2,1)S(1)}, u32[]{:S(2)}, u32[]{:S(2)}) collective-permute-start(bf16[128,128]{1,0:T(8,128)(2,1)S(1)} %reduce-precision_convert_fusion), channel_id=1, source_target_pairs={{0,6},{2,4},{4,2},{6,0},{8,14},{10,12},{12,10},{14,8},{1,7},{3,5},... | collective-permute-start | bytes 98312 | tf_op jit(solution)/shard_map/ppermute | solution.py:233
  47.7 1.2 %collective-permute-start.13 = (bf16[128,128]{1,0:T(8,128)(2,1)S(1)}, bf16[128,128]{1,0:T(8,128)(2,1)S(1)}, u32[]{:S(2)}, u32[]{:S(2)}) collective-permute-start(bf16[128,128]{1,0:T(8,128)(2,1)S(1)} %reduce-precision_convert_fusion), channel_id=1, source_target_pairs={{0,4},{2,6},{4,0},{6,2},{8,12},{10,14},{12,8},{14,10},{1,5},{3,7},... | collective-permute-start | bytes 98312 | tf_op jit(solution)/shard_map/ppermute | solution.py:233
  48.9 1.4 %collective-permute-start.12 = (bf16[128,128]{1,0:T(8,128)(2,1)S(1)}, bf16[128,128]{1,0:T(8,128)(2,1)S(1)}, u32[]{:S(2)}, u32[]{:S(2)}) collective-permute-start(bf16[128,128]{1,0:T(8,128)(2,1)S(1)} %reduce-precision_convert_fusion), channel_id=1, source_target_pairs={{0,2},{2,0},{4,6},{6,4},{8,10},{10,8},{12,14},{14,12},{1,3},{3,1},... | collective-permute-start | bytes 98312 | tf_op jit(solution)/shard_map/ppermute | solution.py:233
  50.3 2.2 %collective-permute-done.13 = bf16[128,128]{1,0:T(8,128)(2,1)S(1)} collective-permute-done((bf16[128,128]{1,0:T(8,128)(2,1)S(1)}, bf16[128,128]{1,0:T(8,128)(2,1)S(1)}, u32[]{:S(2)}, u32[]{:S(2)}) %collective-permute-start.13) | collective-permute-done | bytes 32800 | tf_op jit(solution)/shard_map/ppermute | solution.py:233
  52.5 0.8 collective-permute-done.12
  53.3 3.7 %collective-permute-start.15 = (bf16[128,128]{1,0:T(8,128)(2,1)S(1)}, bf16[128,128]{1,0:T(8,128)(2,1)S(1)}, u32[]{:S(2)}, u32[]{:S(2)}) collective-permute-start(bf16[128,128]{1,0:T(8,128)(2,1)S(1)} %get-tuple-element.31), channel_id=1, source_target_pairs={{0,12},{2,14},{4,8},{6,10},{8,4},{10,6},{12,0},{14,2},{1,13},{3,15... | collective-permute-start | bytes 98312 | tf_op jit(solution)/shard_map/ppermute | solution.py:233
  57.0 2.4 %collective-permute-done.15 = bf16[128,128]{1,0:T(8,128)(2,1)S(1)} collective-permute-done((bf16[128,128]{1,0:T(8,128)(2,1)S(1)}, bf16[128,128]{1,0:T(8,128)(2,1)S(1)}, u32[]{:S(2)}, u32[]{:S(2)}) %collective-permute-start.15) | collective-permute-done | bytes 32800 | tf_op jit(solution)/shard_map/ppermute | solution.py:233
  59.4 10.9 %collective-permute-start.18 = (bf16[128,128]{1,0:T(8,128)(2,1)S(1)}, bf16[128,128]{1,0:T(8,128)(2,1)S(1)}, u32[]{:S(2)}, u32[]{:S(2)}) collective-permute-start(bf16[128,128]{1,0:T(8,128)(2,1)S(1)} %fusion), channel_id=1, source_target_pairs={{0,48},{16,32},{32,16},{48,0},{1,49},{17,33},{33,17},{49,1},{2,50}... | collective-permute-start | bytes 98312 | tf_op jit(solution)/shard_map/ppermute | solution.py:233
  70.3 1.0 %collective-permute-start.16 = (bf16[128,128]{1,0:T(8,128)(2,1)S(1)}, bf16[128,128]{1,0:T(8,128)(2,1)S(1)}, u32[]{:S(2)}, u32[]{:S(2)}) collective-permute-start(bf16[128,128]{1,0:T(8,128)(2,1)S(1)} %fusion), channel_id=1, source_target_pairs={{0,16},{16,0},{32,48},{48,32},{1,17},{17,1},{33,49},{49,33},{2,18}... | collective-permute-start | bytes 98312 | tf_op jit(solution)/shard_map/ppermute | solution.py:233
  71.3 0.9 %collective-permute-done.18 = bf16[128,128]{1,0:T(8,128)(2,1)S(1)} collective-permute-done((bf16[128,128]{1,0:T(8,128)(2,1)S(1)}, bf16[128,128]{1,0:T(8,128)(2,1)S(1)}, u32[]{:S(2)}, u32[]{:S(2)}) %collective-permute-start.18) | collective-permute-done | bytes 32800 | tf_op jit(solution)/shard_map/ppermute | solution.py:233
  72.2 3.5 %collective-permute-done.17 = bf16[128,128]{1,0:T(8,128)(2,1)S(1)} collective-permute-done((bf16[128,128]{1,0:T(8,128)(2,1)S(1)}, bf16[128,128]{1,0:T(8,128)(2,1)S(1)}, u32[]{:S(2)}, u32[]{:S(2)}) %collective-permute-start.17) | collective-permute-done | bytes 32800 | tf_op jit(solution)/shard_map/ppermute | solution.py:233
  75.8 7.8 %collective-permute-start.21 = (bf16[128,128]{1,0:T(8,128)(2,1)S(1)}, bf16[128,128]{1,0:T(8,128)(2,1)S(1)}, u32[]{:S(2)}, u32[]{:S(2)}) collective-permute-start(bf16[128,128]{1,0:T(8,128)(2,1)S(1)} %fusion.1), channel_id=1, source_target_pairs={{0,192},{64,128},{128,64},{192,0},{1,193},{65,129},{129,65},{193,1... | collective-permute-start | bytes 98312 | tf_op jit(solution)/shard_map/ppermute | solution.py:233
  83.6 0.8 collective-permute-start.20
  84.3 0.2 collective-permute-start.19
  84.5 0.7 copy.7
  85.2 0.3 collective-permute-done.21
  85.5 3.5 %collective-permute-done.20 = bf16[128,128]{1,0:T(8,128)(2,1)S(1)} collective-permute-done((bf16[128,128]{1,0:T(8,128)(2,1)S(1)}, bf16[128,128]{1,0:T(8,128)(2,1)S(1)}, u32[]{:S(2)}, u32[]{:S(2)}) %collective-permute-start.20) | collective-permute-done | bytes 32800 | tf_op jit(solution)/shard_map/ppermute | solution.py:233
  89.0 0.6 fusion.3
  (20 shorter events, 0.4 us)
Async XLA Ops:
  0.6 10.4 %collective-permute-start.1 = (bf16[64,1280]{1,0:T(8,128)(2,1)}, bf16[64,1280]{1,0:T(8,128)(2,1)S(1)}, u32[]{:S(2)}, u32[]{:S(2)}) collective-permute-start(bf16[64,1280]{1,0:T(8,128)(2,1)} %bitcast.4), channel_id=1, source_target_pairs={{2,4},{4,2},{6,8},{8,6},{10,12},{12,10},{14,16},{16,14},{18,20},{2... | collective-permute-start | bytes 491528 | tf_op jit(solution)/shard_map/ppermute | solution.py:228
  2.6 0.9 %copy-start = (bf16[1280,64]{0,1:T(8,128)(2,1)S(1)}, bf16[1280,64]{0,1:T(8,128)(2,1)}, u32[]{:S(2)}) copy-start(bf16[1280,64]{0,1:T(8,128)(2,1)} %param.7) | copy-start | bytes 491524
  3.6 5.9 %copy-start.1 = (bf16[1280,64]{0,1:T(8,128)(2,1)S(1)}, bf16[1280,64]{0,1:T(8,128)(2,1)}, u32[]{:S(2)}) copy-start(bf16[1280,64]{0,1:T(8,128)(2,1)} %param.7) | copy-start | bytes 491524
  3.6 5.8 %collective-permute-start = (bf16[64,1024]{1,0:T(8,128)(2,1)S(1)}, bf16[64,1024]{1,0:T(8,128)(2,1)S(1)}, u32[]{:S(2)}, u32[]{:S(2)}) collective-permute-start(bf16[64,1024]{1,0:T(8,128)(2,1)S(1)} %edge.1), channel_id=1, source_target_pairs={{0,2},{2,0},{4,6},{6,4},{8,10},{10,8},{12,14},{14,12},{16,18},{18,... | collective-permute-start | bytes 393224 | tf_op jit(solution)/shard_map/ppermute | solution.py:228
  11.6 5.6 %collective-permute-start.2 = (bf16[64,1024]{1,0:T(8,128)(2,1)S(1)}, bf16[64,1024]{1,0:T(8,128)(2,1)S(1)}, u32[]{:S(2)}, u32[]{:S(2)}) collective-permute-start(bf16[64,1024]{1,0:T(8,128)(2,1)S(1)} %get-tuple-element.18), channel_id=1, source_target_pairs={{0,2},{2,0},{4,6},{6,4},{8,10},{10,8},{12,14},{14,12},{16,18},{18,... | collective-permute-start | bytes 393224 | tf_op jit(solution)/shard_map/ppermute | solution.py:228
  13.6 6.3 %collective-permute-start.3 = (bf16[64,1024]{1,0:T(8,128)(2,1)S(1)}, bf16[64,1024]{1,0:T(8,128)(2,1)S(1)}, u32[]{:S(2)}, u32[]{:S(2)}) collective-permute-start(bf16[64,1024]{1,0:T(8,128)(2,1)S(1)} %get-tuple-element.19), channel_id=1, source_target_pairs={{2,4},{4,2},{6,8},{8,6},{10,12},{12,10},{14,16},{16,14},{18,20},{2... | collective-permute-start | bytes 393224 | tf_op jit(solution)/shard_map/ppermute | solution.py:228
  20.5 5.2 %collective-permute-start.4 = (bf16[64,1024]{1,0:T(8,128)(2,1)S(1)}, bf16[64,1024]{1,0:T(8,128)(2,1)S(1)}, u32[]{:S(2)}, u32[]{:S(2)}) collective-permute-start(bf16[64,1024]{1,0:T(8,128)(2,1)S(1)} %get-tuple-element.21), channel_id=1, source_target_pairs={{0,2},{2,0},{4,6},{6,4},{8,10},{10,8},{12,14},{14,12},{16,18},{18,... | collective-permute-start | bytes 393224 | tf_op jit(solution)/shard_map/ppermute | solution.py:228
  20.8 7.8 %collective-permute-start.5 = (bf16[64,1024]{1,0:T(8,128)(2,1)S(1)}, bf16[64,1024]{1,0:T(8,128)(2,1)S(1)}, u32[]{:S(2)}, u32[]{:S(2)}) collective-permute-start(bf16[64,1024]{1,0:T(8,128)(2,1)S(1)} %get-tuple-element.22), channel_id=1, source_target_pairs={{2,4},{4,2},{6,8},{8,6},{10,12},{12,10},{14,16},{16,14},{18,20},{2... | collective-permute-start | bytes 393224 | tf_op jit(solution)/shard_map/ppermute | solution.py:228
  29.2 5.1 %collective-permute-start.6 = (bf16[64,1024]{1,0:T(8,128)(2,1)S(1)}, bf16[64,1024]{1,0:T(8,128)(2,1)S(1)}, u32[]{:S(2)}, u32[]{:S(2)}) collective-permute-start(bf16[64,1024]{1,0:T(8,128)(2,1)S(1)} %get-tuple-element.24), channel_id=1, source_target_pairs={{0,2},{2,0},{4,6},{6,4},{8,10},{10,8},{12,14},{14,12},{16,18},{18,... | collective-permute-start | bytes 393224 | tf_op jit(solution)/shard_map/ppermute | solution.py:228
  29.3 6.5 %collective-permute-start.7 = (bf16[64,1024]{1,0:T(8,128)(2,1)S(1)}, bf16[64,1024]{1,0:T(8,128)(2,1)S(1)}, u32[]{:S(2)}, u32[]{:S(2)}) collective-permute-start(bf16[64,1024]{1,0:T(8,128)(2,1)S(1)} %get-tuple-element.25), channel_id=1, source_target_pairs={{2,4},{4,2},{6,8},{8,6},{10,12},{12,10},{14,16},{16,14},{18,20},{2... | collective-permute-start | bytes 393224 | tf_op jit(solution)/shard_map/ppermute | solution.py:228
  36.4 5.1 %collective-permute-start.8 = (bf16[64,1024]{1,0:T(8,128)(2,1)S(1)}, bf16[64,1024]{1,0:T(8,128)(2,1)S(1)}, u32[]{:S(2)}, u32[]{:S(2)}) collective-permute-start(bf16[64,1024]{1,0:T(8,128)(2,1)S(1)} %get-tuple-element.27), channel_id=1, source_target_pairs={{0,2},{2,0},{4,6},{6,4},{8,10},{10,8},{12,14},{14,12},{16,18},{18,... | collective-permute-start | bytes 393224 | tf_op jit(solution)/shard_map/ppermute | solution.py:228
  36.5 6.6 %collective-permute-start.10 = (bf16[64,1024]{1,0:T(8,128)(2,1)S(1)}, bf16[64,1024]{1,0:T(8,128)(2,1)S(1)}, u32[]{:S(2)}, u32[]{:S(2)}) collective-permute-start(bf16[64,1024]{1,0:T(8,128)(2,1)S(1)} %get-tuple-element.30), channel_id=1, source_target_pairs={{2,4},{4,2},{6,8},{8,6},{10,12},{12,10},{14,16},{16,14},{18,20},{2... | collective-permute-start | bytes 393224 | tf_op jit(solution)/shard_map/ppermute | solution.py:228
  43.0 1.4 %collective-permute-start.9 = (bf16[64,1280]{1,0:T(8,128)(2,1)S(1)}, bf16[64,1280]{1,0:T(8,128)(2,1)S(1)}, u32[]{:S(2)}, u32[]{:S(2)}) collective-permute-start(bf16[64,1280]{1,0:T(8,128)(2,1)S(1)} %get-tuple-element.28.v_ref.own_ref), channel_id=1, source_target_pairs={{0,1},{1,0},{2,3},{3,2},{4,5},{5,4},{6,7},{7,6},{8,9},{9,8},{10,11... | collective-permute-start | bytes 491528 | tf_op jit(solution)/shard_map/ppermute | solution.py:233
  43.6 1.5 %collective-permute-start.11 = (bf16[64,1280]{1,0:T(8,128)(2,1)S(1)}, bf16[64,1280]{1,0:T(8,128)(2,1)S(1)}, u32[]{:S(2)}, u32[]{:S(2)}) collective-permute-start(bf16[64,1280]{1,0:T(8,128)(2,1)S(1)} %image.1.image_ref), channel_id=1, source_target_pairs={{0,1},{1,0},{2,3},{3,2},{4,5},{5,4},{6,7},{7,6},{8,9},{9,8},{10,11... | collective-permute-start | bytes 491528 | tf_op jit(solution)/shard_map/ppermute | solution.py:233
  45.6 4.7 %collective-permute-start.14 = (bf16[128,128]{1,0:T(8,128)(2,1)S(1)}, bf16[128,128]{1,0:T(8,128)(2,1)S(1)}, u32[]{:S(2)}, u32[]{:S(2)}) collective-permute-start(bf16[128,128]{1,0:T(8,128)(2,1)S(1)} %reduce-precision_convert_fusion), channel_id=1, source_target_pairs={{0,6},{2,4},{4,2},{6,0},{8,14},{10,12},{12,10},{14,8},{1,7},{3,5},... | collective-permute-start | bytes 98312 | tf_op jit(solution)/shard_map/ppermute | solution.py:233
  47.7 4.8 %collective-permute-start.13 = (bf16[128,128]{1,0:T(8,128)(2,1)S(1)}, bf16[128,128]{1,0:T(8,128)(2,1)S(1)}, u32[]{:S(2)}, u32[]{:S(2)}) collective-permute-start(bf16[128,128]{1,0:T(8,128)(2,1)S(1)} %reduce-precision_convert_fusion), channel_id=1, source_target_pairs={{0,4},{2,6},{4,0},{6,2},{8,12},{10,14},{12,8},{14,10},{1,5},{3,7},... | collective-permute-start | bytes 98312 | tf_op jit(solution)/shard_map/ppermute | solution.py:233
  48.9 4.4 %collective-permute-start.12 = (bf16[128,128]{1,0:T(8,128)(2,1)S(1)}, bf16[128,128]{1,0:T(8,128)(2,1)S(1)}, u32[]{:S(2)}, u32[]{:S(2)}) collective-permute-start(bf16[128,128]{1,0:T(8,128)(2,1)S(1)} %reduce-precision_convert_fusion), channel_id=1, source_target_pairs={{0,2},{2,0},{4,6},{6,4},{8,10},{10,8},{12,14},{14,12},{1,3},{3,1},... | collective-permute-start | bytes 98312 | tf_op jit(solution)/shard_map/ppermute | solution.py:233
  53.3 6.1 %collective-permute-start.15 = (bf16[128,128]{1,0:T(8,128)(2,1)S(1)}, bf16[128,128]{1,0:T(8,128)(2,1)S(1)}, u32[]{:S(2)}, u32[]{:S(2)}) collective-permute-start(bf16[128,128]{1,0:T(8,128)(2,1)S(1)} %get-tuple-element.31), channel_id=1, source_target_pairs={{0,12},{2,14},{4,8},{6,10},{8,4},{10,6},{12,0},{14,2},{1,13},{3,15... | collective-permute-start | bytes 98312 | tf_op jit(solution)/shard_map/ppermute | solution.py:233
  59.4 12.8 %collective-permute-start.18 = (bf16[128,128]{1,0:T(8,128)(2,1)S(1)}, bf16[128,128]{1,0:T(8,128)(2,1)S(1)}, u32[]{:S(2)}, u32[]{:S(2)}) collective-permute-start(bf16[128,128]{1,0:T(8,128)(2,1)S(1)} %fusion), channel_id=1, source_target_pairs={{0,48},{16,32},{32,16},{48,0},{1,49},{17,33},{33,17},{49,1},{2,50}... | collective-permute-start | bytes 98312 | tf_op jit(solution)/shard_map/ppermute | solution.py:233
  70.3 5.4 %collective-permute-start.17 = (bf16[128,128]{1,0:T(8,128)(2,1)S(1)}, bf16[128,128]{1,0:T(8,128)(2,1)S(1)}, u32[]{:S(2)}, u32[]{:S(2)}) collective-permute-start(bf16[128,128]{1,0:T(8,128)(2,1)S(1)} %fusion), channel_id=1, source_target_pairs={{0,32},{16,48},{32,0},{48,16},{1,33},{17,49},{33,1},{49,17},{2,34}... | collective-permute-start | bytes 98312 | tf_op jit(solution)/shard_map/ppermute | solution.py:233
  70.3 5.4 %collective-permute-start.16 = (bf16[128,128]{1,0:T(8,128)(2,1)S(1)}, bf16[128,128]{1,0:T(8,128)(2,1)S(1)}, u32[]{:S(2)}, u32[]{:S(2)}) collective-permute-start(bf16[128,128]{1,0:T(8,128)(2,1)S(1)} %fusion), channel_id=1, source_target_pairs={{0,16},{16,0},{32,48},{48,32},{1,17},{17,1},{33,49},{49,33},{2,18}... | collective-permute-start | bytes 98312 | tf_op jit(solution)/shard_map/ppermute | solution.py:233
  75.8 9.7 %collective-permute-start.21 = (bf16[128,128]{1,0:T(8,128)(2,1)S(1)}, bf16[128,128]{1,0:T(8,128)(2,1)S(1)}, u32[]{:S(2)}, u32[]{:S(2)}) collective-permute-start(bf16[128,128]{1,0:T(8,128)(2,1)S(1)} %fusion.1), channel_id=1, source_target_pairs={{0,192},{64,128},{128,64},{192,0},{1,193},{65,129},{129,65},{193,1... | collective-permute-start | bytes 98312 | tf_op jit(solution)/shard_map/ppermute | solution.py:233
  83.6 5.4 %collective-permute-start.20 = (bf16[128,128]{1,0:T(8,128)(2,1)S(1)}, bf16[128,128]{1,0:T(8,128)(2,1)S(1)}, u32[]{:S(2)}, u32[]{:S(2)}) collective-permute-start(bf16[128,128]{1,0:T(8,128)(2,1)S(1)} %fusion.1), channel_id=1, source_target_pairs={{0,128},{64,192},{128,0},{192,64},{1,129},{65,193},{129,1},{193,65... | collective-permute-start | bytes 98312 | tf_op jit(solution)/shard_map/ppermute | solution.py:233
  84.3 4.7 %collective-permute-start.19 = (bf16[128,128]{1,0:T(8,128)(2,1)S(1)}, bf16[128,128]{1,0:T(8,128)(2,1)S(1)}, u32[]{:S(2)}, u32[]{:S(2)}) collective-permute-start(bf16[128,128]{1,0:T(8,128)(2,1)S(1)} %fusion.1), channel_id=1, source_target_pairs={{0,64},{64,0},{128,192},{192,128},{1,65},{65,1},{129,193},{193,129... | collective-permute-start | bytes 98312 | tf_op jit(solution)/shard_map/ppermute | solution.py:233

commit v5 on v4

--- a/solution.py
+++ b/solution.py
@@ -121,19 +121,23 @@
     return dot_nt(high[:, :depth], a_ref[i : i + step, upper : upper + depth])
 
 
+def halo_sides(ref):
+    return ref[:, ref.shape[1] - DIST * B :], ref[:, : DIST * B]
+
+
 def near_kernel(v_ref, right_ref, a_ref, acc_ref):
     rows = acc_ref.shape[1]
     step = 2 * B
     v = v_ref[...]
 
-    def run(part):
-        halo = right_ref[...]
+    def run(halo, part):
         for i in range(0, rows, step):
             own = dot_nt(v, a_ref[i : i + step, DIST * B : DIST * B + rows])
             acc_ref[:, i : i + step] = own + part(halo, a_ref, i, step)
 
-    pl.when(on_even_chip())(lambda: run(high_part))
-    pl.when(jnp.logical_not(on_even_chip()))(lambda: run(low_part))
+    low, high = halo_sides(right_ref)
+    pl.when(on_even_chip())(lambda: run(high, high_part))
+    pl.when(jnp.logical_not(on_even_chip()))(lambda: run(low, low_part))
 
 
 def finish(acc_ref, left_ref, a_ref, new_ref, older_ref=None):
@@ -147,9 +151,7 @@
                 total = 2.0 * total - older_ref[:, i : i + step].astype(jnp.float32)
             new_ref[:, i : i + step] = total.astype(new_ref.dtype)
 
-    reach = DIST * B
-    low = left_ref[:, left_ref.shape[1] - reach :]
-    high = left_ref[:, :reach]
+    low, high = halo_sides(left_ref)
     pl.when(on_even_chip())(lambda: run(low, low_part))
     pl.when(jnp.logical_not(on_even_chip()))(lambda: run(high, high_part))
 
@@ -167,12 +169,7 @@
     top = new_ref[:, new_ref.shape[1] - reach :]
     bottom = new_ref[:, :reach]
     to_right_ref[...] = jnp.where(on_even_chip(), top, bottom)
-    if to_left_ref is not None:
-        to_left_ref[...] = jnp.where(on_even_chip(), bottom, top)
-
-
-def edge_kernel(new_ref, to_right_ref):
-    depart(new_ref, to_right_ref, None)
+    to_left_ref[...] = jnp.where(on_even_chip(), bottom, top)
 
 
 def first_kernel(acc_ref, left_ref, a_ref, new_ref, to_right_ref, to_left_ref):
@@ -228,16 +225,19 @@
     return lax.ppermute(to_right, every, right), lax.ppermute(to_left, every, left)
 
 
-def swapped(value, axis, distance):
-    count = lax.axis_size(axis)
-    return lax.ppermute(value, axis, [(i, i ^ distance) for i in range(count)])
+def from_other_core(value):
+    return lax.ppermute(value, "band", [(0, 1), (1, 0)])
 
 
 def sum_over_rows(value):
-    for axis, distances in (("z", (1, 2, 3)), ("z", (6,)), ("y", (1, 2, 3)), ("x", (1, 2, 3))):
+    count = lax.axis_size(ROWS)
+    for distances in ((1, 2, 3), (6, 8, 14), (24, 32, 56), (96,)):
         own = lax.reduce_precision(value, exponent_bits=8, mantissa_bits=7)
         sent = own.astype(jnp.bfloat16)
-        others = [swapped(sent, axis, k).astype(jnp.float32) for k in distances]
+        others = [
+            lax.ppermute(sent, ROWS, [(i, i ^ d) for i in range(count)]).astype(jnp.float32)
+            for d in distances
+        ]
         value = own + others[0]
         if len(others) == 3:
             value = value + (others[1] + others[2])
@@ -257,7 +257,7 @@
         return in_vmem(near_kernel, name, [part], v, right, band, flops=near_flops)[0]
 
     start = vectors.T
-    right, left = exchange(*in_vmem(edge_kernel, "edge", [halo], start), start)
+    right, left = exchange(start, start)
     band = build_band(neighbours, counts, hamiltonian)
     acc = near(start, right, "near1")
     level1, *edges = in_vmem(first_kernel, "level1", [field, halo, halo], acc, left, band)
@@ -271,9 +271,9 @@
         older, newer = newer, latest
     right, left = exchange(*edges)
     acc, mine = lax.optimization_barrier((near(newer, right, "near5"), newer))
-    other = swapped(mine, "band", 1)
+    other = from_other_core(mine)
     (image,) = in_vmem(image_kernel, "image", [field], acc, left, band)
-    other_image = swapped(image, "band", 1)
+    other_image = from_other_core(image)
     sums = pl.pallas_call(
         gram_kernel,
         out_shape=jax.ShapeDtypeStruct((2 * width, 2 * width), jnp.float32),

time: 90.1 us -> 90 us (level)
  local copies, waits for them, and re-layouts: 2.25 us -> 1.3 us
    ppermute x5, waiting for transfers between devices: 2.86 us -> 4.25 us  [exchange(): lax.ppermute(to_right, every, right)]
    ppermute x5, waiting for transfers between devices: 2.76 us -> 1.41 us  [exchange(): lax.ppermute(to_left, every, left)]
    unnamed x5 -> x3, local copies, waits for them, and re-layouts: 1.62 us -> 0.67 us
    pallas_call x11 -> x10, Pallas kernels: 10.4 us -> 10.4 us  [in_vmem(): pl.pallas_call(kernel, out_shape=[pltpu.VMEM(s, d) for s, d in outs], in_...]
  transfers between devices with their start and end apart: 22 -> 22, of which waited for: 15 -> 16; matrix products, arithmetic and copies ran while one was open for 1% -> 1% of each run, Pallas kernels for 15% -> 15%
where the time goes in v5:
time: 90 us; the launch traced here: 89.1 us
  starting transfers between devices  49.5 us (55%)
  waiting for transfers between devices  21.2 us (24%)
  Pallas kernels  16.2 us (18%)
  local copies, waits for them, and re-layouts  1.3 us (1%)
    ppermute x10, starting transfers between devices, sum_over_rows(): lax.ppermute(sent, ROWS, [(i, i ^ d) for i in range(count)])  29 us
    ppermute x5, starting transfers between devices, exchange(): lax.ppermute(to_left, every, left)  17.6 us
    ppermute x10, waiting for transfers between devices, sum_over_rows(): lax.ppermute(sent, ROWS, [(i, i ^ d) for i in range(count)])  14.6 us
    pallas_call x10, Pallas kernels, in_vmem(): pl.pallas_call(kernel, out_shape=[pltpu.VMEM(s, d) for s, d in outs], in_...  10.4 us
    pallas_call x1, Pallas kernels, build_band(): pl.pallas_call(band_kernel, out_shape=pltpu.VMEM((block_rows * B, width),...  5.43 us
    ppermute x5, waiting for transfers between devices, exchange(): lax.ppermute(to_right, every, right)  4.25 us
    ppermute x5, starting transfers between devices, exchange(): lax.ppermute(to_right, every, right)  2.3 us
  transfers between devices with their start and end apart: 22, of which 16 were waited for; matrix products, arithmetic and copies ran while one was open for 1% of the time, Pallas kernels for 15%

profile of v5, /device:TPU:32, one launch (start us, length us, event | category | flops | bytes accessed | tf_op | source)
XLA Modules:
  0.0 89.1 jit_solution(1833452417339432549)
XLA Ops:
  0.6 1.9 %collective-permute-start = (bf16[64,1280]{1,0:T(8,128)(2,1)}, bf16[64,1280]{1,0:T(8,128)(2,1)S(1)}, u32[]{:S(2)}, u32[]{:S(2)}) collective-permute-start(bf16[64,1280]{1,0:T(8,128)(2,1)} %bitcast.4), channel_id=1, source_target_pairs={{0,2},{2,0},{4,6},{6,4},{8,10},{10,8},{12,14},{14,12},{16,18},{18,... | collective-permute-start | bytes 491528 | tf_op jit(solution)/shard_map/ppermute | solution.py:225
  2.6 2.0 %collective-permute-start.1 = (bf16[64,1280]{1,0:T(8,128)(2,1)}, bf16[64,1280]{1,0:T(8,128)(2,1)S(1)}, u32[]{:S(2)}, u32[]{:S(2)}) collective-permute-start(bf16[64,1280]{1,0:T(8,128)(2,1)} %bitcast.5), channel_id=1, source_target_pairs={{2,4},{4,2},{6,8},{8,6},{10,12},{12,10},{14,16},{16,14},{18,20},{2... | collective-permute-start | bytes 491528 | tf_op jit(solution)/shard_map/ppermute | solution.py:225
  4.6 5.4 %band.1.a_ref = bf16[1280,3456]{1,0:T(8,128)(2,1)S(1)} custom-call(s32[1,10]{1,0:T(1,128)} %bitcast.8, s32[10,32]{1,0:T(8,128)} %near_ref.1, bf16[10,32,128,128]{3,2,1,0:T(8,128)(2,1)} %h_ref.1), custom_call_target="tpu_custom_call" | custom-call | tf_op jit(solution)/shard_map/band/pallas_call | solution.py:89
  10.0 1.5 %near1.1.acc_ref = f32[64,1280]{1,0:T(8,128)S(1)} custom-call(bf16[64,1280]{1,0:T(8,128)(2,1)S(1)} %bitcast.6, bf16[64,1280]{1,0:T(8,128)(2,1)S(1)} %collective-permute-done.right_ref, bf16[1280,3456]{1,0:T(8,128)(2,1)S(1)} %band.1.a_ref), custom_call_target="tpu_custom_call" | custom-call | flops 314572800 | tf_op jit(solution)/shard_map/near1/pallas_call | solution.py:191
  11.6 0.6 level1.1
  12.2 4.8 %collective-permute-start.3 = (bf16[64,1024]{1,0:T(8,128)(2,1)S(1)}, bf16[64,1024]{1,0:T(8,128)(2,1)S(1)}, u32[]{:S(2)}, u32[]{:S(2)}) collective-permute-start(bf16[64,1024]{1,0:T(8,128)(2,1)S(1)} %get-tuple-element.19), channel_id=1, source_target_pairs={{2,4},{4,2},{6,8},{8,6},{10,12},{12,10},{14,16},{16,14},{18,20},{2... | collective-permute-start | bytes 393224 | tf_op jit(solution)/shard_map/ppermute | solution.py:225
  17.0 0.2 collective-permute-done.2.right_ref
  17.2 1.5 %near2.1.acc_ref = f32[64,1280]{1,0:T(8,128)S(1)} custom-call(bf16[64,1280]{1,0:T(8,128)(2,1)S(1)} %get-tuple-element.17.v_ref.older_ref, bf16[64,1024]{1,0:T(8,128)(2,1)S(1)} %collective-permute-done.2.right_ref, bf16[1280,3456]{1,0:T(8,128)(2,1)S(1)} %band.1.a_ref), custom_call_target="tpu_custom_call" | custom-call | flops 314572800 | tf_op jit(solution)/shard_map/near2/pallas_call | solution.py:191
  18.7 1.2 %collective-permute-done.3.left_ref = bf16[64,1024]{1,0:T(8,128)(2,1)S(1)} collective-permute-done((bf16[64,1024]{1,0:T(8,128)(2,1)S(1)}, bf16[64,1024]{1,0:T(8,128)(2,1)S(1)}, u32[]{:S(2)}, u32[]{:S(2)}) %collective-permute-start.3) | collective-permute-done | bytes 131104 | tf_op jit(solution)/shard_map/ppermute | solution.py:225
  19.9 0.6 level2.1
  20.5 0.1 collective-permute-start.4
  20.6 3.6 %collective-permute-start.5 = (bf16[64,1024]{1,0:T(8,128)(2,1)S(1)}, bf16[64,1024]{1,0:T(8,128)(2,1)S(1)}, u32[]{:S(2)}, u32[]{:S(2)}) collective-permute-start(bf16[64,1024]{1,0:T(8,128)(2,1)S(1)} %get-tuple-element.22), channel_id=1, source_target_pairs={{2,4},{4,2},{6,8},{8,6},{10,12},{12,10},{14,16},{16,14},{18,20},{2... | collective-permute-start | bytes 393224 | tf_op jit(solution)/shard_map/ppermute | solution.py:225
  24.2 1.4 %collective-permute-done.4.right_ref = bf16[64,1024]{1,0:T(8,128)(2,1)S(1)} collective-permute-done((bf16[64,1024]{1,0:T(8,128)(2,1)S(1)}, bf16[64,1024]{1,0:T(8,128)(2,1)S(1)}, u32[]{:S(2)}, u32[]{:S(2)}) %collective-permute-start.4) | collective-permute-done | bytes 131104 | tf_op jit(solution)/shard_map/ppermute | solution.py:225
  25.6 1.5 %near3.1.acc_ref = f32[64,1280]{1,0:T(8,128)S(1)} custom-call(bf16[64,1280]{1,0:T(8,128)(2,1)S(1)} %get-tuple-element.20.v_ref.older_ref, bf16[64,1024]{1,0:T(8,128)(2,1)S(1)} %collective-permute-done.4.right_ref, bf16[1280,3456]{1,0:T(8,128)(2,1)S(1)} %band.1.a_ref), custom_call_target="tpu_custom_call" | custom-call | flops 314572800 | tf_op jit(solution)/shard_map/near3/pallas_call | solution.py:191
  27.1 0.6 level3.1
  27.7 0.1 collective-permute-start.6
  27.8 3.7 %collective-permute-start.7 = (bf16[64,1024]{1,0:T(8,128)(2,1)S(1)}, bf16[64,1024]{1,0:T(8,128)(2,1)S(1)}, u32[]{:S(2)}, u32[]{:S(2)}) collective-permute-start(bf16[64,1024]{1,0:T(8,128)(2,1)S(1)} %get-tuple-element.25), channel_id=1, source_target_pairs={{2,4},{4,2},{6,8},{8,6},{10,12},{12,10},{14,16},{16,14},{18,20},{2... | collective-permute-start | bytes 393224 | tf_op jit(solution)/shard_map/ppermute | solution.py:225
  31.5 1.3 %collective-permute-done.6.right_ref = bf16[64,1024]{1,0:T(8,128)(2,1)S(1)} collective-permute-done((bf16[64,1024]{1,0:T(8,128)(2,1)S(1)}, bf16[64,1024]{1,0:T(8,128)(2,1)S(1)}, u32[]{:S(2)}, u32[]{:S(2)}) %collective-permute-start.6) | collective-permute-done | bytes 131104 | tf_op jit(solution)/shard_map/ppermute | solution.py:225
  32.7 1.5 %near4.1.acc_ref = f32[64,1280]{1,0:T(8,128)S(1)} custom-call(bf16[64,1280]{1,0:T(8,128)(2,1)S(1)} %get-tuple-element.23.v_ref, bf16[64,1024]{1,0:T(8,128)(2,1)S(1)} %collective-permute-done.6.right_ref, bf16[1280,3456]{1,0:T(8,128)(2,1)S(1)} %band.1.a_ref), custom_call_target="tpu_custom_call" | custom-call | flops 314572800 | tf_op jit(solution)/shard_map/near4/pallas_call | solution.py:191
  34.3 0.1 collective-permute-done.7.left_ref
  34.4 0.6 level4.1
  35.1 3.6 %collective-permute-start.10 = (bf16[64,1024]{1,0:T(8,128)(2,1)S(1)}, bf16[64,1024]{1,0:T(8,128)(2,1)S(1)}, u32[]{:S(2)}, u32[]{:S(2)}) collective-permute-start(bf16[64,1024]{1,0:T(8,128)(2,1)S(1)} %get-tuple-element.30), channel_id=1, source_target_pairs={{2,4},{4,2},{6,8},{8,6},{10,12},{12,10},{14,16},{16,14},{18,20},{2... | collective-permute-start | bytes 393224 | tf_op jit(solution)/shard_map/ppermute | solution.py:225
  38.6 1.4 %collective-permute-done.8.right_ref = bf16[64,1024]{1,0:T(8,128)(2,1)S(1)} collective-permute-done((bf16[64,1024]{1,0:T(8,128)(2,1)S(1)}, bf16[64,1024]{1,0:T(8,128)(2,1)S(1)}, u32[]{:S(2)}, u32[]{:S(2)}) %collective-permute-start.8) | collective-permute-done | bytes 131104 | tf_op jit(solution)/shard_map/ppermute | solution.py:225
  40.0 1.5 %near5.1.acc_ref = f32[64,1280]{1,0:T(8,128)S(1)} custom-call(bf16[64,1280]{1,0:T(8,128)(2,1)S(1)} %get-tuple-element.28.v_ref.own_ref, bf16[64,1024]{1,0:T(8,128)(2,1)S(1)} %collective-permute-done.8.right_ref, bf16[1280,3456]{1,0:T(8,128)(2,1)S(1)} %band.1.a_ref), custom_call_target="tpu_custom_call" | custom-call | flops 314572800 | tf_op jit(solution)/shard_map/near5/pallas_call | solution.py:191
  41.6 0.5 image.1.image_ref
  42.2 0.6 collective-permute-start.11
  42.8 0.3 collective-permute-done.9.other_ref
  43.0 0.8 collective-permute-done.11.other_image_ref
  43.8 0.4 gram.1
  44.2 2.1 %collective-permute-start.14 = (bf16[128,128]{1,0:T(8,128)(2,1)S(1)}, bf16[128,128]{1,0:T(8,128)(2,1)S(1)}, u32[]{:S(2)}, u32[]{:S(2)}) collective-permute-start(bf16[128,128]{1,0:T(8,128)(2,1)S(1)} %reduce-precision_convert_fusion), channel_id=1, source_target_pairs={{0,6},{2,4},{4,2},{6,0},{8,14},{10,12},{12,10},{14,8},{16,22},{18,... | collective-permute-start | bytes 98312 | tf_op jit(solution)/shard_map/ppermute | solution.py:238
  46.3 1.1 %collective-permute-start.13 = (bf16[128,128]{1,0:T(8,128)(2,1)S(1)}, bf16[128,128]{1,0:T(8,128)(2,1)S(1)}, u32[]{:S(2)}, u32[]{:S(2)}) collective-permute-start(bf16[128,128]{1,0:T(8,128)(2,1)S(1)} %reduce-precision_convert_fusion), channel_id=1, source_target_pairs={{0,4},{2,6},{4,0},{6,2},{8,12},{10,14},{12,8},{14,10},{16,20},{18,... | collective-permute-start | bytes 98312 | tf_op jit(solution)/shard_map/ppermute | solution.py:238
  47.4 1.4 %collective-permute-start.12 = (bf16[128,128]{1,0:T(8,128)(2,1)S(1)}, bf16[128,128]{1,0:T(8,128)(2,1)S(1)}, u32[]{:S(2)}, u32[]{:S(2)}) collective-permute-start(bf16[128,128]{1,0:T(8,128)(2,1)S(1)} %reduce-precision_convert_fusion), channel_id=1, source_target_pairs={{0,2},{2,0},{4,6},{6,4},{8,10},{10,8},{12,14},{14,12},{16,18},{18,... | collective-permute-start | bytes 98312 | tf_op jit(solution)/shard_map/ppermute | solution.py:238
  48.8 2.4 %collective-permute-done.13 = bf16[128,128]{1,0:T(8,128)(2,1)S(1)} collective-permute-done((bf16[128,128]{1,0:T(8,128)(2,1)S(1)}, bf16[128,128]{1,0:T(8,128)(2,1)S(1)}, u32[]{:S(2)}, u32[]{:S(2)}) %collective-permute-start.13) | collective-permute-done | bytes 32800 | tf_op jit(solution)/shard_map/ppermute | solution.py:238
  51.1 0.7 collective-permute-done.12
  51.8 6.1 %collective-permute-start.17 = (bf16[128,128]{1,0:T(8,128)(2,1)S(1)}, bf16[128,128]{1,0:T(8,128)(2,1)S(1)}, u32[]{:S(2)}, u32[]{:S(2)}) collective-permute-start(bf16[128,128]{1,0:T(8,128)(2,1)S(1)} %get-tuple-element.33), channel_id=1, source_target_pairs={{0,28},{2,30},{4,24},{6,26},{8,20},{10,22},{12,16},{14,18},{16,12}... | collective-permute-start | bytes 98312 | tf_op jit(solution)/shard_map/ppermute | solution.py:238
  57.9 2.4 %collective-permute-start.15 = (bf16[128,128]{1,0:T(8,128)(2,1)S(1)}, bf16[128,128]{1,0:T(8,128)(2,1)S(1)}, u32[]{:S(2)}, u32[]{:S(2)}) collective-permute-start(bf16[128,128]{1,0:T(8,128)(2,1)S(1)} %get-tuple-element.33), channel_id=1, source_target_pairs={{0,12},{2,14},{4,8},{6,10},{8,4},{10,6},{12,0},{14,2},{16,28},{18,... | collective-permute-start | bytes 98312 | tf_op jit(solution)/shard_map/ppermute | solution.py:238
  60.3 1.5 %collective-permute-done.16 = bf16[128,128]{1,0:T(8,128)(2,1)S(1)} collective-permute-done((bf16[128,128]{1,0:T(8,128)(2,1)S(1)}, bf16[128,128]{1,0:T(8,128)(2,1)S(1)}, u32[]{:S(2)}, u32[]{:S(2)}) %collective-permute-start.16) | collective-permute-done | bytes 32800 | tf_op jit(solution)/shard_map/ppermute | solution.py:238
  61.8 2.1 %collective-permute-done.15 = bf16[128,128]{1,0:T(8,128)(2,1)S(1)} collective-permute-done((bf16[128,128]{1,0:T(8,128)(2,1)S(1)}, bf16[128,128]{1,0:T(8,128)(2,1)S(1)}, u32[]{:S(2)}, u32[]{:S(2)}) %collective-permute-start.15) | collective-permute-done | bytes 32800 | tf_op jit(solution)/shard_map/ppermute | solution.py:238
  64.0 13.6 %collective-permute-start.20 = (bf16[128,128]{1,0:T(8,128)(2,1)S(1)}, bf16[128,128]{1,0:T(8,128)(2,1)S(1)}, u32[]{:S(2)}, u32[]{:S(2)}) collective-permute-start(bf16[128,128]{1,0:T(8,128)(2,1)S(1)} %fusion), channel_id=1, source_target_pairs={{0,112},{2,114},{4,116},{6,118},{8,120},{10,122},{12,124},{14,126}... | collective-permute-start | bytes 98312 | tf_op jit(solution)/shard_map/ppermute | solution.py:238
  77.6 0.5 collective-permute-start.19
  78.1 0.1 collective-permute-start.18
  78.3 1.2 %collective-permute-done.20 = bf16[128,128]{1,0:T(8,128)(2,1)S(1)} collective-permute-done((bf16[128,128]{1,0:T(8,128)(2,1)S(1)}, bf16[128,128]{1,0:T(8,128)(2,1)S(1)}, u32[]{:S(2)}, u32[]{:S(2)}) %collective-permute-start.20) | collective-permute-done | bytes 32800 | tf_op jit(solution)/shard_map/ppermute | solution.py:238
  79.5 2.0 %collective-permute-done.19 = bf16[128,128]{1,0:T(8,128)(2,1)S(1)} collective-permute-done((bf16[128,128]{1,0:T(8,128)(2,1)S(1)}, bf16[128,128]{1,0:T(8,128)(2,1)S(1)}, u32[]{:S(2)}, u32[]{:S(2)}) %collective-permute-start.19) | collective-permute-done | bytes 32800 | tf_op jit(solution)/shard_map/ppermute | solution.py:238
  81.5 1.7 %collective-permute-done.18 = bf16[128,128]{1,0:T(8,128)(2,1)S(1)} collective-permute-done((bf16[128,128]{1,0:T(8,128)(2,1)S(1)}, bf16[128,128]{1,0:T(8,128)(2,1)S(1)}, u32[]{:S(2)}, u32[]{:S(2)}) %collective-permute-start.18) | collective-permute-done | bytes 32800 | tf_op jit(solution)/shard_map/ppermute | solution.py:238
  83.3 1.7 %collective-permute-start.21 = (bf16[128,128]{1,0:T(8,128)(2,1)S(1)}, bf16[128,128]{1,0:T(8,128)(2,1)S(1)}, u32[]{:S(2)}, u32[]{:S(2)}) collective-permute-start(bf16[128,128]{1,0:T(8,128)(2,1)S(1)} %get-tuple-element.31), channel_id=1, source_target_pairs={{0,192},{2,194},{4,196},{6,198},{8,200},{10,202},{12,204},{14,206}... | collective-permute-start | bytes 98312 | tf_op jit(solution)/shard_map/ppermute | solution.py:238
  84.9 0.7 copy.7
  85.6 2.9 %collective-permute-done.21 = bf16[128,128]{1,0:T(8,128)(2,1)S(1)} collective-permute-done((bf16[128,128]{1,0:T(8,128)(2,1)S(1)}, bf16[128,128]{1,0:T(8,128)(2,1)S(1)}, u32[]{:S(2)}, u32[]{:S(2)}) %collective-permute-start.21) | collective-permute-done | bytes 32800 | tf_op jit(solution)/shard_map/ppermute | solution.py:238
  88.5 0.6 fusion.3
  (17 shorter events, 0.4 us)
Async XLA Ops:
  0.6 9.4 %copy-start = (bf16[1280,64]{0,1:T(8,128)(2,1)S(1)}, bf16[1280,64]{0,1:T(8,128)(2,1)}, u32[]{:S(2)}) copy-start(bf16[1280,64]{0,1:T(8,128)(2,1)} %param.7) | copy-start | bytes 491524
  0.6 9.4 %collective-permute-start = (bf16[64,1280]{1,0:T(8,128)(2,1)}, bf16[64,1280]{1,0:T(8,128)(2,1)S(1)}, u32[]{:S(2)}, u32[]{:S(2)}) collective-permute-start(bf16[64,1280]{1,0:T(8,128)(2,1)} %bitcast.4), channel_id=1, source_target_pairs={{0,2},{2,0},{4,6},{6,4},{8,10},{10,8},{12,14},{14,12},{16,18},{18,... | collective-permute-start | bytes 491528 | tf_op jit(solution)/shard_map/ppermute | solution.py:225
  2.6 9.0 %collective-permute-start.1 = (bf16[64,1280]{1,0:T(8,128)(2,1)}, bf16[64,1280]{1,0:T(8,128)(2,1)S(1)}, u32[]{:S(2)}, u32[]{:S(2)}) collective-permute-start(bf16[64,1280]{1,0:T(8,128)(2,1)} %bitcast.5), channel_id=1, source_target_pairs={{2,4},{4,2},{6,8},{8,6},{10,12},{12,10},{14,16},{16,14},{18,20},{2... | collective-permute-start | bytes 491528 | tf_op jit(solution)/shard_map/ppermute | solution.py:225
  12.1 5.1 %collective-permute-start.2 = (bf16[64,1024]{1,0:T(8,128)(2,1)S(1)}, bf16[64,1024]{1,0:T(8,128)(2,1)S(1)}, u32[]{:S(2)}, u32[]{:S(2)}) collective-permute-start(bf16[64,1024]{1,0:T(8,128)(2,1)S(1)} %get-tuple-element.18), channel_id=1, source_target_pairs={{0,2},{2,0},{4,6},{6,4},{8,10},{10,8},{12,14},{14,12},{16,18},{18,... | collective-permute-start | bytes 393224 | tf_op jit(solution)/shard_map/ppermute | solution.py:225
  12.2 7.7 %collective-permute-start.3 = (bf16[64,1024]{1,0:T(8,128)(2,1)S(1)}, bf16[64,1024]{1,0:T(8,128)(2,1)S(1)}, u32[]{:S(2)}, u32[]{:S(2)}) collective-permute-start(bf16[64,1024]{1,0:T(8,128)(2,1)S(1)} %get-tuple-element.19), channel_id=1, source_target_pairs={{2,4},{4,2},{6,8},{8,6},{10,12},{12,10},{14,16},{16,14},{18,20},{2... | collective-permute-start | bytes 393224 | tf_op jit(solution)/shard_map/ppermute | solution.py:225
  20.5 5.1 %collective-permute-start.4 = (bf16[64,1024]{1,0:T(8,128)(2,1)S(1)}, bf16[64,1024]{1,0:T(8,128)(2,1)S(1)}, u32[]{:S(2)}, u32[]{:S(2)}) collective-permute-start(bf16[64,1024]{1,0:T(8,128)(2,1)S(1)} %get-tuple-element.21), channel_id=1, source_target_pairs={{0,2},{2,0},{4,6},{6,4},{8,10},{10,8},{12,14},{14,12},{16,18},{18,... | collective-permute-start | bytes 393224 | tf_op jit(solution)/shard_map/ppermute | solution.py:225
  20.6 6.5 %collective-permute-start.5 = (bf16[64,1024]{1,0:T(8,128)(2,1)S(1)}, bf16[64,1024]{1,0:T(8,128)(2,1)S(1)}, u32[]{:S(2)}, u32[]{:S(2)}) collective-permute-start(bf16[64,1024]{1,0:T(8,128)(2,1)S(1)} %get-tuple-element.22), channel_id=1, source_target_pairs={{2,4},{4,2},{6,8},{8,6},{10,12},{12,10},{14,16},{16,14},{18,20},{2... | collective-permute-start | bytes 393224 | tf_op jit(solution)/shard_map/ppermute | solution.py:225
  27.7 5.1 %collective-permute-start.6 = (bf16[64,1024]{1,0:T(8,128)(2,1)S(1)}, bf16[64,1024]{1,0:T(8,128)(2,1)S(1)}, u32[]{:S(2)}, u32[]{:S(2)}) collective-permute-start(bf16[64,1024]{1,0:T(8,128)(2,1)S(1)} %get-tuple-element.24), channel_id=1, source_target_pairs={{0,2},{2,0},{4,6},{6,4},{8,10},{10,8},{12,14},{14,12},{16,18},{18,... | collective-permute-start | bytes 393224 | tf_op jit(solution)/shard_map/ppermute | solution.py:225
  27.8 6.6 %collective-permute-start.7 = (bf16[64,1024]{1,0:T(8,128)(2,1)S(1)}, bf16[64,1024]{1,0:T(8,128)(2,1)S(1)}, u32[]{:S(2)}, u32[]{:S(2)}) collective-permute-start(bf16[64,1024]{1,0:T(8,128)(2,1)S(1)} %get-tuple-element.25), channel_id=1, source_target_pairs={{2,4},{4,2},{6,8},{8,6},{10,12},{12,10},{14,16},{16,14},{18,20},{2... | collective-permute-start | bytes 393224 | tf_op jit(solution)/shard_map/ppermute | solution.py:225
  35.0 5.1 %collective-permute-start.8 = (bf16[64,1024]{1,0:T(8,128)(2,1)S(1)}, bf16[64,1024]{1,0:T(8,128)(2,1)S(1)}, u32[]{:S(2)}, u32[]{:S(2)}) collective-permute-start(bf16[64,1024]{1,0:T(8,128)(2,1)S(1)} %get-tuple-element.27), channel_id=1, source_target_pairs={{0,2},{2,0},{4,6},{6,4},{8,10},{10,8},{12,14},{14,12},{16,18},{18,... | collective-permute-start | bytes 393224 | tf_op jit(solution)/shard_map/ppermute | solution.py:225
  35.1 6.5 %collective-permute-start.10 = (bf16[64,1024]{1,0:T(8,128)(2,1)S(1)}, bf16[64,1024]{1,0:T(8,128)(2,1)S(1)}, u32[]{:S(2)}, u32[]{:S(2)}) collective-permute-start(bf16[64,1024]{1,0:T(8,128)(2,1)S(1)} %get-tuple-element.30), channel_id=1, source_target_pairs={{2,4},{4,2},{6,8},{8,6},{10,12},{12,10},{14,16},{16,14},{18,20},{2... | collective-permute-start | bytes 393224 | tf_op jit(solution)/shard_map/ppermute | solution.py:225
  41.6 1.4 %collective-permute-start.9 = (bf16[64,1280]{1,0:T(8,128)(2,1)S(1)}, bf16[64,1280]{1,0:T(8,128)(2,1)S(1)}, u32[]{:S(2)}, u32[]{:S(2)}) collective-permute-start(bf16[64,1280]{1,0:T(8,128)(2,1)S(1)} %get-tuple-element.28.v_ref.own_ref), channel_id=1, source_target_pairs={{0,1},{1,0},{2,3},{3,2},{4,5},{5,4},{6,7},{7,6},{8,9},{9,8},{10,11... | collective-permute-start | bytes 491528 | tf_op jit(solution)/shard_map/ppermute | solution.py:229
  42.2 1.6 %collective-permute-start.11 = (bf16[64,1280]{1,0:T(8,128)(2,1)S(1)}, bf16[64,1280]{1,0:T(8,128)(2,1)S(1)}, u32[]{:S(2)}, u32[]{:S(2)}) collective-permute-start(bf16[64,1280]{1,0:T(8,128)(2,1)S(1)} %image.1.image_ref), channel_id=1, source_target_pairs={{0,1},{1,0},{2,3},{3,2},{4,5},{5,4},{6,7},{7,6},{8,9},{9,8},{10,11... | collective-permute-start | bytes 491528 | tf_op jit(solution)/shard_map/ppermute | solution.py:229
  44.2 4.6 %collective-permute-start.14 = (bf16[128,128]{1,0:T(8,128)(2,1)S(1)}, bf16[128,128]{1,0:T(8,128)(2,1)S(1)}, u32[]{:S(2)}, u32[]{:S(2)}) collective-permute-start(bf16[128,128]{1,0:T(8,128)(2,1)S(1)} %reduce-precision_convert_fusion), channel_id=1, source_target_pairs={{0,6},{2,4},{4,2},{6,0},{8,14},{10,12},{12,10},{14,8},{16,22},{18,... | collective-permute-start | bytes 98312 | tf_op jit(solution)/shard_map/ppermute | solution.py:238
  46.3 4.8 %collective-permute-start.13 = (bf16[128,128]{1,0:T(8,128)(2,1)S(1)}, bf16[128,128]{1,0:T(8,128)(2,1)S(1)}, u32[]{:S(2)}, u32[]{:S(2)}) collective-permute-start(bf16[128,128]{1,0:T(8,128)(2,1)S(1)} %reduce-precision_convert_fusion), channel_id=1, source_target_pairs={{0,4},{2,6},{4,0},{6,2},{8,12},{10,14},{12,8},{14,10},{16,20},{18,... | collective-permute-start | bytes 98312 | tf_op jit(solution)/shard_map/ppermute | solution.py:238
  47.4 4.4 %collective-permute-start.12 = (bf16[128,128]{1,0:T(8,128)(2,1)S(1)}, bf16[128,128]{1,0:T(8,128)(2,1)S(1)}, u32[]{:S(2)}, u32[]{:S(2)}) collective-permute-start(bf16[128,128]{1,0:T(8,128)(2,1)S(1)} %reduce-precision_convert_fusion), channel_id=1, source_target_pairs={{0,2},{2,0},{4,6},{6,4},{8,10},{10,8},{12,14},{14,12},{16,18},{18,... | collective-permute-start | bytes 98312 | tf_op jit(solution)/shard_map/ppermute | solution.py:238
  51.8 8.5 %collective-permute-start.17 = (bf16[128,128]{1,0:T(8,128)(2,1)S(1)}, bf16[128,128]{1,0:T(8,128)(2,1)S(1)}, u32[]{:S(2)}, u32[]{:S(2)}) collective-permute-start(bf16[128,128]{1,0:T(8,128)(2,1)S(1)} %get-tuple-element.33), channel_id=1, source_target_pairs={{0,28},{2,30},{4,24},{6,26},{8,20},{10,22},{12,16},{14,18},{16,12}... | collective-permute-start | bytes 98312 | tf_op jit(solution)/shard_map/ppermute | solution.py:238
  57.9 3.9 %collective-permute-start.16 = (bf16[128,128]{1,0:T(8,128)(2,1)S(1)}, bf16[128,128]{1,0:T(8,128)(2,1)S(1)}, u32[]{:S(2)}, u32[]{:S(2)}) collective-permute-start(bf16[128,128]{1,0:T(8,128)(2,1)S(1)} %get-tuple-element.33), channel_id=1, source_target_pairs={{0,16},{2,18},{4,20},{6,22},{8,24},{10,26},{12,28},{14,30},{16,0},... | collective-permute-start | bytes 98312 | tf_op jit(solution)/shard_map/ppermute | solution.py:238
  57.9 6.0 %collective-permute-start.15 = (bf16[128,128]{1,0:T(8,128)(2,1)S(1)}, bf16[128,128]{1,0:T(8,128)(2,1)S(1)}, u32[]{:S(2)}, u32[]{:S(2)}) collective-permute-start(bf16[128,128]{1,0:T(8,128)(2,1)S(1)} %get-tuple-element.33), channel_id=1, source_target_pairs={{0,12},{2,14},{4,8},{6,10},{8,4},{10,6},{12,0},{14,2},{16,28},{18,... | collective-permute-start | bytes 98312 | tf_op jit(solution)/shard_map/ppermute | solution.py:238
  64.0 15.5 %collective-permute-start.20 = (bf16[128,128]{1,0:T(8,128)(2,1)S(1)}, bf16[128,128]{1,0:T(8,128)(2,1)S(1)}, u32[]{:S(2)}, u32[]{:S(2)}) collective-permute-start(bf16[128,128]{1,0:T(8,128)(2,1)S(1)} %fusion), channel_id=1, source_target_pairs={{0,112},{2,114},{4,116},{6,118},{8,120},{10,122},{12,124},{14,126}... | collective-permute-start | bytes 98312 | tf_op jit(solution)/shard_map/ppermute | solution.py:238
  77.6 3.9 %collective-permute-start.19 = (bf16[128,128]{1,0:T(8,128)(2,1)S(1)}, bf16[128,128]{1,0:T(8,128)(2,1)S(1)}, u32[]{:S(2)}, u32[]{:S(2)}) collective-permute-start(bf16[128,128]{1,0:T(8,128)(2,1)S(1)} %fusion), channel_id=1, source_target_pairs={{0,64},{2,66},{4,68},{6,70},{8,72},{10,74},{12,76},{14,78},{16,80}... | collective-permute-start | bytes 98312 | tf_op jit(solution)/shard_map/ppermute | solution.py:238
  78.1 5.1 %collective-permute-start.18 = (bf16[128,128]{1,0:T(8,128)(2,1)S(1)}, bf16[128,128]{1,0:T(8,128)(2,1)S(1)}, u32[]{:S(2)}, u32[]{:S(2)}) collective-permute-start(bf16[128,128]{1,0:T(8,128)(2,1)S(1)} %fusion), channel_id=1, source_target_pairs={{0,48},{2,50},{4,52},{6,54},{8,56},{10,58},{12,60},{14,62},{16,32}... | collective-permute-start | bytes 98312 | tf_op jit(solution)/shard_map/ppermute | solution.py:238
  83.3 5.2 %collective-permute-start.21 = (bf16[128,128]{1,0:T(8,128)(2,1)S(1)}, bf16[128,128]{1,0:T(8,128)(2,1)S(1)}, u32[]{:S(2)}, u32[]{:S(2)}) collective-permute-start(bf16[128,128]{1,0:T(8,128)(2,1)S(1)} %get-tuple-element.31), channel_id=1, source_target_pairs={{0,192},{2,194},{4,196},{6,198},{8,200},{10,202},{12,204},{14,206}... | collective-permute-start | bytes 98312 | tf_op jit(solution)/shard_map/ppermute | solution.py:238

commit v6 on v5

--- a/solution.py
+++ b/solution.py
@@ -125,30 +125,35 @@
     return ref[:, ref.shape[1] - DIST * B :], ref[:, : DIST * B]
 
 
-def near_kernel(v_ref, right_ref, a_ref, acc_ref):
+def near_kernel(v_ref, right_ref, a_ref, acc_ref, older_ref=None):
     rows = acc_ref.shape[1]
     step = 2 * B
     v = v_ref[...]
 
     def run(halo, part):
         for i in range(0, rows, step):
-            own = dot_nt(v, a_ref[i : i + step, DIST * B : DIST * B + rows])
-            acc_ref[:, i : i + step] = own + part(halo, a_ref, i, step)
+            total = dot_nt(v, a_ref[i : i + step, DIST * B : DIST * B + rows])
+            total += part(halo, a_ref, i, step)
+            if older_ref is not None:
+                total = 2.0 * total - older_ref[:, i : i + step].astype(jnp.float32)
+            acc_ref[:, i : i + step] = total
 
     low, high = halo_sides(right_ref)
     pl.when(on_even_chip())(lambda: run(high, high_part))
     pl.when(jnp.logical_not(on_even_chip()))(lambda: run(low, low_part))
 
 
-def finish(acc_ref, left_ref, a_ref, new_ref, older_ref=None):
+def near_next_kernel(v_ref, right_ref, a_ref, older_ref, acc_ref):
+    near_kernel(v_ref, right_ref, a_ref, acc_ref, older_ref)
+
+
+def finish(acc_ref, left_ref, a_ref, new_ref, scale=1.0):
     rows = acc_ref.shape[1]
     step = 2 * B
 
     def run(halo, part):
         for i in range(0, rows, step):
-            total = acc_ref[:, i : i + step] + part(halo, a_ref, i, step)
-            if older_ref is not None:
-                total = 2.0 * total - older_ref[:, i : i + step].astype(jnp.float32)
+            total = acc_ref[:, i : i + step] + scale * part(halo, a_ref, i, step)
             new_ref[:, i : i + step] = total.astype(new_ref.dtype)
 
     low, high = halo_sides(left_ref)
@@ -177,8 +182,8 @@
     depart(new_ref, to_right_ref, to_left_ref)
 
 
-def next_kernel(acc_ref, left_ref, a_ref, older_ref, new_ref, to_right_ref, to_left_ref):
-    finish(acc_ref, left_ref, a_ref, new_ref, older_ref)
+def next_kernel(acc_ref, left_ref, a_ref, new_ref, to_right_ref, to_left_ref):
+    finish(acc_ref, left_ref, a_ref, new_ref, 2.0)
     depart(new_ref, to_right_ref, to_left_ref)
 
 
@@ -231,7 +236,7 @@
 
 def sum_over_rows(value):
     count = lax.axis_size(ROWS)
-    for distances in ((1, 2, 3), (6, 8, 14), (24, 32, 56), (96,)):
+    for distances in ((1, 2, 3), (6,), (8, 16, 24), (32, 64, 96)):
         own = lax.reduce_precision(value, exponent_bits=8, mantissa_bits=7)
         sent = own.astype(jnp.bfloat16)
         others = [
@@ -253,8 +258,9 @@
     part = ((width, rows), jnp.float32)
     near_flops = 3 * width * rows * rows
 
-    def near(v, right, name):
-        return in_vmem(near_kernel, name, [part], v, right, band, flops=near_flops)[0]
+    def near(v, right, name, *older):
+        kernel = near_next_kernel if older else near_kernel
+        return in_vmem(kernel, name, [part], v, right, band, *older, flops=near_flops)[0]
 
     start = vectors.T
     right, left = exchange(start, start)
@@ -264,9 +270,9 @@
     older, newer = start, level1
     for degree in range(2, 5):
         right, left = exchange(*edges)
-        acc = near(newer, right, "near%d" % degree)
+        acc = near(newer, right, "near%d" % degree, older)
         latest, *edges = in_vmem(
-            next_kernel, "level%d" % degree, [field, halo, halo], acc, left, band, older
+            next_kernel, "level%d" % degree, [field, halo, halo], acc, left, band
         )
         older, newer = newer, latest
     right, left = exchange(*edges)

time: 90 us -> 88.3 us (0.981)
  waiting for transfers between devices: 21.2 us -> 19.8 us
    ppermute x10, waiting for transfers between devices: 14.6 us -> 13.2 us  [sum_over_rows(): lax.ppermute(sent, ROWS, [(i, i ^ d) for i in range(count)])]
  transfers between devices with their start and end apart: 22 -> 22, of which waited for: 16 -> 15; matrix products, arithmetic and copies ran while one was open for 1% -> 1% of each run, Pallas kernels for 15% -> 16%
where the time goes in v6:
time: 88.3 us; the launch traced here: 88 us
  starting transfers between devices  49.5 us (56%)
  waiting for transfers between devices  19.8 us (22%)
  Pallas kernels  16.5 us (19%)
  local copies, waits for them, and re-layouts  1.3 us (1%)
    ppermute x10, starting transfers between devices, sum_over_rows(): lax.ppermute(sent, ROWS, [(i, i ^ d) for i in range(count)])  29.5 us
    ppermute x5, starting transfers between devices, exchange(): lax.ppermute(to_left, every, left)  17 us
    ppermute x10, waiting for transfers between devices, sum_over_rows(): lax.ppermute(sent, ROWS, [(i, i ^ d) for i in range(count)])  13.2 us
    pallas_call x10, Pallas kernels, in_vmem(): pl.pallas_call(kernel, out_shape=[pltpu.VMEM(s, d) for s, d in outs], in_...  10.4 us
    pallas_call x1, Pallas kernels, build_band(): pl.pallas_call(band_kernel, out_shape=pltpu.VMEM((block_rows * B, width),...  5.65 us
    ppermute x5, waiting for transfers between devices, exchange(): lax.ppermute(to_right, every, right)  4.85 us
    ppermute x5, starting transfers between devices, exchange(): lax.ppermute(to_right, every, right)  2.48 us
  transfers between devices with their start and end apart: 22, of which 15 were waited for; matrix products, arithmetic and copies ran while one was open for 1% of the time, Pallas kernels for 16%

profile of v6, /device:TPU:32, one launch (start us, length us, event | category | flops | bytes accessed | tf_op | source)
XLA Modules:
  0.0 88.0 jit_solution(1664102997586580350)
XLA Ops:
  0.6 1.9 %collective-permute-start = (bf16[64,1280]{1,0:T(8,128)(2,1)}, bf16[64,1280]{1,0:T(8,128)(2,1)S(1)}, u32[]{:S(2)}, u32[]{:S(2)}) collective-permute-start(bf16[64,1280]{1,0:T(8,128)(2,1)} %bitcast.4), channel_id=1, source_target_pairs={{0,2},{2,0},{4,6},{6,4},{8,10},{10,8},{12,14},{14,12},{16,18},{18,... | collective-permute-start | bytes 491528 | tf_op jit(solution)/shard_map/ppermute | solution.py:230
  2.6 2.0 %collective-permute-start.1 = (bf16[64,1280]{1,0:T(8,128)(2,1)}, bf16[64,1280]{1,0:T(8,128)(2,1)S(1)}, u32[]{:S(2)}, u32[]{:S(2)}) collective-permute-start(bf16[64,1280]{1,0:T(8,128)(2,1)} %bitcast.5), channel_id=1, source_target_pairs={{2,4},{4,2},{6,8},{8,6},{10,12},{12,10},{14,16},{16,14},{18,20},{2... | collective-permute-start | bytes 491528 | tf_op jit(solution)/shard_map/ppermute | solution.py:230
  4.6 5.7 %band.1.a_ref = bf16[1280,3456]{1,0:T(8,128)(2,1)S(1)} custom-call(s32[1,10]{1,0:T(1,128)} %bitcast.8, s32[10,32]{1,0:T(8,128)} %near_ref.1, bf16[10,32,128,128]{3,2,1,0:T(8,128)(2,1)} %h_ref.1), custom_call_target="tpu_custom_call" | custom-call | tf_op jit(solution)/shard_map/band/pallas_call | solution.py:89
  10.2 1.5 %near1.1.acc_ref = f32[64,1280]{1,0:T(8,128)S(1)} custom-call(bf16[64,1280]{1,0:T(8,128)(2,1)S(1)} %bitcast.6, bf16[64,1280]{1,0:T(8,128)(2,1)S(1)} %collective-permute-done.right_ref, bf16[1280,3456]{1,0:T(8,128)(2,1)S(1)} %band.1.a_ref), custom_call_target="tpu_custom_call" | custom-call | flops 314572800 | tf_op jit(solution)/shard_map/near1/pallas_call | solution.py:196
  11.8 0.6 level1.1
  12.5 4.1 %collective-permute-start.3 = (bf16[64,1024]{1,0:T(8,128)(2,1)S(1)}, bf16[64,1024]{1,0:T(8,128)(2,1)S(1)}, u32[]{:S(2)}, u32[]{:S(2)}) collective-permute-start(bf16[64,1024]{1,0:T(8,128)(2,1)S(1)} %get-tuple-element.19), channel_id=1, source_target_pairs={{2,4},{4,2},{6,8},{8,6},{10,12},{12,10},{14,16},{16,14},{18,20},{2... | collective-permute-start | bytes 393224 | tf_op jit(solution)/shard_map/ppermute | solution.py:230
  16.6 0.8 collective-permute-done.2.right_ref
  17.4 1.5 %near2.1.acc_ref = f32[64,1280]{1,0:T(8,128)S(1)} custom-call(bf16[64,1280]{1,0:T(8,128)(2,1)S(1)} %get-tuple-element.17.v_ref.older_ref, bf16[64,1024]{1,0:T(8,128)(2,1)S(1)} %collective-permute-done.2.right_ref, bf16[1280,3456]{1,0:T(8,128)(2,1)S(1)} %band.1.a_ref, bf16[64,1280]{1,0:T(8,128)(2,1)S(1)} %bitcast.7), custom_call_target="tpu_custom_call" | custom-call | flops 314572800 | tf_op jit(solution)/shard_map/near2/pallas_call | solution.py:196
  19.0 0.6 collective-permute-done.3.left_ref
  19.5 0.5 level2.1
  20.1 0.1 collective-permute-start.4
  20.2 3.6 %collective-permute-start.5 = (bf16[64,1024]{1,0:T(8,128)(2,1)S(1)}, bf16[64,1024]{1,0:T(8,128)(2,1)S(1)}, u32[]{:S(2)}, u32[]{:S(2)}) collective-permute-start(bf16[64,1024]{1,0:T(8,128)(2,1)S(1)} %get-tuple-element.22), channel_id=1, source_target_pairs={{2,4},{4,2},{6,8},{8,6},{10,12},{12,10},{14,16},{16,14},{18,20},{2... | collective-permute-start | bytes 393224 | tf_op jit(solution)/shard_map/ppermute | solution.py:230
  23.8 1.4 %collective-permute-done.4.right_ref = bf16[64,1024]{1,0:T(8,128)(2,1)S(1)} collective-permute-done((bf16[64,1024]{1,0:T(8,128)(2,1)S(1)}, bf16[64,1024]{1,0:T(8,128)(2,1)S(1)}, u32[]{:S(2)}, u32[]{:S(2)}) %collective-permute-start.4) | collective-permute-done | bytes 131104 | tf_op jit(solution)/shard_map/ppermute | solution.py:230
  25.2 1.5 %near3.1.acc_ref = f32[64,1280]{1,0:T(8,128)S(1)} custom-call(bf16[64,1280]{1,0:T(8,128)(2,1)S(1)} %get-tuple-element.20.v_ref.older_ref, bf16[64,1024]{1,0:T(8,128)(2,1)S(1)} %collective-permute-done.4.right_ref, bf16[1280,3456]{1,0:T(8,128)(2,1)S(1)} %band.1.a_ref, bf16[64,1280]{1,0:T(8,128)(2,1)S(1)} %get-tuple-element.17.v_ref.older_ref), custom_call_target="tpu_custom_call" | custom-call | flops 314572800 | tf_op jit(solution)/shard_map/near3/pallas_call | solution.py:196
  26.7 0.5 level3.1
  27.3 0.1 collective-permute-start.6
  27.4 3.7 %collective-permute-start.7 = (bf16[64,1024]{1,0:T(8,128)(2,1)S(1)}, bf16[64,1024]{1,0:T(8,128)(2,1)S(1)}, u32[]{:S(2)}, u32[]{:S(2)}) collective-permute-start(bf16[64,1024]{1,0:T(8,128)(2,1)S(1)} %get-tuple-element.25), channel_id=1, source_target_pairs={{2,4},{4,2},{6,8},{8,6},{10,12},{12,10},{14,16},{16,14},{18,20},{2... | collective-permute-start | bytes 393224 | tf_op jit(solution)/shard_map/ppermute | solution.py:230
  31.1 1.3 %collective-permute-done.6.right_ref = bf16[64,1024]{1,0:T(8,128)(2,1)S(1)} collective-permute-done((bf16[64,1024]{1,0:T(8,128)(2,1)S(1)}, bf16[64,1024]{1,0:T(8,128)(2,1)S(1)}, u32[]{:S(2)}, u32[]{:S(2)}) %collective-permute-start.6) | collective-permute-done | bytes 131104 | tf_op jit(solution)/shard_map/ppermute | solution.py:230
  32.3 1.5 %near4.1.acc_ref = f32[64,1280]{1,0:T(8,128)S(1)} custom-call(bf16[64,1280]{1,0:T(8,128)(2,1)S(1)} %get-tuple-element.23.v_ref, bf16[64,1024]{1,0:T(8,128)(2,1)S(1)} %collective-permute-done.6.right_ref, bf16[1280,3456]{1,0:T(8,128)(2,1)S(1)} %band.1.a_ref, bf16[64,1280]{1,0:T(8,128)(2,1)S(1)} %get-tuple-element.20.v_ref.older_ref), custom_call_target="tpu_custom_call" | custom-call | flops 314572800 | tf_op jit(solution)/shard_map/near4/pallas_call | solution.py:196
  33.9 0.1 collective-permute-done.7.left_ref
  34.0 0.5 level4.1
  34.6 0.3 collective-permute-start.8
  34.8 3.6 %collective-permute-start.10 = (bf16[64,1024]{1,0:T(8,128)(2,1)S(1)}, bf16[64,1024]{1,0:T(8,128)(2,1)S(1)}, u32[]{:S(2)}, u32[]{:S(2)}) collective-permute-start(bf16[64,1024]{1,0:T(8,128)(2,1)S(1)} %get-tuple-element.30), channel_id=1, source_target_pairs={{2,4},{4,2},{6,8},{8,6},{10,12},{12,10},{14,16},{16,14},{18,20},{2... | collective-permute-start | bytes 393224 | tf_op jit(solution)/shard_map/ppermute | solution.py:230
  38.4 1.4 %collective-permute-done.8.right_ref = bf16[64,1024]{1,0:T(8,128)(2,1)S(1)} collective-permute-done((bf16[64,1024]{1,0:T(8,128)(2,1)S(1)}, bf16[64,1024]{1,0:T(8,128)(2,1)S(1)}, u32[]{:S(2)}, u32[]{:S(2)}) %collective-permute-start.8) | collective-permute-done | bytes 131104 | tf_op jit(solution)/shard_map/ppermute | solution.py:230
  39.8 1.5 %near5.1.acc_ref = f32[64,1280]{1,0:T(8,128)S(1)} custom-call(bf16[64,1280]{1,0:T(8,128)(2,1)S(1)} %get-tuple-element.28.v_ref.own_ref, bf16[64,1024]{1,0:T(8,128)(2,1)S(1)} %collective-permute-done.8.right_ref, bf16[1280,3456]{1,0:T(8,128)(2,1)S(1)} %band.1.a_ref), custom_call_target="tpu_custom_call" | custom-call | flops 314572800 | tf_op jit(solution)/shard_map/near5/pallas_call | solution.py:196
  41.4 0.5 image.1.image_ref
  41.9 0.6 collective-permute-start.11
  42.5 0.3 collective-permute-done.9.other_ref
  42.8 0.8 collective-permute-done.11.other_image_ref
  43.5 0.4 gram.1
  43.9 2.1 %collective-permute-start.14 = (bf16[128,128]{1,0:T(8,128)(2,1)S(1)}, bf16[128,128]{1,0:T(8,128)(2,1)S(1)}, u32[]{:S(2)}, u32[]{:S(2)}) collective-permute-start(bf16[128,128]{1,0:T(8,128)(2,1)S(1)} %reduce-precision_convert_fusion), channel_id=1, source_target_pairs={{0,6},{2,4},{4,2},{6,0},{8,14},{10,12},{12,10},{14,8},{16,22},{18,... | collective-permute-start | bytes 98312 | tf_op jit(solution)/shard_map/ppermute | solution.py:243
  46.0 1.1 %collective-permute-start.13 = (bf16[128,128]{1,0:T(8,128)(2,1)S(1)}, bf16[128,128]{1,0:T(8,128)(2,1)S(1)}, u32[]{:S(2)}, u32[]{:S(2)}) collective-permute-start(bf16[128,128]{1,0:T(8,128)(2,1)S(1)} %reduce-precision_convert_fusion), channel_id=1, source_target_pairs={{0,4},{2,6},{4,0},{6,2},{8,12},{10,14},{12,8},{14,10},{16,20},{18,... | collective-permute-start | bytes 98312 | tf_op jit(solution)/shard_map/ppermute | solution.py:243
  47.2 1.4 %collective-permute-start.12 = (bf16[128,128]{1,0:T(8,128)(2,1)S(1)}, bf16[128,128]{1,0:T(8,128)(2,1)S(1)}, u32[]{:S(2)}, u32[]{:S(2)}) collective-permute-start(bf16[128,128]{1,0:T(8,128)(2,1)S(1)} %reduce-precision_convert_fusion), channel_id=1, source_target_pairs={{0,2},{2,0},{4,6},{6,4},{8,10},{10,8},{12,14},{14,12},{16,18},{18,... | collective-permute-start | bytes 98312 | tf_op jit(solution)/shard_map/ppermute | solution.py:243
  48.5 2.4 %collective-permute-done.13 = bf16[128,128]{1,0:T(8,128)(2,1)S(1)} collective-permute-done((bf16[128,128]{1,0:T(8,128)(2,1)S(1)}, bf16[128,128]{1,0:T(8,128)(2,1)S(1)}, u32[]{:S(2)}, u32[]{:S(2)}) %collective-permute-start.13) | collective-permute-done | bytes 32800 | tf_op jit(solution)/shard_map/ppermute | solution.py:243
  50.9 0.7 collective-permute-done.12
  51.6 5.4 %collective-permute-start.15 = (bf16[128,128]{1,0:T(8,128)(2,1)S(1)}, bf16[128,128]{1,0:T(8,128)(2,1)S(1)}, u32[]{:S(2)}, u32[]{:S(2)}) collective-permute-start(bf16[128,128]{1,0:T(8,128)(2,1)S(1)} %get-tuple-element.31), channel_id=1, source_target_pairs={{0,12},{2,14},{4,8},{6,10},{8,4},{10,6},{12,0},{14,2},{16,28},{18,... | collective-permute-start | bytes 98312 | tf_op jit(solution)/shard_map/ppermute | solution.py:243
  57.0 1.9 %collective-permute-done.15 = bf16[128,128]{1,0:T(8,128)(2,1)S(1)} collective-permute-done((bf16[128,128]{1,0:T(8,128)(2,1)S(1)}, bf16[128,128]{1,0:T(8,128)(2,1)S(1)}, u32[]{:S(2)}, u32[]{:S(2)}) %collective-permute-start.15) | collective-permute-done | bytes 32800 | tf_op jit(solution)/shard_map/ppermute | solution.py:243
  58.9 12.2 %collective-permute-start.18 = (bf16[128,128]{1,0:T(8,128)(2,1)S(1)}, bf16[128,128]{1,0:T(8,128)(2,1)S(1)}, u32[]{:S(2)}, u32[]{:S(2)}) collective-permute-start(bf16[128,128]{1,0:T(8,128)(2,1)S(1)} %fusion), channel_id=1, source_target_pairs={{0,48},{2,50},{4,52},{6,54},{8,56},{10,58},{12,60},{14,62},{16,32}... | collective-permute-start | bytes 98312 | tf_op jit(solution)/shard_map/ppermute | solution.py:243
  71.0 1.0 %collective-permute-start.16 = (bf16[128,128]{1,0:T(8,128)(2,1)S(1)}, bf16[128,128]{1,0:T(8,128)(2,1)S(1)}, u32[]{:S(2)}, u32[]{:S(2)}) collective-permute-start(bf16[128,128]{1,0:T(8,128)(2,1)S(1)} %fusion), channel_id=1, source_target_pairs={{0,16},{2,18},{4,20},{6,22},{8,24},{10,26},{12,28},{14,30},{16,0},... | collective-permute-start | bytes 98312 | tf_op jit(solution)/shard_map/ppermute | solution.py:243
  72.0 0.9 %collective-permute-done.18 = bf16[128,128]{1,0:T(8,128)(2,1)S(1)} collective-permute-done((bf16[128,128]{1,0:T(8,128)(2,1)S(1)}, bf16[128,128]{1,0:T(8,128)(2,1)S(1)}, u32[]{:S(2)}, u32[]{:S(2)}) %collective-permute-start.18) | collective-permute-done | bytes 32800 | tf_op jit(solution)/shard_map/ppermute | solution.py:243
  72.9 3.5 %collective-permute-done.17 = bf16[128,128]{1,0:T(8,128)(2,1)S(1)} collective-permute-done((bf16[128,128]{1,0:T(8,128)(2,1)S(1)}, bf16[128,128]{1,0:T(8,128)(2,1)S(1)}, u32[]{:S(2)}, u32[]{:S(2)}) %collective-permute-start.17) | collective-permute-done | bytes 32800 | tf_op jit(solution)/shard_map/ppermute | solution.py:243
  76.5 5.4 %collective-permute-start.21 = (bf16[128,128]{1,0:T(8,128)(2,1)S(1)}, bf16[128,128]{1,0:T(8,128)(2,1)S(1)}, u32[]{:S(2)}, u32[]{:S(2)}) collective-permute-start(bf16[128,128]{1,0:T(8,128)(2,1)S(1)} %fusion.1), channel_id=1, source_target_pairs={{0,192},{2,194},{4,196},{6,198},{8,200},{10,202},{12,204},{14,206}... | collective-permute-start | bytes 98312 | tf_op jit(solution)/shard_map/ppermute | solution.py:243
  81.9 0.3 collective-permute-start.20
  82.2 0.7 collective-permute-start.19
  82.8 0.7 copy.7
  83.5 0.3 collective-permute-done.21
  83.8 3.5 %collective-permute-done.20 = bf16[128,128]{1,0:T(8,128)(2,1)S(1)} collective-permute-done((bf16[128,128]{1,0:T(8,128)(2,1)S(1)}, bf16[128,128]{1,0:T(8,128)(2,1)S(1)}, u32[]{:S(2)}, u32[]{:S(2)}) %collective-permute-start.20) | collective-permute-done | bytes 32800 | tf_op jit(solution)/shard_map/ppermute | solution.py:243
  87.3 0.6 fusion.3
  (17 shorter events, 0.3 us)
Async XLA Ops:
  0.6 9.6 %copy-start = (bf16[1280,64]{0,1:T(8,128)(2,1)S(1)}, bf16[1280,64]{0,1:T(8,128)(2,1)}, u32[]{:S(2)}) copy-start(bf16[1280,64]{0,1:T(8,128)(2,1)} %param.7) | copy-start | bytes 491524
  0.6 9.6 %collective-permute-start = (bf16[64,1280]{1,0:T(8,128)(2,1)}, bf16[64,1280]{1,0:T(8,128)(2,1)S(1)}, u32[]{:S(2)}, u32[]{:S(2)}) collective-permute-start(bf16[64,1280]{1,0:T(8,128)(2,1)} %bitcast.4), channel_id=1, source_target_pairs={{0,2},{2,0},{4,6},{6,4},{8,10},{10,8},{12,14},{14,12},{16,18},{18,... | collective-permute-start | bytes 491528 | tf_op jit(solution)/shard_map/ppermute | solution.py:230
  2.6 9.2 %collective-permute-start.1 = (bf16[64,1280]{1,0:T(8,128)(2,1)}, bf16[64,1280]{1,0:T(8,128)(2,1)S(1)}, u32[]{:S(2)}, u32[]{:S(2)}) collective-permute-start(bf16[64,1280]{1,0:T(8,128)(2,1)} %bitcast.5), channel_id=1, source_target_pairs={{2,4},{4,2},{6,8},{8,6},{10,12},{12,10},{14,16},{16,14},{18,20},{2... | collective-permute-start | bytes 491528 | tf_op jit(solution)/shard_map/ppermute | solution.py:230
  12.4 5.1 %collective-permute-start.2 = (bf16[64,1024]{1,0:T(8,128)(2,1)S(1)}, bf16[64,1024]{1,0:T(8,128)(2,1)S(1)}, u32[]{:S(2)}, u32[]{:S(2)}) collective-permute-start(bf16[64,1024]{1,0:T(8,128)(2,1)S(1)} %get-tuple-element.18), channel_id=1, source_target_pairs={{0,2},{2,0},{4,6},{6,4},{8,10},{10,8},{12,14},{14,12},{16,18},{18,... | collective-permute-start | bytes 393224 | tf_op jit(solution)/shard_map/ppermute | solution.py:230
  12.5 7.1 %collective-permute-start.3 = (bf16[64,1024]{1,0:T(8,128)(2,1)S(1)}, bf16[64,1024]{1,0:T(8,128)(2,1)S(1)}, u32[]{:S(2)}, u32[]{:S(2)}) collective-permute-start(bf16[64,1024]{1,0:T(8,128)(2,1)S(1)} %get-tuple-element.19), channel_id=1, source_target_pairs={{2,4},{4,2},{6,8},{8,6},{10,12},{12,10},{14,16},{16,14},{18,20},{2... | collective-permute-start | bytes 393224 | tf_op jit(solution)/shard_map/ppermute | solution.py:230
  20.1 5.1 %collective-permute-start.4 = (bf16[64,1024]{1,0:T(8,128)(2,1)S(1)}, bf16[64,1024]{1,0:T(8,128)(2,1)S(1)}, u32[]{:S(2)}, u32[]{:S(2)}) collective-permute-start(bf16[64,1024]{1,0:T(8,128)(2,1)S(1)} %get-tuple-element.21), channel_id=1, source_target_pairs={{0,2},{2,0},{4,6},{6,4},{8,10},{10,8},{12,14},{14,12},{16,18},{18,... | collective-permute-start | bytes 393224 | tf_op jit(solution)/shard_map/ppermute | solution.py:230
  20.2 6.5 %collective-permute-start.5 = (bf16[64,1024]{1,0:T(8,128)(2,1)S(1)}, bf16[64,1024]{1,0:T(8,128)(2,1)S(1)}, u32[]{:S(2)}, u32[]{:S(2)}) collective-permute-start(bf16[64,1024]{1,0:T(8,128)(2,1)S(1)} %get-tuple-element.22), channel_id=1, source_target_pairs={{2,4},{4,2},{6,8},{8,6},{10,12},{12,10},{14,16},{16,14},{18,20},{2... | collective-permute-start | bytes 393224 | tf_op jit(solution)/shard_map/ppermute | solution.py:230
  27.3 5.1 %collective-permute-start.6 = (bf16[64,1024]{1,0:T(8,128)(2,1)S(1)}, bf16[64,1024]{1,0:T(8,128)(2,1)S(1)}, u32[]{:S(2)}, u32[]{:S(2)}) collective-permute-start(bf16[64,1024]{1,0:T(8,128)(2,1)S(1)} %get-tuple-element.24), channel_id=1, source_target_pairs={{0,2},{2,0},{4,6},{6,4},{8,10},{10,8},{12,14},{14,12},{16,18},{18,... | collective-permute-start | bytes 393224 | tf_op jit(solution)/shard_map/ppermute | solution.py:230
  27.4 6.6 %collective-permute-start.7 = (bf16[64,1024]{1,0:T(8,128)(2,1)S(1)}, bf16[64,1024]{1,0:T(8,128)(2,1)S(1)}, u32[]{:S(2)}, u32[]{:S(2)}) collective-permute-start(bf16[64,1024]{1,0:T(8,128)(2,1)S(1)} %get-tuple-element.25), channel_id=1, source_target_pairs={{2,4},{4,2},{6,8},{8,6},{10,12},{12,10},{14,16},{16,14},{18,20},{2... | collective-permute-start | bytes 393224 | tf_op jit(solution)/shard_map/ppermute | solution.py:230
  34.6 5.2 %collective-permute-start.8 = (bf16[64,1024]{1,0:T(8,128)(2,1)S(1)}, bf16[64,1024]{1,0:T(8,128)(2,1)S(1)}, u32[]{:S(2)}, u32[]{:S(2)}) collective-permute-start(bf16[64,1024]{1,0:T(8,128)(2,1)S(1)} %get-tuple-element.27), channel_id=1, source_target_pairs={{0,2},{2,0},{4,6},{6,4},{8,10},{10,8},{12,14},{14,12},{16,18},{18,... | collective-permute-start | bytes 393224 | tf_op jit(solution)/shard_map/ppermute | solution.py:230
  34.8 6.5 %collective-permute-start.10 = (bf16[64,1024]{1,0:T(8,128)(2,1)S(1)}, bf16[64,1024]{1,0:T(8,128)(2,1)S(1)}, u32[]{:S(2)}, u32[]{:S(2)}) collective-permute-start(bf16[64,1024]{1,0:T(8,128)(2,1)S(1)} %get-tuple-element.30), channel_id=1, source_target_pairs={{2,4},{4,2},{6,8},{8,6},{10,12},{12,10},{14,16},{16,14},{18,20},{2... | collective-permute-start | bytes 393224 | tf_op jit(solution)/shard_map/ppermute | solution.py:230
  41.3 1.4 %collective-permute-start.9 = (bf16[64,1280]{1,0:T(8,128)(2,1)S(1)}, bf16[64,1280]{1,0:T(8,128)(2,1)S(1)}, u32[]{:S(2)}, u32[]{:S(2)}) collective-permute-start(bf16[64,1280]{1,0:T(8,128)(2,1)S(1)} %get-tuple-element.28.v_ref.own_ref), channel_id=1, source_target_pairs={{0,1},{1,0},{2,3},{3,2},{4,5},{5,4},{6,7},{7,6},{8,9},{9,8},{10,11... | collective-permute-start | bytes 491528 | tf_op jit(solution)/shard_map/ppermute | solution.py:234
  41.9 1.6 %collective-permute-start.11 = (bf16[64,1280]{1,0:T(8,128)(2,1)S(1)}, bf16[64,1280]{1,0:T(8,128)(2,1)S(1)}, u32[]{:S(2)}, u32[]{:S(2)}) collective-permute-start(bf16[64,1280]{1,0:T(8,128)(2,1)S(1)} %image.1.image_ref), channel_id=1, source_target_pairs={{0,1},{1,0},{2,3},{3,2},{4,5},{5,4},{6,7},{7,6},{8,9},{9,8},{10,11... | collective-permute-start | bytes 491528 | tf_op jit(solution)/shard_map/ppermute | solution.py:234
  43.9 4.6 %collective-permute-start.14 = (bf16[128,128]{1,0:T(8,128)(2,1)S(1)}, bf16[128,128]{1,0:T(8,128)(2,1)S(1)}, u32[]{:S(2)}, u32[]{:S(2)}) collective-permute-start(bf16[128,128]{1,0:T(8,128)(2,1)S(1)} %reduce-precision_convert_fusion), channel_id=1, source_target_pairs={{0,6},{2,4},{4,2},{6,0},{8,14},{10,12},{12,10},{14,8},{16,22},{18,... | collective-permute-start | bytes 98312 | tf_op jit(solution)/shard_map/ppermute | solution.py:243
  46.0 4.8 %collective-permute-start.13 = (bf16[128,128]{1,0:T(8,128)(2,1)S(1)}, bf16[128,128]{1,0:T(8,128)(2,1)S(1)}, u32[]{:S(2)}, u32[]{:S(2)}) collective-permute-start(bf16[128,128]{1,0:T(8,128)(2,1)S(1)} %reduce-precision_convert_fusion), channel_id=1, source_target_pairs={{0,4},{2,6},{4,0},{6,2},{8,12},{10,14},{12,8},{14,10},{16,20},{18,... | collective-permute-start | bytes 98312 | tf_op jit(solution)/shard_map/ppermute | solution.py:243
  47.2 4.4 %collective-permute-start.12 = (bf16[128,128]{1,0:T(8,128)(2,1)S(1)}, bf16[128,128]{1,0:T(8,128)(2,1)S(1)}, u32[]{:S(2)}, u32[]{:S(2)}) collective-permute-start(bf16[128,128]{1,0:T(8,128)(2,1)S(1)} %reduce-precision_convert_fusion), channel_id=1, source_target_pairs={{0,2},{2,0},{4,6},{6,4},{8,10},{10,8},{12,14},{14,12},{16,18},{18,... | collective-permute-start | bytes 98312 | tf_op jit(solution)/shard_map/ppermute | solution.py:243
  51.6 7.3 %collective-permute-start.15 = (bf16[128,128]{1,0:T(8,128)(2,1)S(1)}, bf16[128,128]{1,0:T(8,128)(2,1)S(1)}, u32[]{:S(2)}, u32[]{:S(2)}) collective-permute-start(bf16[128,128]{1,0:T(8,128)(2,1)S(1)} %get-tuple-element.31), channel_id=1, source_target_pairs={{0,12},{2,14},{4,8},{6,10},{8,4},{10,6},{12,0},{14,2},{16,28},{18,... | collective-permute-start | bytes 98312 | tf_op jit(solution)/shard_map/ppermute | solution.py:243
  58.9 14.1 %collective-permute-start.18 = (bf16[128,128]{1,0:T(8,128)(2,1)S(1)}, bf16[128,128]{1,0:T(8,128)(2,1)S(1)}, u32[]{:S(2)}, u32[]{:S(2)}) collective-permute-start(bf16[128,128]{1,0:T(8,128)(2,1)S(1)} %fusion), channel_id=1, source_target_pairs={{0,48},{2,50},{4,52},{6,54},{8,56},{10,58},{12,60},{14,62},{16,32}... | collective-permute-start | bytes 98312 | tf_op jit(solution)/shard_map/ppermute | solution.py:243
  71.0 5.4 %collective-permute-start.17 = (bf16[128,128]{1,0:T(8,128)(2,1)S(1)}, bf16[128,128]{1,0:T(8,128)(2,1)S(1)}, u32[]{:S(2)}, u32[]{:S(2)}) collective-permute-start(bf16[128,128]{1,0:T(8,128)(2,1)S(1)} %fusion), channel_id=1, source_target_pairs={{0,32},{2,34},{4,36},{6,38},{8,40},{10,42},{12,44},{14,46},{16,48}... | collective-permute-start | bytes 98312 | tf_op jit(solution)/shard_map/ppermute | solution.py:243
  71.0 5.4 %collective-permute-start.16 = (bf16[128,128]{1,0:T(8,128)(2,1)S(1)}, bf16[128,128]{1,0:T(8,128)(2,1)S(1)}, u32[]{:S(2)}, u32[]{:S(2)}) collective-permute-start(bf16[128,128]{1,0:T(8,128)(2,1)S(1)} %fusion), channel_id=1, source_target_pairs={{0,16},{2,18},{4,20},{6,22},{8,24},{10,26},{12,28},{14,30},{16,0},... | collective-permute-start | bytes 98312 | tf_op jit(solution)/shard_map/ppermute | solution.py:243
  76.5 7.3 %collective-permute-start.21 = (bf16[128,128]{1,0:T(8,128)(2,1)S(1)}, bf16[128,128]{1,0:T(8,128)(2,1)S(1)}, u32[]{:S(2)}, u32[]{:S(2)}) collective-permute-start(bf16[128,128]{1,0:T(8,128)(2,1)S(1)} %fusion.1), channel_id=1, source_target_pairs={{0,192},{2,194},{4,196},{6,198},{8,200},{10,202},{12,204},{14,206}... | collective-permute-start | bytes 98312 | tf_op jit(solution)/shard_map/ppermute | solution.py:243
  81.9 5.4 %collective-permute-start.20 = (bf16[128,128]{1,0:T(8,128)(2,1)S(1)}, bf16[128,128]{1,0:T(8,128)(2,1)S(1)}, u32[]{:S(2)}, u32[]{:S(2)}) collective-permute-start(bf16[128,128]{1,0:T(8,128)(2,1)S(1)} %fusion.1), channel_id=1, source_target_pairs={{0,128},{2,130},{4,132},{6,134},{8,136},{10,138},{12,140},{14,142}... | collective-permute-start | bytes 98312 | tf_op jit(solution)/shard_map/ppermute | solution.py:243
  82.2 5.1 %collective-permute-start.19 = (bf16[128,128]{1,0:T(8,128)(2,1)S(1)}, bf16[128,128]{1,0:T(8,128)(2,1)S(1)}, u32[]{:S(2)}, u32[]{:S(2)}) collective-permute-start(bf16[128,128]{1,0:T(8,128)(2,1)S(1)} %fusion.1), channel_id=1, source_target_pairs={{0,64},{2,66},{4,68},{6,70},{8,72},{10,74},{12,76},{14,78},{16,80}... | collective-permute-start | bytes 98312 | tf_op jit(solution)/shard_map/ppermute | solution.py:243

commit v7 on v6

--- a/solution.py
+++ b/solution.py
@@ -236,7 +236,7 @@
 
 def sum_over_rows(value):
     count = lax.axis_size(ROWS)
-    for distances in ((1, 2, 3), (6,), (8, 16, 24), (32, 64, 96)):
+    for distances in ((7,), (1, 2, 3), (8, 16, 24), (32, 64, 96)):
         own = lax.reduce_precision(value, exponent_bits=8, mantissa_bits=7)
         sent = own.astype(jnp.bfloat16)
         others = [

time: 88.3 us -> 87.1 us (0.986)
  starting transfers between devices: 49.5 us -> 47.4 us
  waiting for transfers between devices: 19.8 us -> 20.7 us
    ppermute x10, starting transfers between devices: 29.5 us -> 27.5 us  [sum_over_rows(): lax.ppermute(sent, ROWS, [(i, i ^ d) for i in range(count)])]
    ppermute x10, waiting for transfers between devices: 13.2 us -> 14.1 us  [sum_over_rows(): lax.ppermute(sent, ROWS, [(i, i ^ d) for i in range(count)])]
  transfers between devices with their start and end apart: 22 -> 22, of which waited for: 15 -> 16; matrix products, arithmetic and copies ran while one was open for 1% -> 1% of each run, Pallas kernels for 16% -> 16%
where the time goes in v7:
time: 87.1 us; the launch traced here: 86.9 us
  starting transfers between devices  47.4 us (54%)
  waiting for transfers between devices  20.7 us (24%)
  Pallas kernels  16.5 us (19%)
  local copies, waits for them, and re-layouts  1.3 us (1%)
    ppermute x10, starting transfers between devices, sum_over_rows(): lax.ppermute(sent, ROWS, [(i, i ^ d) for i in range(count)])  27.5 us
    ppermute x5, starting transfers between devices, exchange(): lax.ppermute(to_left, every, left)  16.8 us
    ppermute x10, waiting for transfers between devices, sum_over_rows(): lax.ppermute(sent, ROWS, [(i, i ^ d) for i in range(count)])  14.1 us
    pallas_call x10, Pallas kernels, in_vmem(): pl.pallas_call(kernel, out_shape=[pltpu.VMEM(s, d) for s, d in outs], in_...  10.4 us
    pallas_call x1, Pallas kernels, build_band(): pl.pallas_call(band_kernel, out_shape=pltpu.VMEM((block_rows * B, width),...  5.7 us
    ppermute x5, waiting for transfers between devices, exchange(): lax.ppermute(to_right, every, right)  4.96 us
    ppermute x5, starting transfers between devices, exchange(): lax.ppermute(to_right, every, right)  2.48 us
  transfers between devices with their start and end apart: 22, of which 16 were waited for; matrix products, arithmetic and copies ran while one was open for 1% of the time, Pallas kernels for 16%

profile of v7, /device:TPU:32, one launch (start us, length us, event | category | flops | bytes accessed | tf_op | source)
XLA Modules:
  0.0 86.9 jit_solution(3965788286532982907)
XLA Ops:
  0.6 1.9 %collective-permute-start = (bf16[64,1280]{1,0:T(8,128)(2,1)}, bf16[64,1280]{1,0:T(8,128)(2,1)S(1)}, u32[]{:S(2)}, u32[]{:S(2)}) collective-permute-start(bf16[64,1280]{1,0:T(8,128)(2,1)} %bitcast.4), channel_id=1, source_target_pairs={{0,2},{2,0},{4,6},{6,4},{8,10},{10,8},{12,14},{14,12},{16,18},{18,... | collective-permute-start | bytes 491528 | tf_op jit(solution)/shard_map/ppermute | solution.py:230
  2.6 2.0 %collective-permute-start.1 = (bf16[64,1280]{1,0:T(8,128)(2,1)}, bf16[64,1280]{1,0:T(8,128)(2,1)S(1)}, u32[]{:S(2)}, u32[]{:S(2)}) collective-permute-start(bf16[64,1280]{1,0:T(8,128)(2,1)} %bitcast.5), channel_id=1, source_target_pairs={{2,4},{4,2},{6,8},{8,6},{10,12},{12,10},{14,16},{16,14},{18,20},{2... | collective-permute-start | bytes 491528 | tf_op jit(solution)/shard_map/ppermute | solution.py:230
  4.6 5.7 %band.1.a_ref = bf16[1280,3456]{1,0:T(8,128)(2,1)S(1)} custom-call(s32[1,10]{1,0:T(1,128)} %bitcast.8, s32[10,32]{1,0:T(8,128)} %near_ref.1, bf16[10,32,128,128]{3,2,1,0:T(8,128)(2,1)} %h_ref.1), custom_call_target="tpu_custom_call" | custom-call | tf_op jit(solution)/shard_map/band/pallas_call | solution.py:89
  10.3 1.5 %near1.1.acc_ref = f32[64,1280]{1,0:T(8,128)S(1)} custom-call(bf16[64,1280]{1,0:T(8,128)(2,1)S(1)} %bitcast.6, bf16[64,1280]{1,0:T(8,128)(2,1)S(1)} %collective-permute-done.right_ref, bf16[1280,3456]{1,0:T(8,128)(2,1)S(1)} %band.1.a_ref), custom_call_target="tpu_custom_call" | custom-call | flops 314572800 | tf_op jit(solution)/shard_map/near1/pallas_call | solution.py:196
  11.9 0.6 level1.1
  12.5 4.0 %collective-permute-start.3 = (bf16[64,1024]{1,0:T(8,128)(2,1)S(1)}, bf16[64,1024]{1,0:T(8,128)(2,1)S(1)}, u32[]{:S(2)}, u32[]{:S(2)}) collective-permute-start(bf16[64,1024]{1,0:T(8,128)(2,1)S(1)} %get-tuple-element.19), channel_id=1, source_target_pairs={{2,4},{4,2},{6,8},{8,6},{10,12},{12,10},{14,16},{16,14},{18,20},{2... | collective-permute-start | bytes 393224 | tf_op jit(solution)/shard_map/ppermute | solution.py:230
  16.5 0.9 %collective-permute-done.2.right_ref = bf16[64,1024]{1,0:T(8,128)(2,1)S(1)} collective-permute-done((bf16[64,1024]{1,0:T(8,128)(2,1)S(1)}, bf16[64,1024]{1,0:T(8,128)(2,1)S(1)}, u32[]{:S(2)}, u32[]{:S(2)}) %collective-permute-start.2) | collective-permute-done | bytes 131104 | tf_op jit(solution)/shard_map/ppermute | solution.py:230
  17.5 1.5 %near2.1.acc_ref = f32[64,1280]{1,0:T(8,128)S(1)} custom-call(bf16[64,1280]{1,0:T(8,128)(2,1)S(1)} %get-tuple-element.17.v_ref.older_ref, bf16[64,1024]{1,0:T(8,128)(2,1)S(1)} %collective-permute-done.2.right_ref, bf16[1280,3456]{1,0:T(8,128)(2,1)S(1)} %band.1.a_ref, bf16[64,1280]{1,0:T(8,128)(2,1)S(1)} %bitcast.7), custom_call_target="tpu_custom_call" | custom-call | flops 314572800 | tf_op jit(solution)/shard_map/near2/pallas_call | solution.py:196
  19.0 0.5 collective-permute-done.3.left_ref
  19.5 0.5 level2.1
  20.0 0.1 collective-permute-start.4
  20.1 3.6 %collective-permute-start.5 = (bf16[64,1024]{1,0:T(8,128)(2,1)S(1)}, bf16[64,1024]{1,0:T(8,128)(2,1)S(1)}, u32[]{:S(2)}, u32[]{:S(2)}) collective-permute-start(bf16[64,1024]{1,0:T(8,128)(2,1)S(1)} %get-tuple-element.22), channel_id=1, source_target_pairs={{2,4},{4,2},{6,8},{8,6},{10,12},{12,10},{14,16},{16,14},{18,20},{2... | collective-permute-start | bytes 393224 | tf_op jit(solution)/shard_map/ppermute | solution.py:230
  23.7 1.4 %collective-permute-done.4.right_ref = bf16[64,1024]{1,0:T(8,128)(2,1)S(1)} collective-permute-done((bf16[64,1024]{1,0:T(8,128)(2,1)S(1)}, bf16[64,1024]{1,0:T(8,128)(2,1)S(1)}, u32[]{:S(2)}, u32[]{:S(2)}) %collective-permute-start.4) | collective-permute-done | bytes 131104 | tf_op jit(solution)/shard_map/ppermute | solution.py:230
  25.1 1.5 %near3.1.acc_ref = f32[64,1280]{1,0:T(8,128)S(1)} custom-call(bf16[64,1280]{1,0:T(8,128)(2,1)S(1)} %get-tuple-element.20.v_ref.older_ref, bf16[64,1024]{1,0:T(8,128)(2,1)S(1)} %collective-permute-done.4.right_ref, bf16[1280,3456]{1,0:T(8,128)(2,1)S(1)} %band.1.a_ref, bf16[64,1280]{1,0:T(8,128)(2,1)S(1)} %get-tuple-element.17.v_ref.older_ref), custom_call_target="tpu_custom_call" | custom-call | flops 314572800 | tf_op jit(solution)/shard_map/near3/pallas_call | solution.py:196
  26.7 0.5 level3.1
  27.2 0.1 collective-permute-start.6
  27.3 3.7 %collective-permute-start.7 = (bf16[64,1024]{1,0:T(8,128)(2,1)S(1)}, bf16[64,1024]{1,0:T(8,128)(2,1)S(1)}, u32[]{:S(2)}, u32[]{:S(2)}) collective-permute-start(bf16[64,1024]{1,0:T(8,128)(2,1)S(1)} %get-tuple-element.25), channel_id=1, source_target_pairs={{2,4},{4,2},{6,8},{8,6},{10,12},{12,10},{14,16},{16,14},{18,20},{2... | collective-permute-start | bytes 393224 | tf_op jit(solution)/shard_map/ppermute | solution.py:230
  31.0 1.3 %collective-permute-done.6.right_ref = bf16[64,1024]{1,0:T(8,128)(2,1)S(1)} collective-permute-done((bf16[64,1024]{1,0:T(8,128)(2,1)S(1)}, bf16[64,1024]{1,0:T(8,128)(2,1)S(1)}, u32[]{:S(2)}, u32[]{:S(2)}) %collective-permute-start.6) | collective-permute-done | bytes 131104 | tf_op jit(solution)/shard_map/ppermute | solution.py:230
  32.3 1.5 %near4.1.acc_ref = f32[64,1280]{1,0:T(8,128)S(1)} custom-call(bf16[64,1280]{1,0:T(8,128)(2,1)S(1)} %get-tuple-element.23.v_ref, bf16[64,1024]{1,0:T(8,128)(2,1)S(1)} %collective-permute-done.6.right_ref, bf16[1280,3456]{1,0:T(8,128)(2,1)S(1)} %band.1.a_ref, bf16[64,1280]{1,0:T(8,128)(2,1)S(1)} %get-tuple-element.20.v_ref.older_ref), custom_call_target="tpu_custom_call" | custom-call | flops 314572800 | tf_op jit(solution)/shard_map/near4/pallas_call | solution.py:196
  33.8 0.1 collective-permute-done.7.left_ref
  33.9 0.5 level4.1
  34.5 0.3 collective-permute-start.8
  34.8 3.6 %collective-permute-start.10 = (bf16[64,1024]{1,0:T(8,128)(2,1)S(1)}, bf16[64,1024]{1,0:T(8,128)(2,1)S(1)}, u32[]{:S(2)}, u32[]{:S(2)}) collective-permute-start(bf16[64,1024]{1,0:T(8,128)(2,1)S(1)} %get-tuple-element.30), channel_id=1, source_target_pairs={{2,4},{4,2},{6,8},{8,6},{10,12},{12,10},{14,16},{16,14},{18,20},{2... | collective-permute-start | bytes 393224 | tf_op jit(solution)/shard_map/ppermute | solution.py:230
  38.4 1.4 %collective-permute-done.8.right_ref = bf16[64,1024]{1,0:T(8,128)(2,1)S(1)} collective-permute-done((bf16[64,1024]{1,0:T(8,128)(2,1)S(1)}, bf16[64,1024]{1,0:T(8,128)(2,1)S(1)}, u32[]{:S(2)}, u32[]{:S(2)}) %collective-permute-start.8) | collective-permute-done | bytes 131104 | tf_op jit(solution)/shard_map/ppermute | solution.py:230
  39.7 1.5 %near5.1.acc_ref = f32[64,1280]{1,0:T(8,128)S(1)} custom-call(bf16[64,1280]{1,0:T(8,128)(2,1)S(1)} %get-tuple-element.28.v_ref.own_ref, bf16[64,1024]{1,0:T(8,128)(2,1)S(1)} %collective-permute-done.8.right_ref, bf16[1280,3456]{1,0:T(8,128)(2,1)S(1)} %band.1.a_ref), custom_call_target="tpu_custom_call" | custom-call | flops 314572800 | tf_op jit(solution)/shard_map/near5/pallas_call | solution.py:196
  41.3 0.5 image.1.image_ref
  41.9 0.6 collective-permute-start.11
  42.4 0.3 collective-permute-done.9.other_ref
  42.7 0.8 collective-permute-done.11.other_image_ref
  43.5 0.4 gram.1
  43.9 5.6 %collective-permute-start.12 = (bf16[128,128]{1,0:T(8,128)(2,1)S(1)}, bf16[128,128]{1,0:T(8,128)(2,1)S(1)}, u32[]{:S(2)}, u32[]{:S(2)}) collective-permute-start(bf16[128,128]{1,0:T(8,128)(2,1)S(1)} %reduce-precision_convert_fusion), channel_id=1, source_target_pairs={{0,14},{2,12},{4,10},{6,8},{8,6},{10,4},{12,2},{14,0},{16,30},{18,... | collective-permute-start | bytes 98312 | tf_op jit(solution)/shard_map/ppermute | solution.py:243
  49.4 1.9 %collective-permute-done.12 = bf16[128,128]{1,0:T(8,128)(2,1)S(1)} collective-permute-done((bf16[128,128]{1,0:T(8,128)(2,1)S(1)}, bf16[128,128]{1,0:T(8,128)(2,1)S(1)}, u32[]{:S(2)}, u32[]{:S(2)}) %collective-permute-start.12) | collective-permute-done | bytes 32800 | tf_op jit(solution)/shard_map/ppermute | solution.py:243
  51.3 1.7 %collective-permute-start.15 = (bf16[128,128]{1,0:T(8,128)(2,1)S(1)}, bf16[128,128]{1,0:T(8,128)(2,1)S(1)}, u32[]{:S(2)}, u32[]{:S(2)}) collective-permute-start(bf16[128,128]{1,0:T(8,128)(2,1)S(1)} %fusion), channel_id=1, source_target_pairs={{0,6},{2,4},{4,2},{6,0},{8,14},{10,12},{12,10},{14,8},{16,22},{18,... | collective-permute-start | bytes 98312 | tf_op jit(solution)/shard_map/ppermute | solution.py:243
  53.0 2.1 %collective-permute-start.14 = (bf16[128,128]{1,0:T(8,128)(2,1)S(1)}, bf16[128,128]{1,0:T(8,128)(2,1)S(1)}, u32[]{:S(2)}, u32[]{:S(2)}) collective-permute-start(bf16[128,128]{1,0:T(8,128)(2,1)S(1)} %fusion), channel_id=1, source_target_pairs={{0,4},{2,6},{4,0},{6,2},{8,12},{10,14},{12,8},{14,10},{16,20},{18,... | collective-permute-start | bytes 98312 | tf_op jit(solution)/shard_map/ppermute | solution.py:243
  55.1 0.9 %collective-permute-done.15 = bf16[128,128]{1,0:T(8,128)(2,1)S(1)} collective-permute-done((bf16[128,128]{1,0:T(8,128)(2,1)S(1)}, bf16[128,128]{1,0:T(8,128)(2,1)S(1)}, u32[]{:S(2)}, u32[]{:S(2)}) %collective-permute-start.15) | collective-permute-done | bytes 32800 | tf_op jit(solution)/shard_map/ppermute | solution.py:243
  56.1 1.8 %collective-permute-done.14 = bf16[128,128]{1,0:T(8,128)(2,1)S(1)} collective-permute-done((bf16[128,128]{1,0:T(8,128)(2,1)S(1)}, bf16[128,128]{1,0:T(8,128)(2,1)S(1)}, u32[]{:S(2)}, u32[]{:S(2)}) %collective-permute-start.14) | collective-permute-done | bytes 32800 | tf_op jit(solution)/shard_map/ppermute | solution.py:243
  57.8 1.2 %collective-permute-done.13 = bf16[128,128]{1,0:T(8,128)(2,1)S(1)} collective-permute-done((bf16[128,128]{1,0:T(8,128)(2,1)S(1)}, bf16[128,128]{1,0:T(8,128)(2,1)S(1)}, u32[]{:S(2)}, u32[]{:S(2)}) %collective-permute-start.13) | collective-permute-done | bytes 32800 | tf_op jit(solution)/shard_map/ppermute | solution.py:243
  59.1 12.5 %collective-permute-start.18 = (bf16[128,128]{1,0:T(8,128)(2,1)S(1)}, bf16[128,128]{1,0:T(8,128)(2,1)S(1)}, u32[]{:S(2)}, u32[]{:S(2)}) collective-permute-start(bf16[128,128]{1,0:T(8,128)(2,1)S(1)} %get-tuple-element.31), channel_id=1, source_target_pairs={{0,48},{2,50},{4,52},{6,54},{8,56},{10,58},{12,60},{14,62},{16,32}... | collective-permute-start | bytes 98312 | tf_op jit(solution)/shard_map/ppermute | solution.py:243
  71.6 1.0 %collective-permute-start.16 = (bf16[128,128]{1,0:T(8,128)(2,1)S(1)}, bf16[128,128]{1,0:T(8,128)(2,1)S(1)}, u32[]{:S(2)}, u32[]{:S(2)}) collective-permute-start(bf16[128,128]{1,0:T(8,128)(2,1)S(1)} %get-tuple-element.31), channel_id=1, source_target_pairs={{0,16},{2,18},{4,20},{6,22},{8,24},{10,26},{12,28},{14,30},{16,0},... | collective-permute-start | bytes 98312 | tf_op jit(solution)/shard_map/ppermute | solution.py:243
  72.6 1.1 %collective-permute-done.18 = bf16[128,128]{1,0:T(8,128)(2,1)S(1)} collective-permute-done((bf16[128,128]{1,0:T(8,128)(2,1)S(1)}, bf16[128,128]{1,0:T(8,128)(2,1)S(1)}, u32[]{:S(2)}, u32[]{:S(2)}) %collective-permute-start.18) | collective-permute-done | bytes 32800 | tf_op jit(solution)/shard_map/ppermute | solution.py:243
  73.7 3.3 %collective-permute-done.17 = bf16[128,128]{1,0:T(8,128)(2,1)S(1)} collective-permute-done((bf16[128,128]{1,0:T(8,128)(2,1)S(1)}, bf16[128,128]{1,0:T(8,128)(2,1)S(1)}, u32[]{:S(2)}, u32[]{:S(2)}) %collective-permute-start.17) | collective-permute-done | bytes 32800 | tf_op jit(solution)/shard_map/ppermute | solution.py:243
  77.0 3.7 %collective-permute-start.21 = (bf16[128,128]{1,0:T(8,128)(2,1)S(1)}, bf16[128,128]{1,0:T(8,128)(2,1)S(1)}, u32[]{:S(2)}, u32[]{:S(2)}) collective-permute-start(bf16[128,128]{1,0:T(8,128)(2,1)S(1)} %fusion.1), channel_id=1, source_target_pairs={{0,192},{2,194},{4,196},{6,198},{8,200},{10,202},{12,204},{14,206}... | collective-permute-start | bytes 98312 | tf_op jit(solution)/shard_map/ppermute | solution.py:243
  80.8 0.3 collective-permute-start.20
  81.1 0.6 collective-permute-start.19
  81.7 0.7 copy.7
  82.4 0.3 collective-permute-done.21
  82.7 3.5 %collective-permute-done.20 = bf16[128,128]{1,0:T(8,128)(2,1)S(1)} collective-permute-done((bf16[128,128]{1,0:T(8,128)(2,1)S(1)}, bf16[128,128]{1,0:T(8,128)(2,1)S(1)}, u32[]{:S(2)}, u32[]{:S(2)}) %collective-permute-start.20) | collective-permute-done | bytes 32800 | tf_op jit(solution)/shard_map/ppermute | solution.py:243
  86.2 0.6 fusion.3
  (17 shorter events, 0.3 us)
Async XLA Ops:
  0.6 9.7 %copy-start = (bf16[1280,64]{0,1:T(8,128)(2,1)S(1)}, bf16[1280,64]{0,1:T(8,128)(2,1)}, u32[]{:S(2)}) copy-start(bf16[1280,64]{0,1:T(8,128)(2,1)} %param.7) | copy-start | bytes 491524
  0.6 9.6 %collective-permute-start = (bf16[64,1280]{1,0:T(8,128)(2,1)}, bf16[64,1280]{1,0:T(8,128)(2,1)S(1)}, u32[]{:S(2)}, u32[]{:S(2)}) collective-permute-start(bf16[64,1280]{1,0:T(8,128)(2,1)} %bitcast.4), channel_id=1, source_target_pairs={{0,2},{2,0},{4,6},{6,4},{8,10},{10,8},{12,14},{14,12},{16,18},{18,... | collective-permute-start | bytes 491528 | tf_op jit(solution)/shard_map/ppermute | solution.py:230
  2.6 9.3 %collective-permute-start.1 = (bf16[64,1280]{1,0:T(8,128)(2,1)}, bf16[64,1280]{1,0:T(8,128)(2,1)S(1)}, u32[]{:S(2)}, u32[]{:S(2)}) collective-permute-start(bf16[64,1280]{1,0:T(8,128)(2,1)} %bitcast.5), channel_id=1, source_target_pairs={{2,4},{4,2},{6,8},{8,6},{10,12},{12,10},{14,16},{16,14},{18,20},{2... | collective-permute-start | bytes 491528 | tf_op jit(solution)/shard_map/ppermute | solution.py:230
  12.4 5.1 %collective-permute-start.2 = (bf16[64,1024]{1,0:T(8,128)(2,1)S(1)}, bf16[64,1024]{1,0:T(8,128)(2,1)S(1)}, u32[]{:S(2)}, u32[]{:S(2)}) collective-permute-start(bf16[64,1024]{1,0:T(8,128)(2,1)S(1)} %get-tuple-element.18), channel_id=1, source_target_pairs={{0,2},{2,0},{4,6},{6,4},{8,10},{10,8},{12,14},{14,12},{16,18},{18,... | collective-permute-start | bytes 393224 | tf_op jit(solution)/shard_map/ppermute | solution.py:230
  12.5 7.0 %collective-permute-start.3 = (bf16[64,1024]{1,0:T(8,128)(2,1)S(1)}, bf16[64,1024]{1,0:T(8,128)(2,1)S(1)}, u32[]{:S(2)}, u32[]{:S(2)}) collective-permute-start(bf16[64,1024]{1,0:T(8,128)(2,1)S(1)} %get-tuple-element.19), channel_id=1, source_target_pairs={{2,4},{4,2},{6,8},{8,6},{10,12},{12,10},{14,16},{16,14},{18,20},{2... | collective-permute-start | bytes 393224 | tf_op jit(solution)/shard_map/ppermute | solution.py:230
  20.0 5.1 %collective-permute-start.4 = (bf16[64,1024]{1,0:T(8,128)(2,1)S(1)}, bf16[64,1024]{1,0:T(8,128)(2,1)S(1)}, u32[]{:S(2)}, u32[]{:S(2)}) collective-permute-start(bf16[64,1024]{1,0:T(8,128)(2,1)S(1)} %get-tuple-element.21), channel_id=1, source_target_pairs={{0,2},{2,0},{4,6},{6,4},{8,10},{10,8},{12,14},{14,12},{16,18},{18,... | collective-permute-start | bytes 393224 | tf_op jit(solution)/shard_map/ppermute | solution.py:230
  20.1 6.5 %collective-permute-start.5 = (bf16[64,1024]{1,0:T(8,128)(2,1)S(1)}, bf16[64,1024]{1,0:T(8,128)(2,1)S(1)}, u32[]{:S(2)}, u32[]{:S(2)}) collective-permute-start(bf16[64,1024]{1,0:T(8,128)(2,1)S(1)} %get-tuple-element.22), channel_id=1, source_target_pairs={{2,4},{4,2},{6,8},{8,6},{10,12},{12,10},{14,16},{16,14},{18,20},{2... | collective-permute-start | bytes 393224 | tf_op jit(solution)/shard_map/ppermute | solution.py:230
  27.2 5.1 %collective-permute-start.6 = (bf16[64,1024]{1,0:T(8,128)(2,1)S(1)}, bf16[64,1024]{1,0:T(8,128)(2,1)S(1)}, u32[]{:S(2)}, u32[]{:S(2)}) collective-permute-start(bf16[64,1024]{1,0:T(8,128)(2,1)S(1)} %get-tuple-element.24), channel_id=1, source_target_pairs={{0,2},{2,0},{4,6},{6,4},{8,10},{10,8},{12,14},{14,12},{16,18},{18,... | collective-permute-start | bytes 393224 | tf_op jit(solution)/shard_map/ppermute | solution.py:230
  27.3 6.6 %collective-permute-start.7 = (bf16[64,1024]{1,0:T(8,128)(2,1)S(1)}, bf16[64,1024]{1,0:T(8,128)(2,1)S(1)}, u32[]{:S(2)}, u32[]{:S(2)}) collective-permute-start(bf16[64,1024]{1,0:T(8,128)(2,1)S(1)} %get-tuple-element.25), channel_id=1, source_target_pairs={{2,4},{4,2},{6,8},{8,6},{10,12},{12,10},{14,16},{16,14},{18,20},{2... | collective-permute-start | bytes 393224 | tf_op jit(solution)/shard_map/ppermute | solution.py:230
  34.5 5.2 %collective-permute-start.8 = (bf16[64,1024]{1,0:T(8,128)(2,1)S(1)}, bf16[64,1024]{1,0:T(8,128)(2,1)S(1)}, u32[]{:S(2)}, u32[]{:S(2)}) collective-permute-start(bf16[64,1024]{1,0:T(8,128)(2,1)S(1)} %get-tuple-element.27), channel_id=1, source_target_pairs={{0,2},{2,0},{4,6},{6,4},{8,10},{10,8},{12,14},{14,12},{16,18},{18,... | collective-permute-start | bytes 393224 | tf_op jit(solution)/shard_map/ppermute | solution.py:230
  34.8 6.5 %collective-permute-start.10 = (bf16[64,1024]{1,0:T(8,128)(2,1)S(1)}, bf16[64,1024]{1,0:T(8,128)(2,1)S(1)}, u32[]{:S(2)}, u32[]{:S(2)}) collective-permute-start(bf16[64,1024]{1,0:T(8,128)(2,1)S(1)} %get-tuple-element.30), channel_id=1, source_target_pairs={{2,4},{4,2},{6,8},{8,6},{10,12},{12,10},{14,16},{16,14},{18,20},{2... | collective-permute-start | bytes 393224 | tf_op jit(solution)/shard_map/ppermute | solution.py:230
  41.3 1.4 %collective-permute-start.9 = (bf16[64,1280]{1,0:T(8,128)(2,1)S(1)}, bf16[64,1280]{1,0:T(8,128)(2,1)S(1)}, u32[]{:S(2)}, u32[]{:S(2)}) collective-permute-start(bf16[64,1280]{1,0:T(8,128)(2,1)S(1)} %get-tuple-element.28.v_ref.own_ref), channel_id=1, source_target_pairs={{0,1},{1,0},{2,3},{3,2},{4,5},{5,4},{6,7},{7,6},{8,9},{9,8},{10,11... | collective-permute-start | bytes 491528 | tf_op jit(solution)/shard_map/ppermute | solution.py:234
  41.9 1.6 %collective-permute-start.11 = (bf16[64,1280]{1,0:T(8,128)(2,1)S(1)}, bf16[64,1280]{1,0:T(8,128)(2,1)S(1)}, u32[]{:S(2)}, u32[]{:S(2)}) collective-permute-start(bf16[64,1280]{1,0:T(8,128)(2,1)S(1)} %image.1.image_ref), channel_id=1, source_target_pairs={{0,1},{1,0},{2,3},{3,2},{4,5},{5,4},{6,7},{7,6},{8,9},{9,8},{10,11... | collective-permute-start | bytes 491528 | tf_op jit(solution)/shard_map/ppermute | solution.py:234
  43.9 7.5 %collective-permute-start.12 = (bf16[128,128]{1,0:T(8,128)(2,1)S(1)}, bf16[128,128]{1,0:T(8,128)(2,1)S(1)}, u32[]{:S(2)}, u32[]{:S(2)}) collective-permute-start(bf16[128,128]{1,0:T(8,128)(2,1)S(1)} %reduce-precision_convert_fusion), channel_id=1, source_target_pairs={{0,14},{2,12},{4,10},{6,8},{8,6},{10,4},{12,2},{14,0},{16,30},{18,... | collective-permute-start | bytes 98312 | tf_op jit(solution)/shard_map/ppermute | solution.py:243
  51.3 4.7 %collective-permute-start.15 = (bf16[128,128]{1,0:T(8,128)(2,1)S(1)}, bf16[128,128]{1,0:T(8,128)(2,1)S(1)}, u32[]{:S(2)}, u32[]{:S(2)}) collective-permute-start(bf16[128,128]{1,0:T(8,128)(2,1)S(1)} %fusion), channel_id=1, source_target_pairs={{0,6},{2,4},{4,2},{6,0},{8,14},{10,12},{12,10},{14,8},{16,22},{18,... | collective-permute-start | bytes 98312 | tf_op jit(solution)/shard_map/ppermute | solution.py:243
  53.0 4.8 %collective-permute-start.14 = (bf16[128,128]{1,0:T(8,128)(2,1)S(1)}, bf16[128,128]{1,0:T(8,128)(2,1)S(1)}, u32[]{:S(2)}, u32[]{:S(2)}) collective-permute-start(bf16[128,128]{1,0:T(8,128)(2,1)S(1)} %fusion), channel_id=1, source_target_pairs={{0,4},{2,6},{4,0},{6,2},{8,12},{10,14},{12,8},{14,10},{16,20},{18,... | collective-permute-start | bytes 98312 | tf_op jit(solution)/shard_map/ppermute | solution.py:243
  55.1 3.9 %collective-permute-start.13 = (bf16[128,128]{1,0:T(8,128)(2,1)S(1)}, bf16[128,128]{1,0:T(8,128)(2,1)S(1)}, u32[]{:S(2)}, u32[]{:S(2)}) collective-permute-start(bf16[128,128]{1,0:T(8,128)(2,1)S(1)} %fusion), channel_id=1, source_target_pairs={{0,2},{2,0},{4,6},{6,4},{8,10},{10,8},{12,14},{14,12},{16,18},{18,... | collective-permute-start | bytes 98312 | tf_op jit(solution)/shard_map/ppermute | solution.py:243
  59.1 14.6 %collective-permute-start.18 = (bf16[128,128]{1,0:T(8,128)(2,1)S(1)}, bf16[128,128]{1,0:T(8,128)(2,1)S(1)}, u32[]{:S(2)}, u32[]{:S(2)}) collective-permute-start(bf16[128,128]{1,0:T(8,128)(2,1)S(1)} %get-tuple-element.31), channel_id=1, source_target_pairs={{0,48},{2,50},{4,52},{6,54},{8,56},{10,58},{12,60},{14,62},{16,32}... | collective-permute-start | bytes 98312 | tf_op jit(solution)/shard_map/ppermute | solution.py:243
  71.6 5.4 %collective-permute-start.17 = (bf16[128,128]{1,0:T(8,128)(2,1)S(1)}, bf16[128,128]{1,0:T(8,128)(2,1)S(1)}, u32[]{:S(2)}, u32[]{:S(2)}) collective-permute-start(bf16[128,128]{1,0:T(8,128)(2,1)S(1)} %get-tuple-element.31), channel_id=1, source_target_pairs={{0,32},{2,34},{4,36},{6,38},{8,40},{10,42},{12,44},{14,46},{16,48}... | collective-permute-start | bytes 98312 | tf_op jit(solution)/shard_map/ppermute | solution.py:243
  71.6 5.4 %collective-permute-start.16 = (bf16[128,128]{1,0:T(8,128)(2,1)S(1)}, bf16[128,128]{1,0:T(8,128)(2,1)S(1)}, u32[]{:S(2)}, u32[]{:S(2)}) collective-permute-start(bf16[128,128]{1,0:T(8,128)(2,1)S(1)} %get-tuple-element.31), channel_id=1, source_target_pairs={{0,16},{2,18},{4,20},{6,22},{8,24},{10,26},{12,28},{14,30},{16,0},... | collective-permute-start | bytes 98312 | tf_op jit(solution)/shard_map/ppermute | solution.py:243
  77.0 5.6 %collective-permute-start.21 = (bf16[128,128]{1,0:T(8,128)(2,1)S(1)}, bf16[128,128]{1,0:T(8,128)(2,1)S(1)}, u32[]{:S(2)}, u32[]{:S(2)}) collective-permute-start(bf16[128,128]{1,0:T(8,128)(2,1)S(1)} %fusion.1), channel_id=1, source_target_pairs={{0,192},{2,194},{4,196},{6,198},{8,200},{10,202},{12,204},{14,206}... | collective-permute-start | bytes 98312 | tf_op jit(solution)/shard_map/ppermute | solution.py:243
  80.8 5.4 %collective-permute-start.20 = (bf16[128,128]{1,0:T(8,128)(2,1)S(1)}, bf16[128,128]{1,0:T(8,128)(2,1)S(1)}, u32[]{:S(2)}, u32[]{:S(2)}) collective-permute-start(bf16[128,128]{1,0:T(8,128)(2,1)S(1)} %fusion.1), channel_id=1, source_target_pairs={{0,128},{2,130},{4,132},{6,134},{8,136},{10,138},{12,140},{14,142}... | collective-permute-start | bytes 98312 | tf_op jit(solution)/shard_map/ppermute | solution.py:243
  81.1 5.1 %collective-permute-start.19 = (bf16[128,128]{1,0:T(8,128)(2,1)S(1)}, bf16[128,128]{1,0:T(8,128)(2,1)S(1)}, u32[]{:S(2)}, u32[]{:S(2)}) collective-permute-start(bf16[128,128]{1,0:T(8,128)(2,1)S(1)} %fusion.1), channel_id=1, source_target_pairs={{0,64},{2,66},{4,68},{6,70},{8,72},{10,74},{12,76},{14,78},{16,80}... | collective-permute-start | bytes 98312 | tf_op jit(solution)/shard_map/ppermute | solution.py:243

commit v8 on v7

--- a/solution.py
+++ b/solution.py
@@ -147,6 +147,13 @@
     near_kernel(v_ref, right_ref, a_ref, acc_ref, older_ref)
 
 
+def near_last_kernel(v_ref, right_ref, a_ref, acc_ref, copy_ref, sem):
+    out = pltpu.make_async_copy(v_ref, copy_ref, sem)
+    out.start()
+    near_kernel(v_ref, right_ref, a_ref, acc_ref)
+    out.wait()
+
+
 def finish(acc_ref, left_ref, a_ref, new_ref, scale=1.0):
     rows = acc_ref.shape[1]
     step = 2 * B
@@ -276,7 +283,17 @@
         )
         older, newer = newer, latest
     right, left = exchange(*edges)
-    acc, mine = lax.optimization_barrier((near(newer, right, "near5"), newer))
+    acc, filtered = pl.pallas_call(
+        near_last_kernel,
+        out_shape=[pltpu.VMEM(*part), pltpu.HBM(*field)],
+        in_specs=[pl.BlockSpec(memory_space=pltpu.VMEM)] * 3,
+        out_specs=[pl.BlockSpec(memory_space=pltpu.VMEM), pl.BlockSpec(memory_space=pltpu.HBM)],
+        scratch_shapes=[pltpu.SemaphoreType.DMA],
+        compiler_params=pltpu.CompilerParams(vmem_limit_bytes=16 * MIB),
+        cost_estimate=pl.CostEstimate(flops=near_flops, bytes_accessed=0, transcendentals=0),
+        name="near5",
+    )(newer, right, band)
+    acc, mine = lax.optimization_barrier((acc, newer))
     other = from_other_core(mine)
     (image,) = in_vmem(image_kernel, "image", [field], acc, left, band)
     other_image = from_other_core(image)
@@ -289,7 +306,7 @@
         name="gram",
     )(newer, other, image, other_image)
     sums = sum_over_rows(sums) * (1.0 / (rows * lax.axis_size(ROWS)))
-    return newer.T, sums[:width], sums[width:]
+    return filtered.T, sums[:width], sums[width:]
 
 
 def solution(mesh):

time: 87.1 us -> 86.9 us (level)
    pallas_call x0 -> x1, Pallas kernels: none -> 1.55 us  [body(): pl.pallas_call(near_last_kernel, out_shape=[pltpu.VMEM(*part), pltpu.HBM(...]
    pallas_call x10 -> x9, Pallas kernels: 10.4 us -> 8.9 us  [in_vmem(): pl.pallas_call(kernel, out_shape=[pltpu.VMEM(s, d) for s, d in outs], in_...]
  transfers between devices with their start and end apart: 22 -> 22, of which waited for: 16 -> 16; matrix products, arithmetic and copies ran while one was open for 1% -> 0% of each run, Pallas kernels for 16% -> 16%
where the time goes in v8:
time: 86.9 us; the launch traced here: 86.7 us
  starting transfers between devices  47.9 us (55%)
  waiting for transfers between devices  21.2 us (24%)
  Pallas kernels  16 us (18%)
    ppermute x10, starting transfers between devices, sum_over_rows(): lax.ppermute(sent, ROWS, [(i, i ^ d) for i in range(count)])  27.3 us
    ppermute x5, starting transfers between devices, exchange(): lax.ppermute(to_left, every, left)  17.5 us
    ppermute x10, waiting for transfers between devices, sum_over_rows(): lax.ppermute(sent, ROWS, [(i, i ^ d) for i in range(count)])  14.6 us
    pallas_call x9, Pallas kernels, in_vmem(): pl.pallas_call(kernel, out_shape=[pltpu.VMEM(s, d) for s, d in outs], in_...  8.9 us
    pallas_call x1, Pallas kernels, build_band(): pl.pallas_call(band_kernel, out_shape=pltpu.VMEM((block_rows * B, width),...  5.21 us
    ppermute x5, waiting for transfers between devices, exchange(): lax.ppermute(to_right, every, right)  4.26 us
    ppermute x5, starting transfers between devices, exchange(): lax.ppermute(to_right, every, right)  2.48 us
  transfers between devices with their start and end apart: 22, of which 16 were waited for; matrix products, arithmetic and copies ran while one was open for 0% of the time, Pallas kernels for 16%

profile of v8, /device:TPU:32, one launch (start us, length us, event | category | flops | bytes accessed | tf_op | source)
XLA Modules:
  0.0 86.7 jit_solution(16557243557865146577)
XLA Ops:
  0.6 1.9 %collective-permute-start = (bf16[64,1280]{1,0:T(8,128)(2,1)}, bf16[64,1280]{1,0:T(8,128)(2,1)S(1)}, u32[]{:S(2)}, u32[]{:S(2)}) collective-permute-start(bf16[64,1280]{1,0:T(8,128)(2,1)} %bitcast.3), channel_id=1, source_target_pairs={{0,2},{2,0},{4,6},{6,4},{8,10},{10,8},{12,14},{14,12},{16,18},{18,... | collective-permute-start | bytes 491528 | tf_op jit(solution)/shard_map/ppermute | solution.py:237
  2.6 2.0 %collective-permute-start.1 = (bf16[64,1280]{1,0:T(8,128)(2,1)}, bf16[64,1280]{1,0:T(8,128)(2,1)S(1)}, u32[]{:S(2)}, u32[]{:S(2)}) collective-permute-start(bf16[64,1280]{1,0:T(8,128)(2,1)} %bitcast.4), channel_id=1, source_target_pairs={{2,4},{4,2},{6,8},{8,6},{10,12},{12,10},{14,16},{16,14},{18,20},{2... | collective-permute-start | bytes 491528 | tf_op jit(solution)/shard_map/ppermute | solution.py:237
  4.6 5.2 %band.1.a_ref = bf16[1280,3456]{1,0:T(8,128)(2,1)S(1)} custom-call(s32[1,10]{1,0:T(1,128)} %bitcast.7, s32[10,32]{1,0:T(8,128)} %near_ref.1, bf16[10,32,128,128]{3,2,1,0:T(8,128)(2,1)} %h_ref.1), custom_call_target="tpu_custom_call" | custom-call | tf_op jit(solution)/shard_map/band/pallas_call | solution.py:89
  9.8 1.5 %near1.1.acc_ref = f32[64,1280]{1,0:T(8,128)S(1)} custom-call(bf16[64,1280]{1,0:T(8,128)(2,1)S(1)} %bitcast.5, bf16[64,1280]{1,0:T(8,128)(2,1)S(1)} %collective-permute-done.right_ref, bf16[1280,3456]{1,0:T(8,128)(2,1)S(1)} %band.1.a_ref), custom_call_target="tpu_custom_call" | custom-call | flops 314572800 | tf_op jit(solution)/shard_map/near1/pallas_call | solution.py:203
  11.4 0.6 level1.1
  11.9 0.1 collective-permute-start.2
  12.0 4.7 %collective-permute-start.3 = (bf16[64,1024]{1,0:T(8,128)(2,1)S(1)}, bf16[64,1024]{1,0:T(8,128)(2,1)S(1)}, u32[]{:S(2)}, u32[]{:S(2)}) collective-permute-start(bf16[64,1024]{1,0:T(8,128)(2,1)S(1)} %get-tuple-element.21), channel_id=1, source_target_pairs={{2,4},{4,2},{6,8},{8,6},{10,12},{12,10},{14,16},{16,14},{18,20},{2... | collective-permute-start | bytes 393224 | tf_op jit(solution)/shard_map/ppermute | solution.py:237
  16.8 0.2 collective-permute-done.2.right_ref
  17.0 1.5 %near2.1.acc_ref = f32[64,1280]{1,0:T(8,128)S(1)} custom-call(bf16[64,1280]{1,0:T(8,128)(2,1)S(1)} %get-tuple-element.19.v_ref.older_ref, bf16[64,1024]{1,0:T(8,128)(2,1)S(1)} %collective-permute-done.2.right_ref, bf16[1280,3456]{1,0:T(8,128)(2,1)S(1)} %band.1.a_ref, bf16[64,1280]{1,0:T(8,128)(2,1)S(1)} %bitcast.6), custom_call_target="tpu_custom_call" | custom-call | flops 314572800 | tf_op jit(solution)/shard_map/near2/pallas_call | solution.py:203
  18.5 1.2 %collective-permute-done.3.left_ref = bf16[64,1024]{1,0:T(8,128)(2,1)S(1)} collective-permute-done((bf16[64,1024]{1,0:T(8,128)(2,1)S(1)}, bf16[64,1024]{1,0:T(8,128)(2,1)S(1)}, u32[]{:S(2)}, u32[]{:S(2)}) %collective-permute-start.3) | collective-permute-done | bytes 131104 | tf_op jit(solution)/shard_map/ppermute | solution.py:237
  19.7 0.5 level2.1
  20.2 0.1 collective-permute-start.4
  20.3 3.6 %collective-permute-start.5 = (bf16[64,1024]{1,0:T(8,128)(2,1)S(1)}, bf16[64,1024]{1,0:T(8,128)(2,1)S(1)}, u32[]{:S(2)}, u32[]{:S(2)}) collective-permute-start(bf16[64,1024]{1,0:T(8,128)(2,1)S(1)} %get-tuple-element.24), channel_id=1, source_target_pairs={{2,4},{4,2},{6,8},{8,6},{10,12},{12,10},{14,16},{16,14},{18,20},{2... | collective-permute-start | bytes 393224 | tf_op jit(solution)/shard_map/ppermute | solution.py:237
  23.9 1.4 %collective-permute-done.4.right_ref = bf16[64,1024]{1,0:T(8,128)(2,1)S(1)} collective-permute-done((bf16[64,1024]{1,0:T(8,128)(2,1)S(1)}, bf16[64,1024]{1,0:T(8,128)(2,1)S(1)}, u32[]{:S(2)}, u32[]{:S(2)}) %collective-permute-start.4) | collective-permute-done | bytes 131104 | tf_op jit(solution)/shard_map/ppermute | solution.py:237
  25.3 1.5 %near3.1.acc_ref = f32[64,1280]{1,0:T(8,128)S(1)} custom-call(bf16[64,1280]{1,0:T(8,128)(2,1)S(1)} %get-tuple-element.22.v_ref.older_ref, bf16[64,1024]{1,0:T(8,128)(2,1)S(1)} %collective-permute-done.4.right_ref, bf16[1280,3456]{1,0:T(8,128)(2,1)S(1)} %band.1.a_ref, bf16[64,1280]{1,0:T(8,128)(2,1)S(1)} %get-tuple-element.19.v_ref.older_ref), custom_call_target="tpu_custom_call" | custom-call | flops 314572800 | tf_op jit(solution)/shard_map/near3/pallas_call | solution.py:203
  26.9 0.5 level3.1
  27.4 0.1 collective-permute-start.6
  27.5 3.7 %collective-permute-start.7 = (bf16[64,1024]{1,0:T(8,128)(2,1)S(1)}, bf16[64,1024]{1,0:T(8,128)(2,1)S(1)}, u32[]{:S(2)}, u32[]{:S(2)}) collective-permute-start(bf16[64,1024]{1,0:T(8,128)(2,1)S(1)} %get-tuple-element.27), channel_id=1, source_target_pairs={{2,4},{4,2},{6,8},{8,6},{10,12},{12,10},{14,16},{16,14},{18,20},{2... | collective-permute-start | bytes 393224 | tf_op jit(solution)/shard_map/ppermute | solution.py:237
  31.2 1.3 %collective-permute-done.6.right_ref = bf16[64,1024]{1,0:T(8,128)(2,1)S(1)} collective-permute-done((bf16[64,1024]{1,0:T(8,128)(2,1)S(1)}, bf16[64,1024]{1,0:T(8,128)(2,1)S(1)}, u32[]{:S(2)}, u32[]{:S(2)}) %collective-permute-start.6) | collective-permute-done | bytes 131104 | tf_op jit(solution)/shard_map/ppermute | solution.py:237
  32.5 1.5 %near4.1.acc_ref = f32[64,1280]{1,0:T(8,128)S(1)} custom-call(bf16[64,1280]{1,0:T(8,128)(2,1)S(1)} %get-tuple-element.25.v_ref, bf16[64,1024]{1,0:T(8,128)(2,1)S(1)} %collective-permute-done.6.right_ref, bf16[1280,3456]{1,0:T(8,128)(2,1)S(1)} %band.1.a_ref, bf16[64,1280]{1,0:T(8,128)(2,1)S(1)} %get-tuple-element.22.v_ref.older_ref), custom_call_target="tpu_custom_call" | custom-call | flops 314572800 | tf_op jit(solution)/shard_map/near4/pallas_call | solution.py:203
  34.0 0.1 collective-permute-done.7.left_ref
  34.1 0.5 level4.1
  34.7 0.3 collective-permute-start.8
  35.0 3.6 %collective-permute-start.10 = (bf16[64,1024]{1,0:T(8,128)(2,1)S(1)}, bf16[64,1024]{1,0:T(8,128)(2,1)S(1)}, u32[]{:S(2)}, u32[]{:S(2)}) collective-permute-start(bf16[64,1024]{1,0:T(8,128)(2,1)S(1)} %get-tuple-element.34), channel_id=1, source_target_pairs={{2,4},{4,2},{6,8},{8,6},{10,12},{12,10},{14,16},{16,14},{18,20},{2... | collective-permute-start | bytes 393224 | tf_op jit(solution)/shard_map/ppermute | solution.py:237
  38.6 1.4 %collective-permute-done.8.right_ref = bf16[64,1024]{1,0:T(8,128)(2,1)S(1)} collective-permute-done((bf16[64,1024]{1,0:T(8,128)(2,1)S(1)}, bf16[64,1024]{1,0:T(8,128)(2,1)S(1)}, u32[]{:S(2)}, u32[]{:S(2)}) %collective-permute-start.8) | collective-permute-done | bytes 131104 | tf_op jit(solution)/shard_map/ppermute | solution.py:237
  39.9 1.6 %near5.1 = (f32[64,1280]{1,0:T(8,128)S(1)}, bf16[64,1280]{1,0:T(8,128)(2,1)}) custom-call(bf16[64,1280]{1,0:T(8,128)(2,1)S(1)} %get-tuple-element.32.v_ref.own_ref, bf16[64,1024]{1,0:T(8,128)(2,1)S(1)} %collective-permute-done.8.right_ref, bf16[1280,3456]{1,0:T(8,128)(2,1)S(1)} %band.1.a_ref), custom_call_target="tpu_custom_call" | custom-call | flops 314572800 | tf_op jit(solution)/shard_map/near5/pallas_call | solution.py:286
  41.5 0.1 collective-permute-start.9
  41.6 0.5 image.1.image_ref
  42.2 0.6 collective-permute-start.11
  42.7 0.3 collective-permute-done.9.other_ref
  43.0 0.8 collective-permute-done.11.other_image_ref
  43.8 0.4 gram.1
  44.2 5.5 %collective-permute-start.12 = (bf16[128,128]{1,0:T(8,128)(2,1)S(1)}, bf16[128,128]{1,0:T(8,128)(2,1)S(1)}, u32[]{:S(2)}, u32[]{:S(2)}) collective-permute-start(bf16[128,128]{1,0:T(8,128)(2,1)S(1)} %reduce-precision_convert_fusion), channel_id=1, source_target_pairs={{0,14},{2,12},{4,10},{6,8},{8,6},{10,4},{12,2},{14,0},{16,30},{18,... | collective-permute-start | bytes 98312 | tf_op jit(solution)/shard_map/ppermute | solution.py:250
  49.6 1.9 %collective-permute-done.12 = bf16[128,128]{1,0:T(8,128)(2,1)S(1)} collective-permute-done((bf16[128,128]{1,0:T(8,128)(2,1)S(1)}, bf16[128,128]{1,0:T(8,128)(2,1)S(1)}, u32[]{:S(2)}, u32[]{:S(2)}) %collective-permute-start.12) | collective-permute-done | bytes 32800 | tf_op jit(solution)/shard_map/ppermute | solution.py:250
  51.5 1.7 %collective-permute-start.15 = (bf16[128,128]{1,0:T(8,128)(2,1)S(1)}, bf16[128,128]{1,0:T(8,128)(2,1)S(1)}, u32[]{:S(2)}, u32[]{:S(2)}) collective-permute-start(bf16[128,128]{1,0:T(8,128)(2,1)S(1)} %fusion), channel_id=1, source_target_pairs={{0,6},{2,4},{4,2},{6,0},{8,14},{10,12},{12,10},{14,8},{16,22},{18,... | collective-permute-start | bytes 98312 | tf_op jit(solution)/shard_map/ppermute | solution.py:250
  53.3 2.0 %collective-permute-start.14 = (bf16[128,128]{1,0:T(8,128)(2,1)S(1)}, bf16[128,128]{1,0:T(8,128)(2,1)S(1)}, u32[]{:S(2)}, u32[]{:S(2)}) collective-permute-start(bf16[128,128]{1,0:T(8,128)(2,1)S(1)} %fusion), channel_id=1, source_target_pairs={{0,4},{2,6},{4,0},{6,2},{8,12},{10,14},{12,8},{14,10},{16,20},{18,... | collective-permute-start | bytes 98312 | tf_op jit(solution)/shard_map/ppermute | solution.py:250
  55.3 1.0 %collective-permute-done.15 = bf16[128,128]{1,0:T(8,128)(2,1)S(1)} collective-permute-done((bf16[128,128]{1,0:T(8,128)(2,1)S(1)}, bf16[128,128]{1,0:T(8,128)(2,1)S(1)}, u32[]{:S(2)}, u32[]{:S(2)}) %collective-permute-start.15) | collective-permute-done | bytes 32800 | tf_op jit(solution)/shard_map/ppermute | solution.py:250
  56.3 1.8 %collective-permute-done.14 = bf16[128,128]{1,0:T(8,128)(2,1)S(1)} collective-permute-done((bf16[128,128]{1,0:T(8,128)(2,1)S(1)}, bf16[128,128]{1,0:T(8,128)(2,1)S(1)}, u32[]{:S(2)}, u32[]{:S(2)}) %collective-permute-start.14) | collective-permute-done | bytes 32800 | tf_op jit(solution)/shard_map/ppermute | solution.py:250
  58.1 1.1 %collective-permute-done.13 = bf16[128,128]{1,0:T(8,128)(2,1)S(1)} collective-permute-done((bf16[128,128]{1,0:T(8,128)(2,1)S(1)}, bf16[128,128]{1,0:T(8,128)(2,1)S(1)}, u32[]{:S(2)}, u32[]{:S(2)}) %collective-permute-start.13) | collective-permute-done | bytes 32800 | tf_op jit(solution)/shard_map/ppermute | solution.py:250
  59.3 12.3 %collective-permute-start.18 = (bf16[128,128]{1,0:T(8,128)(2,1)S(1)}, bf16[128,128]{1,0:T(8,128)(2,1)S(1)}, u32[]{:S(2)}, u32[]{:S(2)}) collective-permute-start(bf16[128,128]{1,0:T(8,128)(2,1)S(1)} %get-tuple-element.35), channel_id=1, source_target_pairs={{0,48},{2,50},{4,52},{6,54},{8,56},{10,58},{12,60},{14,62},{16,32}... | collective-permute-start | bytes 98312 | tf_op jit(solution)/shard_map/ppermute | solution.py:250
  71.6 1.0 %collective-permute-start.16 = (bf16[128,128]{1,0:T(8,128)(2,1)S(1)}, bf16[128,128]{1,0:T(8,128)(2,1)S(1)}, u32[]{:S(2)}, u32[]{:S(2)}) collective-permute-start(bf16[128,128]{1,0:T(8,128)(2,1)S(1)} %get-tuple-element.35), channel_id=1, source_target_pairs={{0,16},{2,18},{4,20},{6,22},{8,24},{10,26},{12,28},{14,30},{16,0},... | collective-permute-start | bytes 98312 | tf_op jit(solution)/shard_map/ppermute | solution.py:250
  72.6 1.1 %collective-permute-done.18 = bf16[128,128]{1,0:T(8,128)(2,1)S(1)} collective-permute-done((bf16[128,128]{1,0:T(8,128)(2,1)S(1)}, bf16[128,128]{1,0:T(8,128)(2,1)S(1)}, u32[]{:S(2)}, u32[]{:S(2)}) %collective-permute-start.18) | collective-permute-done | bytes 32800 | tf_op jit(solution)/shard_map/ppermute | solution.py:250
  73.7 3.3 %collective-permute-done.17 = bf16[128,128]{1,0:T(8,128)(2,1)S(1)} collective-permute-done((bf16[128,128]{1,0:T(8,128)(2,1)S(1)}, bf16[128,128]{1,0:T(8,128)(2,1)S(1)}, u32[]{:S(2)}, u32[]{:S(2)}) %collective-permute-start.17) | collective-permute-done | bytes 32800 | tf_op jit(solution)/shard_map/ppermute | solution.py:250
  77.0 3.6 %collective-permute-start.21 = (bf16[128,128]{1,0:T(8,128)(2,1)S(1)}, bf16[128,128]{1,0:T(8,128)(2,1)S(1)}, u32[]{:S(2)}, u32[]{:S(2)}) collective-permute-start(bf16[128,128]{1,0:T(8,128)(2,1)S(1)} %fusion.1), channel_id=1, source_target_pairs={{0,192},{2,194},{4,196},{6,198},{8,200},{10,202},{12,204},{14,206}... | collective-permute-start | bytes 98312 | tf_op jit(solution)/shard_map/ppermute | solution.py:250
  80.6 1.1 %collective-permute-start.20 = (bf16[128,128]{1,0:T(8,128)(2,1)S(1)}, bf16[128,128]{1,0:T(8,128)(2,1)S(1)}, u32[]{:S(2)}, u32[]{:S(2)}) collective-permute-start(bf16[128,128]{1,0:T(8,128)(2,1)S(1)} %fusion.1), channel_id=1, source_target_pairs={{0,128},{2,130},{4,132},{6,134},{8,136},{10,138},{12,140},{14,142}... | collective-permute-start | bytes 98312 | tf_op jit(solution)/shard_map/ppermute | solution.py:250
  81.8 0.8 collective-permute-done.21
  82.5 3.5 %collective-permute-done.20 = bf16[128,128]{1,0:T(8,128)(2,1)S(1)} collective-permute-done((bf16[128,128]{1,0:T(8,128)(2,1)S(1)}, bf16[128,128]{1,0:T(8,128)(2,1)S(1)}, u32[]{:S(2)}, u32[]{:S(2)}) %collective-permute-start.20) | collective-permute-done | bytes 32800 | tf_op jit(solution)/shard_map/ppermute | solution.py:250
  86.1 0.6 fusion.3
  (16 shorter events, 0.2 us)
Async XLA Ops:
  0.6 9.2 %copy-start = (bf16[1280,64]{0,1:T(8,128)(2,1)S(1)}, bf16[1280,64]{0,1:T(8,128)(2,1)}, u32[]{:S(2)}) copy-start(bf16[1280,64]{0,1:T(8,128)(2,1)} %param.7) | copy-start | bytes 491524
  0.6 9.1 %collective-permute-start = (bf16[64,1280]{1,0:T(8,128)(2,1)}, bf16[64,1280]{1,0:T(8,128)(2,1)S(1)}, u32[]{:S(2)}, u32[]{:S(2)}) collective-permute-start(bf16[64,1280]{1,0:T(8,128)(2,1)} %bitcast.3), channel_id=1, source_target_pairs={{0,2},{2,0},{4,6},{6,4},{8,10},{10,8},{12,14},{14,12},{16,18},{18,... | collective-permute-start | bytes 491528 | tf_op jit(solution)/shard_map/ppermute | solution.py:237
  2.6 8.8 %collective-permute-start.1 = (bf16[64,1280]{1,0:T(8,128)(2,1)}, bf16[64,1280]{1,0:T(8,128)(2,1)S(1)}, u32[]{:S(2)}, u32[]{:S(2)}) collective-permute-start(bf16[64,1280]{1,0:T(8,128)(2,1)} %bitcast.4), channel_id=1, source_target_pairs={{2,4},{4,2},{6,8},{8,6},{10,12},{12,10},{14,16},{16,14},{18,20},{2... | collective-permute-start | bytes 491528 | tf_op jit(solution)/shard_map/ppermute | solution.py:237
  11.9 5.1 %collective-permute-start.2 = (bf16[64,1024]{1,0:T(8,128)(2,1)S(1)}, bf16[64,1024]{1,0:T(8,128)(2,1)S(1)}, u32[]{:S(2)}, u32[]{:S(2)}) collective-permute-start(bf16[64,1024]{1,0:T(8,128)(2,1)S(1)} %get-tuple-element.20), channel_id=1, source_target_pairs={{0,2},{2,0},{4,6},{6,4},{8,10},{10,8},{12,14},{14,12},{16,18},{18,... | collective-permute-start | bytes 393224 | tf_op jit(solution)/shard_map/ppermute | solution.py:237
  12.0 7.7 %collective-permute-start.3 = (bf16[64,1024]{1,0:T(8,128)(2,1)S(1)}, bf16[64,1024]{1,0:T(8,128)(2,1)S(1)}, u32[]{:S(2)}, u32[]{:S(2)}) collective-permute-start(bf16[64,1024]{1,0:T(8,128)(2,1)S(1)} %get-tuple-element.21), channel_id=1, source_target_pairs={{2,4},{4,2},{6,8},{8,6},{10,12},{12,10},{14,16},{16,14},{18,20},{2... | collective-permute-start | bytes 393224 | tf_op jit(solution)/shard_map/ppermute | solution.py:237
  20.2 5.1 %collective-permute-start.4 = (bf16[64,1024]{1,0:T(8,128)(2,1)S(1)}, bf16[64,1024]{1,0:T(8,128)(2,1)S(1)}, u32[]{:S(2)}, u32[]{:S(2)}) collective-permute-start(bf16[64,1024]{1,0:T(8,128)(2,1)S(1)} %get-tuple-element.23), channel_id=1, source_target_pairs={{0,2},{2,0},{4,6},{6,4},{8,10},{10,8},{12,14},{14,12},{16,18},{18,... | collective-permute-start | bytes 393224 | tf_op jit(solution)/shard_map/ppermute | solution.py:237
  20.3 6.5 %collective-permute-start.5 = (bf16[64,1024]{1,0:T(8,128)(2,1)S(1)}, bf16[64,1024]{1,0:T(8,128)(2,1)S(1)}, u32[]{:S(2)}, u32[]{:S(2)}) collective-permute-start(bf16[64,1024]{1,0:T(8,128)(2,1)S(1)} %get-tuple-element.24), channel_id=1, source_target_pairs={{2,4},{4,2},{6,8},{8,6},{10,12},{12,10},{14,16},{16,14},{18,20},{2... | collective-permute-start | bytes 393224 | tf_op jit(solution)/shard_map/ppermute | solution.py:237
  27.4 5.1 %collective-permute-start.6 = (bf16[64,1024]{1,0:T(8,128)(2,1)S(1)}, bf16[64,1024]{1,0:T(8,128)(2,1)S(1)}, u32[]{:S(2)}, u32[]{:S(2)}) collective-permute-start(bf16[64,1024]{1,0:T(8,128)(2,1)S(1)} %get-tuple-element.26), channel_id=1, source_target_pairs={{0,2},{2,0},{4,6},{6,4},{8,10},{10,8},{12,14},{14,12},{16,18},{18,... | collective-permute-start | bytes 393224 | tf_op jit(solution)/shard_map/ppermute | solution.py:237
  27.5 6.6 %collective-permute-start.7 = (bf16[64,1024]{1,0:T(8,128)(2,1)S(1)}, bf16[64,1024]{1,0:T(8,128)(2,1)S(1)}, u32[]{:S(2)}, u32[]{:S(2)}) collective-permute-start(bf16[64,1024]{1,0:T(8,128)(2,1)S(1)} %get-tuple-element.27), channel_id=1, source_target_pairs={{2,4},{4,2},{6,8},{8,6},{10,12},{12,10},{14,16},{16,14},{18,20},{2... | collective-permute-start | bytes 393224 | tf_op jit(solution)/shard_map/ppermute | solution.py:237
  34.7 5.2 %collective-permute-start.8 = (bf16[64,1024]{1,0:T(8,128)(2,1)S(1)}, bf16[64,1024]{1,0:T(8,128)(2,1)S(1)}, u32[]{:S(2)}, u32[]{:S(2)}) collective-permute-start(bf16[64,1024]{1,0:T(8,128)(2,1)S(1)} %get-tuple-element.29), channel_id=1, source_target_pairs={{0,2},{2,0},{4,6},{6,4},{8,10},{10,8},{12,14},{14,12},{16,18},{18,... | collective-permute-start | bytes 393224 | tf_op jit(solution)/shard_map/ppermute | solution.py:237
  35.0 6.6 %collective-permute-start.10 = (bf16[64,1024]{1,0:T(8,128)(2,1)S(1)}, bf16[64,1024]{1,0:T(8,128)(2,1)S(1)}, u32[]{:S(2)}, u32[]{:S(2)}) collective-permute-start(bf16[64,1024]{1,0:T(8,128)(2,1)S(1)} %get-tuple-element.34), channel_id=1, source_target_pairs={{2,4},{4,2},{6,8},{8,6},{10,12},{12,10},{14,16},{16,14},{18,20},{2... | collective-permute-start | bytes 393224 | tf_op jit(solution)/shard_map/ppermute | solution.py:237
  41.5 1.5 %collective-permute-start.9 = (bf16[64,1280]{1,0:T(8,128)(2,1)S(1)}, bf16[64,1280]{1,0:T(8,128)(2,1)S(1)}, u32[]{:S(2)}, u32[]{:S(2)}) collective-permute-start(bf16[64,1280]{1,0:T(8,128)(2,1)S(1)} %get-tuple-element.32.v_ref.own_ref), channel_id=1, source_target_pairs={{0,1},{1,0},{2,3},{3,2},{4,5},{5,4},{6,7},{7,6},{8,9},{9,8},{10,11... | collective-permute-start | bytes 491528 | tf_op jit(solution)/shard_map/ppermute | solution.py:241
  42.2 1.6 %collective-permute-start.11 = (bf16[64,1280]{1,0:T(8,128)(2,1)S(1)}, bf16[64,1280]{1,0:T(8,128)(2,1)S(1)}, u32[]{:S(2)}, u32[]{:S(2)}) collective-permute-start(bf16[64,1280]{1,0:T(8,128)(2,1)S(1)} %image.1.image_ref), channel_id=1, source_target_pairs={{0,1},{1,0},{2,3},{3,2},{4,5},{5,4},{6,7},{7,6},{8,9},{9,8},{10,11... | collective-permute-start | bytes 491528 | tf_op jit(solution)/shard_map/ppermute | solution.py:241
  44.2 7.4 %collective-permute-start.12 = (bf16[128,128]{1,0:T(8,128)(2,1)S(1)}, bf16[128,128]{1,0:T(8,128)(2,1)S(1)}, u32[]{:S(2)}, u32[]{:S(2)}) collective-permute-start(bf16[128,128]{1,0:T(8,128)(2,1)S(1)} %reduce-precision_convert_fusion), channel_id=1, source_target_pairs={{0,14},{2,12},{4,10},{6,8},{8,6},{10,4},{12,2},{14,0},{16,30},{18,... | collective-permute-start | bytes 98312 | tf_op jit(solution)/shard_map/ppermute | solution.py:250
  51.5 4.8 %collective-permute-start.15 = (bf16[128,128]{1,0:T(8,128)(2,1)S(1)}, bf16[128,128]{1,0:T(8,128)(2,1)S(1)}, u32[]{:S(2)}, u32[]{:S(2)}) collective-permute-start(bf16[128,128]{1,0:T(8,128)(2,1)S(1)} %fusion), channel_id=1, source_target_pairs={{0,6},{2,4},{4,2},{6,0},{8,14},{10,12},{12,10},{14,8},{16,22},{18,... | collective-permute-start | bytes 98312 | tf_op jit(solution)/shard_map/ppermute | solution.py:250
  53.3 4.8 %collective-permute-start.14 = (bf16[128,128]{1,0:T(8,128)(2,1)S(1)}, bf16[128,128]{1,0:T(8,128)(2,1)S(1)}, u32[]{:S(2)}, u32[]{:S(2)}) collective-permute-start(bf16[128,128]{1,0:T(8,128)(2,1)S(1)} %fusion), channel_id=1, source_target_pairs={{0,4},{2,6},{4,0},{6,2},{8,12},{10,14},{12,8},{14,10},{16,20},{18,... | collective-permute-start | bytes 98312 | tf_op jit(solution)/shard_map/ppermute | solution.py:250
  55.3 3.9 %collective-permute-start.13 = (bf16[128,128]{1,0:T(8,128)(2,1)S(1)}, bf16[128,128]{1,0:T(8,128)(2,1)S(1)}, u32[]{:S(2)}, u32[]{:S(2)}) collective-permute-start(bf16[128,128]{1,0:T(8,128)(2,1)S(1)} %fusion), channel_id=1, source_target_pairs={{0,2},{2,0},{4,6},{6,4},{8,10},{10,8},{12,14},{14,12},{16,18},{18,... | collective-permute-start | bytes 98312 | tf_op jit(solution)/shard_map/ppermute | solution.py:250
  59.3 14.4 %collective-permute-start.18 = (bf16[128,128]{1,0:T(8,128)(2,1)S(1)}, bf16[128,128]{1,0:T(8,128)(2,1)S(1)}, u32[]{:S(2)}, u32[]{:S(2)}) collective-permute-start(bf16[128,128]{1,0:T(8,128)(2,1)S(1)} %get-tuple-element.35), channel_id=1, source_target_pairs={{0,48},{2,50},{4,52},{6,54},{8,56},{10,58},{12,60},{14,62},{16,32}... | collective-permute-start | bytes 98312 | tf_op jit(solution)/shard_map/ppermute | solution.py:250
  71.6 5.4 %collective-permute-start.17 = (bf16[128,128]{1,0:T(8,128)(2,1)S(1)}, bf16[128,128]{1,0:T(8,128)(2,1)S(1)}, u32[]{:S(2)}, u32[]{:S(2)}) collective-permute-start(bf16[128,128]{1,0:T(8,128)(2,1)S(1)} %get-tuple-element.35), channel_id=1, source_target_pairs={{0,32},{2,34},{4,36},{6,38},{8,40},{10,42},{12,44},{14,46},{16,48}... | collective-permute-start | bytes 98312 | tf_op jit(solution)/shard_map/ppermute | solution.py:250
  71.6 5.4 %collective-permute-start.16 = (bf16[128,128]{1,0:T(8,128)(2,1)S(1)}, bf16[128,128]{1,0:T(8,128)(2,1)S(1)}, u32[]{:S(2)}, u32[]{:S(2)}) collective-permute-start(bf16[128,128]{1,0:T(8,128)(2,1)S(1)} %get-tuple-element.35), channel_id=1, source_target_pairs={{0,16},{2,18},{4,20},{6,22},{8,24},{10,26},{12,28},{14,30},{16,0},... | collective-permute-start | bytes 98312 | tf_op jit(solution)/shard_map/ppermute | solution.py:250
  77.0 5.5 %collective-permute-start.21 = (bf16[128,128]{1,0:T(8,128)(2,1)S(1)}, bf16[128,128]{1,0:T(8,128)(2,1)S(1)}, u32[]{:S(2)}, u32[]{:S(2)}) collective-permute-start(bf16[128,128]{1,0:T(8,128)(2,1)S(1)} %fusion.1), channel_id=1, source_target_pairs={{0,192},{2,194},{4,196},{6,198},{8,200},{10,202},{12,204},{14,206}... | collective-permute-start | bytes 98312 | tf_op jit(solution)/shard_map/ppermute | solution.py:250
  80.6 5.4 %collective-permute-start.20 = (bf16[128,128]{1,0:T(8,128)(2,1)S(1)}, bf16[128,128]{1,0:T(8,128)(2,1)S(1)}, u32[]{:S(2)}, u32[]{:S(2)}) collective-permute-start(bf16[128,128]{1,0:T(8,128)(2,1)S(1)} %fusion.1), channel_id=1, source_target_pairs={{0,128},{2,130},{4,132},{6,134},{8,136},{10,138},{12,140},{14,142}... | collective-permute-start | bytes 98312 | tf_op jit(solution)/shard_map/ppermute | solution.py:250
  81.8 4.3 %collective-permute-start.19 = (bf16[128,128]{1,0:T(8,128)(2,1)S(1)}, bf16[128,128]{1,0:T(8,128)(2,1)S(1)}, u32[]{:S(2)}, u32[]{:S(2)}) collective-permute-start(bf16[128,128]{1,0:T(8,128)(2,1)S(1)} %fusion.1), channel_id=1, source_target_pairs={{0,64},{2,66},{4,68},{6,70},{8,72},{10,74},{12,76},{14,78},{16,80}... | collective-permute-start | bytes 98312 | tf_op jit(solution)/shard_map/ppermute | solution.py:250
